TPU v7x, 32 devices: a whole 2x2x4 slice. The times are simulated.
32 devices in a mesh: grp: 2 (over x), cross: 16 (over z, y, core).
Axes of the slice: x: 2, y: 2, z: 4, core: 2. Of those that a mesh axis runs over, the one named last changes fastest.
Arguments:
- state: float32 [3, 512, 2048], P(None, 'grp', 'cross'), parts along dimension 1, may hold values from -4 to 4, as said below
- log_mu: float32 [512, 2048], P('grp', 'cross'), parts along dimension 0, may hold values from -2.3 to -0.7
- log_xi: float32 [512, 2048], P('grp', 'cross'), parts along dimension 0, may hold values from 0 to 1.6
- dir_mu: float32 [512, 2048], P('grp', 'cross'), parts along dimension 0, may hold values from -4 to 4
- dir_xi: float32 [512, 2048], P('grp', 'cross'), parts along dimension 0, may hold values from -4 to 4
- wet: int32 [512, 2048], P('grp', 'cross'), parts along dimension 0, may hold values from 0 to 1, as said below
- observed: int32 [512, 2048], P('grp', 'cross'), parts along dimension 0, may hold values from 0 to 1, as said below
- terrain: int32 [512, 2048], P('grp', 'cross'), parts along dimension 0, may hold values from 0 to 7
- class_weight: float32 [8], replicated, may hold values from 0.01 to 0.1
Outputs:
- hvp_mu: float32 [512, 2048], P('grp', 'cross'), parts along dimension 0
- hvp_xi: float32 [512, 2048], P('grp', 'cross'), parts along dimension 0
There are 2 independent parts, one for each index of `grp`. A program takes and returns all parts, laid end to end along the dimension named above; an argument that names none is the same for every part. Nothing has to cross between parts.
Inputs may be any that keep to these rules, and one draw needn't show every extreme that they name: state[0] holds heights, never negative; state[1] and state[2] hold discharges. 1 marks a cell that was wet in the checkpoint. 1 marks a pixel with an observed deposit depth.
All inputs are finite; a program needn't handle non-finite values.
Results may differ from a plain program's by a relative error of at most 0.00002.
Values sent between devices are 32-bit elements; how exact they have to be, the bound alone decides.
No kernel may reach another device: no remote copies, remote signals or barrier semaphores. Data moves between devices by JAX's collectives and lax.ppermute only.
A program may use at most 64 MiB of HBM per device.

v0:
```python
import functools

import jax
import jax.numpy as jnp
from jax import lax
from jax.experimental import pallas as pl
from jax.experimental.pallas import tpu as pltpu
from jax.sharding import PartitionSpec as P

COS_SLOPE = 0.8
SIN_SLOPE = 0.6
DEPTH_FLOOR = 0.05
SPEED_EPS = 0.01
COURANT = 0.2
DATA_WEIGHT = 100000.0

LANES = 128
TILE = 8
H, Q1, Q2, FA, FB, DA, DB, DM, DX, WR, OB = range(11)
FIELDS = 11
UNROLL = 2


def load(ref, k, col, groups):
    return jnp.concatenate([ref[k, g, pl.ds(col, TILE), :] for g in range(groups)], axis=0)


def store(ref, k, col, value, groups):
    for g in range(groups):
        ref[k, g, pl.ds(col, TILE), :] = value[g * TILE : (g + 1) * TILE]


class Grid:
    def __init__(self, groups, cols):
        self.groups = groups
        self.cols = cols
        self.tiles = cols // TILE + 2
        self.lane = lax.broadcasted_iota(jnp.int32, (groups * TILE, LANES), 1)
        self.blank = jnp.zeros((TILE, LANES), jnp.float32)

    def rows_next(self, v):
        turned = pltpu.roll(v, LANES - 1, 1)
        after = jnp.concatenate([turned[TILE:], self.blank], axis=0)
        return jnp.where(self.lane == LANES - 1, after, turned)

    def rows_prev(self, v):
        turned = pltpu.roll(v, 1, 1)
        before = jnp.concatenate([self.blank, turned[: -TILE]], axis=0)
        return jnp.where(self.lane == 0, before, turned)

    def both_rows(self, v):
        return self.rows_next(v), self.rows_prev(v)

    def get(self, ref, k, col):
        return load(ref, k, col, self.groups)

    def put(self, ref, k, col, v):
        store(ref, k, col, v, self.groups)

    def both_cols(self, ref, k, col):
        return load(ref, k, col + 1, self.groups), load(ref, k, col - 1, self.groups)

    def sweep(self, body, first=0, last=None, carry=None):
        last = self.tiles if last is None else last
        steps, rest = divmod(last - first, UNROLL)

        def visit(t, col, carry):
            return body(t, col) if carry is None else body(t, col, carry)

        def step(i, carry):
            for u in range(UNROLL):
                t = first + i * UNROLL + u
                carry = visit(t, pl.multiple_of((t + 1) * TILE, TILE), carry)
            return carry

        carry = lax.fori_loop(0, steps, step, carry)
        for t in range(last - rest, last):
            carry = visit(t, (t + 1) * TILE, carry)
        return carry

    def inside(self, t, ends):
        return jnp.logical_not(((t == 0) & ends[0]) | ((t == self.tiles - 1) & ends[1]))


def end_flags():
    me = lax.axis_index("cross")
    return me == 0, me == lax.axis_size("cross") - 1


def speed_of(height, down, across):
    inv = 1.0 / jnp.maximum(height, DEPTH_FLOOR)
    vel_down = down * inv
    vel_across = across * inv
    return jnp.sqrt(vel_down * vel_down + vel_across * vel_across) + jnp.sqrt(COS_SLOPE * jnp.maximum(height, 0.0))


def velocities(height, down, across):
    inv = 1.0 / jnp.maximum(height, DEPTH_FLOOR)
    return inv, down * inv, across * inv


def friction(height, vel_down, vel_across, dry, turbulent):
    squared = vel_down * vel_down + vel_across * vel_across + SPEED_EPS
    inv_speed = lax.rsqrt(squared)
    speed = squared * inv_speed
    return inv_speed, speed, dry * height * inv_speed, turbulent * speed


def splat_max(rows, shape):
    return jnp.broadcast_to(jnp.max(rows, axis=0, keepdims=True), shape)


def prepare(state, log_mu, log_xi, dir_mu, dir_xi, wet, observed, terrain, class_weight,
            own, edge_a, edge_b, row, count_row, code, turned):
    rows, cols = log_mu.shape
    groups = rows // LANES
    step_rows = 16

    def scan(i, carry):
        top, seen = carry
        at = pl.ds(pl.multiple_of(i * step_rows, step_rows), step_rows)
        seen_here = observed[at, :]
        code[at, :] = (wet[at, :] + 2 * seen_here + 4 * terrain[at, :]).astype(jnp.float32)
        here = speed_of(state[0, at, :], state[1, at, :], state[2, at, :])
        return jnp.maximum(top, here), seen + seen_here.astype(jnp.float32)

    zero = jnp.zeros((step_rows, cols), jnp.float32)
    top, seen = lax.fori_loop(0, rows // step_rows, scan, (zero, zero))
    row[...] = jnp.full(row.shape, jnp.max(top), jnp.float32)
    count_row[...] = jnp.full(count_row.shape, jnp.sum(seen), jnp.float32)

    for g in range(groups):
        at = pl.ds(g * LANES, LANES)
        for k in range(3):
            own[k, g] = state[k, at, :].T
        own[DM, g] = dir_mu[at, :].T
        own[DX, g] = dir_xi[at, :].T
        turned[0, g] = log_mu[at, :].T
        turned[1, g] = log_xi[at, :].T
        turned[2, g] = code[at, :].T

    def derive(i, carry):
        for g in range(groups):
            at = pl.ds(pl.multiple_of(i * TILE, TILE), TILE)
            bits = turned[2, g, at, :].astype(jnp.int32)
            wet_here = (bits & 1).astype(jnp.float32)
            kind = bits >> 2
            dry = wet_here * jnp.exp(turned[0, g, at, :]) * COS_SLOPE
            turbulent = wet_here * jnp.exp(-turned[1, g, at, :])
            own[FA, g, at, :] = dry
            own[FB, g, at, :] = turbulent
            own[DA, g, at, :] = dry * own[DM, g, at, :]
            own[DB, g, at, :] = -turbulent * own[DX, g, at, :]
            own[OB, g, at, :] = ((bits >> 1) & 1).astype(jnp.float32)
            weight = jnp.zeros((TILE, LANES), jnp.float32)
            for c in range(class_weight.shape[0]):
                weight = jnp.where(kind == c, class_weight[c], weight)
            own[WR, g, at, :] = weight
        return carry

    lax.fori_loop(0, cols // TILE, derive, 0)
    even = lax.rem(lax.axis_index("cross"), 2) == 0
    for k in range(FIELDS):
        for g in range(groups):
            left = own[k, g, :TILE, :]
            right = own[k, g, cols - TILE :, :]
            edge_a[k, g] = jnp.where(even, right, left)
            edge_b[k, g] = jnp.where(even, left, right)


def open_step(own, edge_a, edge_b, ext, xy, base):
    groups, cols = own.shape[1], own.shape[2]
    grid = Grid(groups, cols)
    even = lax.rem(lax.axis_index("cross"), 2) == 0
    for k in range(FIELDS):
        for g in range(groups):
            ext[k, g, TILE : 2 * TILE, :] = jnp.where(even, edge_b[k, g], edge_a[k, g])
            ext[k, g, 2 * TILE + cols : 3 * TILE + cols, :] = jnp.where(even, edge_a[k, g], edge_b[k, g])
            ext[k, g, 2 * TILE : 2 * TILE + cols, :] = own[k, g]

    def first(t, col):
        height, down, across = (grid.get(ext, k, col) for k in (H, Q1, Q2))
        _, u, v = velocities(height, down, across)
        inv_speed, speed, dry, turb = friction(height, u, v, grid.get(ext, FA, col), grid.get(ext, FB, col))
        change = grid.get(ext, DA, col) * height * inv_speed + grid.get(ext, DB, col) * speed
        grid.put(xy, 6, col, -u * change)
        grid.put(xy, 7, col, -v * change)
        for k, value in enumerate((u, v, dry, turb)):
            grid.put(base, k, col, value)
        drag = dry + turb
        pressure = 0.5 * COS_SLOPE * height * height
        mixed = down * v
        hn, hp = grid.both_rows(height)
        pn, pp = grid.both_rows(down)
        qn, qp = grid.both_rows(across)
        fn, fp = grid.both_rows(down * u + pressure)
        gn, gp = grid.both_rows(mixed)
        grid.put(base, 4, col, mixed)
        grid.put(base, 5, col, across * v + pressure)
        grid.put(xy, 0, col, 0.6 * height + 0.1 * (hn + hp))
        grid.put(xy, 1, col, 0.6 * down + 0.1 * (pn + pp))
        grid.put(xy, 2, col, 0.6 * across + 0.1 * (qn + qp))
        grid.put(xy, 3, col, -0.5 * (pn - pp))
        grid.put(xy, 4, col, SIN_SLOPE * height - drag * u - 0.5 * (fn - fp))
        grid.put(xy, 5, col, -drag * v - 0.5 * (gn - gp))

    grid.sweep(first)

    def second(t, col):
        hn, hp = grid.both_cols(ext, H, col)
        pn, pp = grid.both_cols(ext, Q1, col)
        qn, qp = grid.both_cols(ext, Q2, col)
        gn, gp = grid.both_cols(base, 4, col)
        fn, fp = grid.both_cols(base, 5, col)
        for k, (n, p) in enumerate(((hn, hp), (pn, pp), (qn, qp))):
            grid.put(xy, k, col, grid.get(xy, k, col) + 0.1 * (n + p))
        for k, (n, p) in enumerate(((qn, qp), (gn, gp), (fn, fp))):
            grid.put(xy, 3 + k, col, grid.get(xy, 3 + k, col) - 0.5 * (n - p))

    grid.sweep(second)


CU, CV, CZ, CW, CE, CB, CD = range(7)
MU, MV, MZ, MW, ME, MB, MM, MH, MY = range(9)


def middle(ends_of, top_rows, ext, xy, count_row, at_one, mid, row, work):
    groups, cols = ext.shape[1], ext.shape[2] - 4 * TILE
    grid = Grid(groups, cols)
    ends = ends_of()
    dt = COURANT / splat_max(top_rows[...], grid.lane.shape)
    half = 0.5 * dt

    def first(t, col):
        keep = grid.inside(t, ends)
        height, down, across = (
            jnp.where(keep, grid.get(xy, k, col) + dt * grid.get(xy, 3 + k, col), 0.0) for k in range(3)
        )
        inv, u, v = velocities(height, down, across)
        inv_speed, speed, dry, turb = friction(height, u, v, grid.get(ext, FA, col), grid.get(ext, FB, col))
        drag = dry + turb
        grid.put(at_one, CU, col, u)
        grid.put(at_one, CV, col, v)
        grid.put(at_one, CZ, col, (grid.get(ext, FB, col) - dry * inv_speed) * inv_speed * inv)
        grid.put(at_one, CW, col, drag * inv)
        grid.put(at_one, CE, col, dry)
        grid.put(at_one, CB, col, turb)
        grid.put(at_one, CD, col, grid.get(ext, DA, col) * height * inv_speed + grid.get(ext, DB, col) * speed)
        pressure = 0.5 * COS_SLOPE * height * height
        mixed = down * v
        for k, value in enumerate((height, down, across, mixed, across * v + pressure)):
            grid.put(work, k, col, value)
        sources = (0.0, dt * (SIN_SLOPE * height - drag * u), -dt * drag * v)
        for k, (value, flux) in enumerate(((height, down), (down, down * u + pressure), (across, mixed))):
            tenth, moved = 0.1 * value, half * flux
            total = grid.get(ext, k, col) + 0.6 * value + sources[k]
            total += grid.rows_next(tenth - moved) + grid.rows_prev(tenth + moved)
            grid.put(mid, k, col, total)

    grid.sweep(first)

    def second(t, col, top):
        keep = grid.inside(t, ends)
        found = []
        for k, (value, flux) in enumerate(((0, 2), (1, 3), (2, 4))):
            vn, vp = grid.both_cols(work, value, col)
            fn, fp = grid.both_cols(work, flux, col)
            total = grid.get(mid, k, col) + 0.1 * (vn + vp) - half * (fn - fp)
            found.append(jnp.where(keep, 0.5 * total, 0.0))
            grid.put(mid, k, col, found[k])
        own = (t > 0) & (t < grid.tiles - 1)
        return jnp.maximum(top, jnp.where(own, speed_of(*found), 0.0))

    top = grid.sweep(second, carry=jnp.zeros(grid.lane.shape, jnp.float32))
    lane = lax.broadcasted_iota(jnp.int32, row.shape, 1)
    count = jnp.broadcast_to(count_row[:1, :], row.shape)
    row[...] = jnp.where(lane < LANES // 2, jnp.full(row.shape, jnp.max(top), jnp.float32), count)


def tangents(ends_of, top_rows, ext, xy, at_one, mid, tan, at_mid, smooth, work):
    groups, cols = ext.shape[1], ext.shape[2] - 4 * TILE
    grid = Grid(groups, cols)
    ends = ends_of()
    dt = COURANT / splat_max(top_rows[...], grid.lane.shape)
    half = 0.5 * dt

    def first(t, col):
        tp, tq = dt * grid.get(xy, 6, col), dt * grid.get(xy, 7, col)
        u, v = grid.get(at_one, CU, col), grid.get(at_one, CV, col)
        w = grid.get(at_one, CW, col)
        along = grid.get(at_one, CZ, col) * (u * tp + v * tq) + grid.get(at_one, CD, col)
        mixed = v * tp + u * tq
        for k, value in enumerate((tp, tq, mixed, 2.0 * v * tq)):
            grid.put(work, k, col, value)
        moved = half * tp
        grid.put(tan, 0, col, grid.rows_prev(moved) - grid.rows_next(moved))
        sources = (-dt * (u * along + w * tp), -dt * (v * along + w * tq))
        for k, (value, flux) in enumerate(((tp, 2.0 * u * tp), (tq, mixed))):
            tenth, moved = 0.1 * value, half * flux
            total = 0.6 * value + sources[k]
            total += grid.rows_next(tenth - moved) + grid.rows_prev(tenth + moved)
            grid.put(tan, 1 + k, col, total)

    grid.sweep(first)

    def second(t, col):
        keep = grid.inside(t, ends)
        qn, qp = grid.both_cols(work, 1, col)
        pn, pp = grid.both_cols(work, 0, col)
        gn, gp = grid.both_cols(work, 2, col)
        fn, fp = grid.both_cols(work, 3, col)
        th = grid.get(tan, 0, col) - half * (qn - qp)
        tp = grid.get(tan, 1, col) + 0.1 * (pn + pp) - half * (gn - gp)
        tq = grid.get(tan, 2, col) + 0.1 * (qn + qp) - half * (fn - fp)
        th, tp, tq = (jnp.where(keep, 0.5 * x, 0.0) for x in (th, tp, tq))
        height, down, across = (grid.get(mid, k, col) for k in range(3))
        inv, u, v = velocities(height, down, across)
        above = jnp.where(height > DEPTH_FLOOR, 1.0, jnp.where(height == DEPTH_FLOOR, 0.5, 0.0))
        turb_of = grid.get(ext, FB, col)
        dry_of = grid.get(ext, FA, col)
        inv_speed, speed, dry, turb = friction(height, u, v, dry_of, turb_of)
        z = (turb_of - dry * inv_speed) * inv_speed * inv
        w = (dry + turb) * inv
        y = dry_of * inv_speed - above * (z * (u * u + v * v) + w)
        eight = COS_SLOPE * height
        for k, value in ((MU, u), (MV, v), (MZ, z), (MW, w), (ME, dry), (MB, turb), (MM, above), (MH, eight), (MY, y)):
            grid.put(at_mid, k, col, value)
        change = grid.get(ext, DA, col) * height * inv_speed + grid.get(ext, DB, col) * speed
        along = z * (u * tp + v * tq) + y * th + change
        lift = above * th
        flux_down = 2.0 * u * tp + eight * th - u * u * lift
        mixed = v * tp + u * tq - u * v * lift
        for k, value in enumerate((th, tp, tq, mixed, 2.0 * v * tq + eight * th - v * v * lift)):
            grid.put(work, 4 + k, col, value)
        hn, hp = grid.both_rows(th)
        pn, pp = grid.both_rows(tp)
        qn, qp = grid.both_rows(tq)
        fn, fp = grid.both_rows(flux_down)
        gn, gp = grid.both_rows(mixed)
        grid.put(tan, 0, col, th)
        grid.put(tan, 1, col, 0.6 * th + 0.1 * (hn + hp))
        grid.put(tan, 2, col, 0.6 * tp + 0.1 * (pn + pp))
        grid.put(tan, 3, col, 0.6 * tq + 0.1 * (qn + qp))
        grid.put(tan, 4, col, -0.5 * (pn - pp))
        grid.put(tan, 5, col, SIN_SLOPE * th - u * along - w * tp - 0.5 * (fn - fp))
        grid.put(tan, 6, col, -v * along - w * tq - 0.5 * (gn - gp))

    grid.sweep(second)

    def third(t, col):
        keep = grid.inside(t, ends)
        hn, hp = grid.both_cols(work, 4, col)
        pn, pp = grid.both_cols(work, 5, col)
        qn, qp = grid.both_cols(work, 6, col)
        gn, gp = grid.both_cols(work, 7, col)
        fn, fp = grid.both_cols(work, 8, col)
        for k, (n, p) in enumerate(((hn, hp), (pn, pp), (qn, qp))):
            grid.put(tan, 1 + k, col, jnp.where(keep, grid.get(tan, 1 + k, col) + 0.1 * (n + p), 0.0))
        for k, (n, p) in enumerate(((qn, qp), (gn, gp), (fn, fp))):
            grid.put(tan, 4 + k, col, jnp.where(keep, grid.get(tan, 4 + k, col) - 0.5 * (n - p), 0.0))

    grid.sweep(third)

    def laplace(ref, k, col):
        value = grid.get(ref, k, col)
        rn, rp = grid.both_rows(value)
        cn, cp = grid.both_cols(ref, k, col)
        return 4.0 * value - rn - rp - cn - cp

    def bend(t, col):
        weight = grid.get(ext, WR, col)
        for k, field in enumerate((DM, DX)):
            grid.put(work, k, col, weight * laplace(ext, field, col))

    grid.sweep(bend)

    def bend_again(t, col):
        for k in range(2):
            grid.put(smooth, k, col, laplace(work, k, col))

    grid.sweep(bend_again, 1, grid.tiles - 1)


def finish(ends_of, cells, top_rows, next_rows, ext, base, at_one, tan, at_mid, smooth, out_mu, out_xi, work, total):
    groups, cols = ext.shape[1], ext.shape[2] - 4 * TILE
    grid = Grid(groups, cols)
    ends = ends_of()
    shape = grid.lane.shape
    dt0 = COURANT / splat_max(top_rows[...], shape)
    rows = next_rows[...]
    lane = lax.broadcasted_iota(jnp.int32, (1, LANES), 1)
    most = jnp.max(rows, axis=0, keepdims=True)
    added = jnp.sum(rows, axis=0, keepdims=True)
    dt1 = COURANT / jnp.broadcast_to(jnp.where(lane < LANES // 2, most, pltpu.roll(most, LANES // 2, 1)), shape)
    count = jnp.where(lane < LANES // 2, pltpu.roll(added, LANES // 2, 1), added)
    weight = jnp.broadcast_to((DATA_WEIGHT * cells) / count, shape)
    half1 = 0.5 * dt1
    half0 = 0.5 * dt0

    def end(t, col):
        def section(k, off):
            return grid.get(tan, 1 + k, col + off) + dt1 * grid.get(tan, 4 + k, col + off)

        th, tp = section(0, 0), section(1, 0)
        tenth, moved = 0.1 * th, half1 * tp
        value = grid.get(tan, 0, col) + 0.6 * th + grid.rows_next(tenth - moved) + grid.rows_prev(tenth + moved)
        value += 0.1 * (section(0, 1) + section(0, -1)) - half1 * (section(2, 1) - section(2, -1))
        grid.put(work, 0, col, weight * grid.get(ext, OB, col) * (0.5 * value))

    grid.sweep(end)

    def back_second(t, col):
        keep = grid.inside(t, ends)
        seed = grid.get(work, 0, col)
        rn, rp = grid.both_rows(seed)
        cn, cp = grid.both_cols(work, 0, col)
        zero = jnp.zeros_like(seed)
        grid.put(work, 1, col, jnp.where(keep, 0.3 * seed + 0.05 * (rn + rp + cn + cp), zero))
        grid.put(work, 2, col, jnp.where(keep, 0.5 * half1 * (rn - rp), zero))
        grid.put(work, 3, col, jnp.where(keep, 0.5 * half1 * (cn - cp), zero))

    grid.sweep(back_second)

    def back_first(t, col):
        keep = grid.inside(t, ends)
        g0, g1, g2 = (grid.get(work, 1 + k, col) for k in range(3))
        r0n, r0p = grid.both_rows(g0)
        r1n, r1p = grid.both_rows(g1)
        r2n, r2p = grid.both_rows(g2)
        c0n, c0p = grid.both_cols(work, 1, col)
        c1n, c1p = grid.both_cols(work, 2, col)
        c2n, c2p = grid.both_cols(work, 3, col)
        u, v = grid.get(at_mid, MU, col), grid.get(at_mid, MV, col)
        z, w = grid.get(at_mid, MZ, col), grid.get(at_mid, MW, col)
        down = half1 * (r1n - r1p)
        cross = half1 * ((r2n - r2p) + (c1n - c1p))
        side = half1 * (c2n - c2p)
        h1, h2 = dt1 * g1, dt1 * g2
        along = u * h1 + v * h2
        grid.put(total, 0, col, grid.get(smooth, 0, col) - grid.get(at_mid, ME, col) * along)
        grid.put(total, 1, col, grid.get(smooth, 1, col) + grid.get(at_mid, MB, col) * along)
        pull = z * along
        part_u = u * down + v * cross
        part_v = v * side
        m0 = 0.5 * grid.get(work, 0, col) + 0.6 * g0 + 0.1 * (r0n + r0p + c0n + c0p)
        m0 += SIN_SLOPE * h1 - grid.get(at_mid, MY, col) * along + grid.get(at_mid, MH, col) * (down + side)
        m0 -= grid.get(at_mid, MM, col) * (u * part_u + v * part_v)
        m1 = 0.6 * g1 + 0.1 * (r1n + r1p + c1n + c1p)
        m1 += half1 * (r0n - r0p) + 2.0 * u * down + v * cross - u * pull - w * h1
        m2 = 0.6 * g2 + 0.1 * (r2n + r2p + c2n + c2p)
        m2 += half1 * (c0n - c0p) + u * cross + 2.0 * v * side - v * pull - w * h2
        for k, value in enumerate((m0, m1, m2)):
            grid.put(work, 4 + k, col, jnp.where(keep, value, 0.0))

    grid.sweep(back_first)

    def early(t, col):
        m0, m1, m2 = (grid.get(work, 4 + k, col) for k in range(3))
        r0n, r0p = grid.both_rows(m0)
        r1n, r1p = grid.both_rows(m1)
        r2n, r2p = grid.both_rows(m2)
        c0n, c0p = grid.both_cols(work, 4, col)
        c1n, c1p = grid.both_cols(work, 5, col)
        c2n, c2p = grid.both_cols(work, 6, col)
        u, v = grid.get(at_one, CU, col), grid.get(at_one, CV, col)
        z, w = grid.get(at_one, CZ, col), grid.get(at_one, CW, col)
        quarter = 0.5 * half0
        down = quarter * (r1n - r1p)
        cross = quarter * ((r2n - r2p) + (c1n - c1p))
        side = quarter * (c2n - c2p)
        p1, p2 = half0 * m1, half0 * m2
        along = u * p1 + v * p2
        pull = z * along
        f1 = 0.3 * m1 + 0.05 * (r1n + r1p + c1n + c1p)
        f1 += quarter * (r0n - r0p) + 2.0 * u * down + v * cross - u * pull - w * p1
        f2 = 0.3 * m2 + 0.05 * (r2n + r2p + c2n + c2p)
        f2 += quarter * (c0n - c0p) + u * cross + 2.0 * v * side - v * pull - w * p2
        start = dt0 * (grid.get(base, 0, col) * f1 + grid.get(base, 1, col) * f2)
        mu = grid.get(total, 0, col) - grid.get(at_one, CE, col) * along - grid.get(base, 2, col) * start
        xi = grid.get(total, 1, col) + grid.get(at_one, CB, col) * along + grid.get(base, 3, col) * start
        grid.put(total, 0, col, mu)
        grid.put(total, 1, col, xi)

    grid.sweep(early, 1, grid.tiles - 1)

    for g in range(groups):
        at = pl.ds(g * LANES, LANES)
        out_mu[at, :] = total[0, g, 2 * TILE : 2 * TILE + cols, :].T
        out_xi[at, :] = total[1, g, 2 * TILE : 2 * TILE + cols, :].T


VMEM = pl.BlockSpec(memory_space=pltpu.VMEM)
SMEM = pl.BlockSpec(memory_space=pltpu.SMEM)


def call(body, name, operands, outs, scratch, flops, small=()):
    outs = [jax.ShapeDtypeStruct(shape, jnp.float32) for shape in outs]
    moved = 4 * sum(x.size for x in operands) + 4 * sum(x.size for x in outs)
    return pl.pallas_call(
        body,
        name=name,
        out_shape=outs,
        in_specs=[SMEM if i in small else VMEM for i in range(len(operands))],
        out_specs=[VMEM] * len(outs),
        scratch_shapes=[pltpu.VMEM(shape, jnp.float32) for shape in scratch],
        compiler_params=pltpu.CompilerParams(vmem_limit_bytes=24 * 1024 * 1024),
        cost_estimate=pl.CostEstimate(flops=flops, bytes_accessed=moved, transcendentals=0),
    )(*operands)


def swap_edges(edge_a, edge_b, count):
    pairs_a = [(i, i ^ 1) for i in range(count)]
    pairs_b = [(i, i - 1 if i % 2 == 0 else i + 1) for i in range(1, count - 1)]
    return lax.ppermute(edge_a, "cross", pairs_a), lax.ppermute(edge_b, "cross", pairs_b)


def share(row):
    return lax.all_to_all(row, "cross", 0, 0, tiled=True)


def local(state, log_mu, log_xi, dir_mu, dir_xi, wet, observed, terrain, class_weight):
    rows, cols = log_mu.shape
    groups = rows // LANES
    count = lax.axis_size("cross")
    cells = rows * cols * count
    wide = (groups, cols + 4 * TILE, LANES)
    edge = (FIELDS, groups, TILE, LANES)
    work = rows * cols

    own, edge_a, edge_b, row, count_row = call(
        prepare,
        "prepare",
        (state, log_mu, log_xi, dir_mu, dir_xi, wet, observed, terrain, class_weight),
        [(FIELDS, groups, cols, LANES), edge, edge, (count, LANES), (TILE, LANES)],
        [(rows, cols), (3, groups, cols, LANES)],
        100 * work,
        small=(8,),
    )
    edge_a, edge_b = swap_edges(edge_a, edge_b, count)
    top_rows = share(row)
    ext, xy, base = call(
        open_step, "open_step", (own, edge_a, edge_b), [(FIELDS,) + wide, (8,) + wide, (6,) + wide], [], 100 * work
    )
    at_one, mid, next_row = call(
        functools.partial(middle, end_flags),
        "middle",
        (top_rows, ext, xy, count_row),
        [(7,) + wide, (3,) + wide, (count, LANES)],
        [(5,) + wide],
        120 * work,
    )
    next_rows = share(next_row)
    tan, at_mid, smooth = call(
        functools.partial(tangents, end_flags),
        "tangents",
        (top_rows, ext, xy, at_one, mid),
        [(7,) + wide, (9,) + wide, (2,) + wide],
        [(9,) + wide],
        200 * work,
    )
    out_mu, out_xi = call(
        functools.partial(finish, end_flags, float(cells)),
        "finish",
        (top_rows, next_rows, ext, base, at_one, tan, at_mid, smooth),
        [(rows, cols), (rows, cols)],
        [(7,) + wide, (2,) + wide],
        200 * work,
    )
    return out_mu, out_xi


def solution(mesh):
    return jax.shard_map(
        local,
        mesh=mesh,
        in_specs=(
            P(None, "grp", "cross"),
            P("grp", "cross"),
            P("grp", "cross"),
            P("grp", "cross"),
            P("grp", "cross"),
            P("grp", "cross"),
            P("grp", "cross"),
            P("grp", "cross"),
            P(),
        ),
        out_specs=(P("grp", "cross"), P("grp", "cross")),
        check_vma=False,
    )
```

profile of v0, /device:TPU:0, one launch (start us, length us, event | category | flops | bytes accessed | tf_op | source)
XLA Modules:
  0.0 53.2 jit_solution(14151699884321575636)
XLA Ops:
  0.6 1.0 %copy-done.13 = f32[3,256,128]{2,1,0:T(8,128)S(1)} copy-done((f32[3,256,128]{2,1,0:T(8,128)S(1)}, f32[3,256,128]{2,1,0:T(8,128)}, u32[]{:S(2)}) %copy-start.13) | copy-done | bytes 393240
  1.6 0.9 %copy-done.14 = f32[256,128]{1,0:T(8,128)S(1)} copy-done((f32[256,128]{1,0:T(8,128)S(1)}, f32[256,128]{1,0:T(8,128)}, u32[]{:S(2)}) %copy-start.14) | copy-done | bytes 131096
  2.5 0.9 %copy-done.15 = f32[256,128]{1,0:T(8,128)S(1)} copy-done((f32[256,128]{1,0:T(8,128)S(1)}, f32[256,128]{1,0:T(8,128)}, u32[]{:S(2)}) %copy-start.15) | copy-done | bytes 131096
  3.4 0.9 %copy-done.16 = f32[256,128]{1,0:T(8,128)S(1)} copy-done((f32[256,128]{1,0:T(8,128)S(1)}, f32[256,128]{1,0:T(8,128)}, u32[]{:S(2)}) %copy-start.16) | copy-done | bytes 131096
  4.3 0.9 %copy-done.17 = f32[256,128]{1,0:T(8,128)S(1)} copy-done((f32[256,128]{1,0:T(8,128)S(1)}, f32[256,128]{1,0:T(8,128)}, u32[]{:S(2)}) %copy-start.17) | copy-done | bytes 131096
  5.3 0.9 %copy-done.18 = s32[256,128]{1,0:T(8,128)S(1)} copy-done((s32[256,128]{1,0:T(8,128)S(1)}, s32[256,128]{1,0:T(8,128)}, u32[]{:S(2)}) %copy-start.18) | copy-done | bytes 131096
  6.2 0.9 %copy-done.19 = s32[256,128]{1,0:T(8,128)S(1)} copy-done((s32[256,128]{1,0:T(8,128)S(1)}, s32[256,128]{1,0:T(8,128)}, u32[]{:S(2)}) %copy-start.19) | copy-done | bytes 131096
  7.1 0.9 %copy-done.20 = s32[256,128]{1,0:T(8,128)S(1)} copy-done((s32[256,128]{1,0:T(8,128)S(1)}, s32[256,128]{1,0:T(8,128)}, u32[]{:S(2)}) %copy-start.20) | copy-done | bytes 131096
  8.0 0.7 %copy-done.21 = f32[8]{0:T(128)S(1)} copy-done((f32[8]{0:T(128)S(1)}, f32[8]{0:T(128)}, u32[]{:S(2)}) %copy-start.21) | copy-done | bytes 56
  8.6 2.2 %prepare.1 = (f32[11,2,128,128]{3,2,1,0:T(8,128)S(1)}, f32[11,2,8,128]{3,2,1,0:T(8,128)S(1)}, f32[11,2,8,128]{3,2,1,0:T(8,128)S(1)}, f32[16,128]{1,0:T(8,128)}, f32[8,128]{1,0:T(8,128)S(1)}) custom-call(f32[3,256,128]{2,1,0:T(8,128)S(1)} %copy-done.13, f32[256,128]{1,0:T(8,128)S(1)} %copy-done.14, f32[256,128]{1,0:T(8,128)S(1)} %copy-done.15, ...), custom_call_target="tpu_custom_call" | custom-call | flops 3276800 | bytes 2945056 | tf_op jit(solution)/shard_map/prepare/pallas_call | solution.py:499
  10.8 1.1 %copy-done.5 = f32[11,2,128,128]{3,2,1,0:T(8,128)} copy-done((f32[11,2,128,128]{3,2,1,0:T(8,128)}, f32[11,2,128,128]{3,2,1,0:T(8,128)S(1)}, u32[]{:S(2)}) %copy-start.5) | copy-done | bytes 1441816
  11.9 0.5 collective-permute-start
  12.4 0.7 %collective-permute-start.1 = (f32[11,2,8,128]{3,2,1,0:T(8,128)S(1)}, f32[11,2,8,128]{3,2,1,0:T(8,128)S(1)}, u32[]{:S(2)}, u32[]{:S(2)}) collective-permute-start(f32[11,2,8,128]{3,2,1,0:T(8,128)S(1)} %get-tuple-element.19), channel_id=1, source_target_pairs={{1,2},{2,1},{3,4},{4,3},{5,6},{6,5},{7,8},{8,7},{9,10},{10,9},{11,... | collective-permute-start | bytes 270344 | tf_op jit(solution)/shard_map/ppermute | solution.py:514
  13.0 8.8 %all-to-all-start = ((f32[16,1,128]{2,1,0:T(1,128)}), f32[16,1,128]{2,1,0:T(1,128)S(1)}, u32[]{:S(2)}, u32[]{:S(2)}) async-start(f32[16,1,128]{2,1,0:T(1,128)} %bitcast.1), calls=%async_computation | async-start | bytes 16384 | tf_op jit(solution)/shard_map/all_to_all | solution.py:518
  21.9 1.4 %copy-done.6 = f32[11,2,128,128]{3,2,1,0:T(8,128)S(1)} copy-done((f32[11,2,128,128]{3,2,1,0:T(8,128)S(1)}, f32[11,2,128,128]{3,2,1,0:T(8,128)}, u32[]{:S(2)}) %copy-start.6) | copy-done | bytes 1441816
  23.2 1.4 %open_step.1 = (f32[11,2,160,128]{3,2,1,0:T(8,128)S(1)}, f32[8,2,160,128]{3,2,1,0:T(8,128)S(1)}, f32[6,2,160,128]{3,2,1,0:T(8,128)S(1)}) custom-call(f32[11,2,128,128]{3,2,1,0:T(8,128)S(1)} %copy-done.6, f32[11,2,8,128]{3,2,1,0:T(8,128)S(1)} %collective-permute-done.edge_a, f32[11,2,8,128]{3,2,1,0:T(8,128)S(1)} %collective-permute-done.1.edge_b), custom_call_target="tpu_custom_call" | custom-call | flops 3276800 | bytes 5718016 | tf_op jit(solution)/shard_map/open_step/pallas_call | solution.py:499
  24.6 0.9 %copy-done.9 = f32[6,2,160,128]{3,2,1,0:T(8,128)} copy-done((f32[6,2,160,128]{3,2,1,0:T(8,128)}, f32[6,2,160,128]{3,2,1,0:T(8,128)S(1)}, u32[]{:S(2)}) %copy-start.9) | copy-done | bytes 983064
  25.6 2.6 %all-to-all-done = f32[16,1,128]{2,1,0:T(1,128)S(1)} async-done(((f32[16,1,128]{2,1,0:T(1,128)}), f32[16,1,128]{2,1,0:T(1,128)S(1)}, u32[]{:S(2)}, u32[]{:S(2)}) %all-to-all-start) | async-done | bytes 8224 | tf_op jit(solution)/shard_map/all_to_all | solution.py:518
  28.2 2.0 %middle.1 = (f32[7,2,160,128]{3,2,1,0:T(8,128)S(1)}, f32[3,2,160,128]{3,2,1,0:T(8,128)S(1)}, f32[16,128]{1,0:T(8,128)}) custom-call(f32[16,128]{1,0:T(8,128)S(1)} %bitcast.8, f32[11,2,160,128]{3,2,1,0:T(8,128)S(1)} %get-tuple-element.20.ext, f32[8,2,160,128]{3,2,1,0:T(8,128)S(1)} %get-tuple-element.21.xy, f32[8,128]{1,0:T(8,128)S(1)} %get-tuple-element.22.count_row), custom_call_target="tpu_custom_call" | custom-call | flops 3932160 | bytes 4771840 | tf_op jit(solution)/shard_map/middle/pallas_call | solution.py:499
  30.2 1.0 %copy-done = f32[7,2,160,128]{3,2,1,0:T(8,128)} copy-done((f32[7,2,160,128]{3,2,1,0:T(8,128)}, f32[7,2,160,128]{3,2,1,0:T(8,128)S(1)}, u32[]{:S(2)}) %copy-start) | copy-done | bytes 1146904
  31.3 0.8 %copy-done.11 = f32[3,2,160,128]{3,2,1,0:T(8,128)} copy-done((f32[3,2,160,128]{3,2,1,0:T(8,128)}, f32[3,2,160,128]{3,2,1,0:T(8,128)S(1)}, u32[]{:S(2)}) %copy-start.11) | copy-done | bytes 491544
  32.0 3.5 %all-to-all-start.1 = ((f32[16,1,128]{2,1,0:T(1,128)}), f32[16,1,128]{2,1,0:T(1,128)S(1)}, u32[]{:S(2)}, u32[]{:S(2)}) async-start(f32[16,1,128]{2,1,0:T(1,128)} %bitcast.4), calls=%async_computation.1 | async-start | bytes 16384 | tf_op jit(solution)/shard_map/all_to_all | solution.py:518
  35.5 1.2 %copy-done.1 = f32[7,2,160,128]{3,2,1,0:T(8,128)S(1)} copy-done((f32[7,2,160,128]{3,2,1,0:T(8,128)S(1)}, f32[7,2,160,128]{3,2,1,0:T(8,128)}, u32[]{:S(2)}) %copy-start.1) | copy-done | bytes 1146904
  36.8 1.0 %copy-done.12 = f32[3,2,160,128]{3,2,1,0:T(8,128)S(1)} copy-done((f32[3,2,160,128]{3,2,1,0:T(8,128)S(1)}, f32[3,2,160,128]{3,2,1,0:T(8,128)}, u32[]{:S(2)}) %copy-start.12) | copy-done | bytes 491544
  37.8 3.8 %tangents.1 = (f32[7,2,160,128]{3,2,1,0:T(8,128)S(1)}, f32[9,2,160,128]{3,2,1,0:T(8,128)S(1)}, f32[2,2,160,128]{3,2,1,0:T(8,128)S(1)}) custom-call(f32[16,128]{1,0:T(8,128)S(1)} %bitcast.9, f32[11,2,160,128]{3,2,1,0:T(8,128)S(1)} %get-tuple-element.20.ext, f32[8,2,160,128]{3,2,1,0:T(8,128)S(1)} %get-tuple-element.21.xy, f32[7,2,160,128]{3,2,1,0:T(8,128)S(1)} %copy-done.1, ...), custom_call_target="tpu_custom_call" | custom-call | flops 6553600 | bytes 7708672 | tf_op jit(solution)/shard_map/tangents/pallas_call | solution.py:499
  41.6 1.1 %copy-done.3 = f32[9,2,160,128]{3,2,1,0:T(8,128)} copy-done((f32[9,2,160,128]{3,2,1,0:T(8,128)}, f32[9,2,160,128]{3,2,1,0:T(8,128)S(1)}, u32[]{:S(2)}) %copy-start.3) | copy-done | bytes 1474584
  42.8 1.0 %copy-done.7 = f32[7,2,160,128]{3,2,1,0:T(8,128)} copy-done((f32[7,2,160,128]{3,2,1,0:T(8,128)}, f32[7,2,160,128]{3,2,1,0:T(8,128)S(1)}, u32[]{:S(2)}) %copy-start.7) | copy-done | bytes 1146904
  43.8 1.3 %copy-done.2 = f32[7,2,160,128]{3,2,1,0:T(8,128)S(1)} copy-done((f32[7,2,160,128]{3,2,1,0:T(8,128)S(1)}, f32[7,2,160,128]{3,2,1,0:T(8,128)}, u32[]{:S(2)}) %copy-start.2) | copy-done | bytes 1146904
  45.0 1.4 %copy-done.4 = f32[9,2,160,128]{3,2,1,0:T(8,128)S(1)} copy-done((f32[9,2,160,128]{3,2,1,0:T(8,128)S(1)}, f32[9,2,160,128]{3,2,1,0:T(8,128)}, u32[]{:S(2)}) %copy-start.4) | copy-done | bytes 1474584
  46.4 1.3 %copy-done.8 = f32[7,2,160,128]{3,2,1,0:T(8,128)S(1)} copy-done((f32[7,2,160,128]{3,2,1,0:T(8,128)S(1)}, f32[7,2,160,128]{3,2,1,0:T(8,128)}, u32[]{:S(2)}) %copy-start.8) | copy-done | bytes 1146904
  47.7 1.2 %copy-done.10 = f32[6,2,160,128]{3,2,1,0:T(8,128)S(1)} copy-done((f32[6,2,160,128]{3,2,1,0:T(8,128)S(1)}, f32[6,2,160,128]{3,2,1,0:T(8,128)}, u32[]{:S(2)}) %copy-start.10) | copy-done | bytes 983064
  48.9 4.3 %finish.1 = (f32[256,128]{1,0:T(8,128)}, f32[256,128]{1,0:T(8,128)}) custom-call(f32[16,128]{1,0:T(8,128)S(1)} %bitcast.10, f32[16,128]{1,0:T(8,128)S(1)} %bitcast.11, f32[11,2,160,128]{3,2,1,0:T(8,128)S(1)} %get-tuple-element.20.ext, f32[6,2,160,128]{3,2,1,0:T(8,128)S(1)} %copy-done.10, f32[7,2,160,128]{3,2,1,0:T(8,128)S(1)} %copy-done.2, ...), custom_call_target="tpu_custom_call" | custom-call | flops 6553600 | bytes 7159808 | tf_op jit(solution)/shard_map/finish/pallas_call | solution.py:499
  (25 shorter events, 0.0 us)
Async XLA Ops:
  0.6 1.0 %copy-start.13 = (f32[3,256,128]{2,1,0:T(8,128)S(1)}, f32[3,256,128]{2,1,0:T(8,128)}, u32[]{:S(2)}) copy-start(f32[3,256,128]{2,1,0:T(8,128)} %state.1) | copy-start | bytes 1179652
  1.6 0.9 %copy-start.14 = (f32[256,128]{1,0:T(8,128)S(1)}, f32[256,128]{1,0:T(8,128)}, u32[]{:S(2)}) copy-start(f32[256,128]{1,0:T(8,128)} %log_mu.1) | copy-start | bytes 393220
  2.5 0.9 %copy-start.15 = (f32[256,128]{1,0:T(8,128)S(1)}, f32[256,128]{1,0:T(8,128)}, u32[]{:S(2)}) copy-start(f32[256,128]{1,0:T(8,128)} %log_xi.1) | copy-start | bytes 393220
  3.4 0.9 %copy-start.16 = (f32[256,128]{1,0:T(8,128)S(1)}, f32[256,128]{1,0:T(8,128)}, u32[]{:S(2)}) copy-start(f32[256,128]{1,0:T(8,128)} %dir_mu.1) | copy-start | bytes 393220
  4.3 0.9 %copy-start.17 = (f32[256,128]{1,0:T(8,128)S(1)}, f32[256,128]{1,0:T(8,128)}, u32[]{:S(2)}) copy-start(f32[256,128]{1,0:T(8,128)} %dir_xi.1) | copy-start | bytes 393220
  5.2 0.9 %copy-start.18 = (s32[256,128]{1,0:T(8,128)S(1)}, s32[256,128]{1,0:T(8,128)}, u32[]{:S(2)}) copy-start(s32[256,128]{1,0:T(8,128)} %wet.1) | copy-start | bytes 393220
  6.2 0.9 %copy-start.19 = (s32[256,128]{1,0:T(8,128)S(1)}, s32[256,128]{1,0:T(8,128)}, u32[]{:S(2)}) copy-start(s32[256,128]{1,0:T(8,128)} %observed.1) | copy-start | bytes 393220
  7.1 0.9 %copy-start.20 = (s32[256,128]{1,0:T(8,128)S(1)}, s32[256,128]{1,0:T(8,128)}, u32[]{:S(2)}) copy-start(s32[256,128]{1,0:T(8,128)} %terrain.1) | copy-start | bytes 393220
  8.0 0.7 %copy-start.21 = (f32[8]{0:T(128)S(1)}, f32[8]{0:T(128)}, u32[]{:S(2)}) copy-start(f32[8]{0:T(128)} %class_weight.1) | copy-start | bytes 100
  10.8 1.1 %copy-start.5 = (f32[11,2,128,128]{3,2,1,0:T(8,128)}, f32[11,2,128,128]{3,2,1,0:T(8,128)S(1)}, u32[]{:S(2)}) copy-start(f32[11,2,128,128]{3,2,1,0:T(8,128)S(1)} %get-tuple-element.17.own) | copy-start | bytes 4325380
  11.9 9.9 %collective-permute-start = (f32[11,2,8,128]{3,2,1,0:T(8,128)S(1)}, f32[11,2,8,128]{3,2,1,0:T(8,128)S(1)}, u32[]{:S(2)}, u32[]{:S(2)}) collective-permute-start(f32[11,2,8,128]{3,2,1,0:T(8,128)S(1)} %get-tuple-element.18), channel_id=1, source_target_pairs={{0,1},{1,0},{2,3},{3,2},{4,5},{5,4},{6,7},{7,6},{8,9},{9,8},{10,11... | collective-permute-start | bytes 270344 | tf_op jit(solution)/shard_map/ppermute | solution.py:514
  12.4 9.5 %collective-permute-start.1 = (f32[11,2,8,128]{3,2,1,0:T(8,128)S(1)}, f32[11,2,8,128]{3,2,1,0:T(8,128)S(1)}, u32[]{:S(2)}, u32[]{:S(2)}) collective-permute-start(f32[11,2,8,128]{3,2,1,0:T(8,128)S(1)} %get-tuple-element.19), channel_id=1, source_target_pairs={{1,2},{2,1},{3,4},{4,3},{5,6},{6,5},{7,8},{8,7},{9,10},{10,9},{11,... | collective-permute-start | bytes 270344 | tf_op jit(solution)/shard_map/ppermute | solution.py:514
  13.0 15.1 %all-to-all-start = ((f32[16,1,128]{2,1,0:T(1,128)}), f32[16,1,128]{2,1,0:T(1,128)S(1)}, u32[]{:S(2)}, u32[]{:S(2)}) async-start(f32[16,1,128]{2,1,0:T(1,128)} %bitcast.1), calls=%async_computation | async-start | bytes 16384 | tf_op jit(solution)/shard_map/all_to_all | solution.py:518
  21.9 1.4 %copy-start.6 = (f32[11,2,128,128]{3,2,1,0:T(8,128)S(1)}, f32[11,2,128,128]{3,2,1,0:T(8,128)}, u32[]{:S(2)}) copy-start(f32[11,2,128,128]{3,2,1,0:T(8,128)} %copy-done.5) | copy-start | bytes 4325380
  24.6 0.9 %copy-start.9 = (f32[6,2,160,128]{3,2,1,0:T(8,128)}, f32[6,2,160,128]{3,2,1,0:T(8,128)S(1)}, u32[]{:S(2)}) copy-start(f32[6,2,160,128]{3,2,1,0:T(8,128)S(1)} %get-tuple-element.24.base) | copy-start | bytes 2949124
  30.2 1.0 %copy-start = (f32[7,2,160,128]{3,2,1,0:T(8,128)}, f32[7,2,160,128]{3,2,1,0:T(8,128)S(1)}, u32[]{:S(2)}) copy-start(f32[7,2,160,128]{3,2,1,0:T(8,128)S(1)} %get-tuple-element.25.at_one) | copy-start | bytes 3440644
  31.3 0.8 %copy-start.11 = (f32[3,2,160,128]{3,2,1,0:T(8,128)}, f32[3,2,160,128]{3,2,1,0:T(8,128)S(1)}, u32[]{:S(2)}) copy-start(f32[3,2,160,128]{3,2,1,0:T(8,128)S(1)} %get-tuple-element.26.mid) | copy-start | bytes 1474564
  32.0 11.7 %all-to-all-start.1 = ((f32[16,1,128]{2,1,0:T(1,128)}), f32[16,1,128]{2,1,0:T(1,128)S(1)}, u32[]{:S(2)}, u32[]{:S(2)}) async-start(f32[16,1,128]{2,1,0:T(1,128)} %bitcast.4), calls=%async_computation.1 | async-start | bytes 16384 | tf_op jit(solution)/shard_map/all_to_all | solution.py:518
  35.5 1.3 %copy-start.1 = (f32[7,2,160,128]{3,2,1,0:T(8,128)S(1)}, f32[7,2,160,128]{3,2,1,0:T(8,128)}, u32[]{:S(2)}) copy-start(f32[7,2,160,128]{3,2,1,0:T(8,128)} %copy-done) | copy-start | bytes 3440644
  36.8 1.0 %copy-start.12 = (f32[3,2,160,128]{3,2,1,0:T(8,128)S(1)}, f32[3,2,160,128]{3,2,1,0:T(8,128)}, u32[]{:S(2)}) copy-start(f32[3,2,160,128]{3,2,1,0:T(8,128)} %copy-done.11) | copy-start | bytes 1474564
  41.6 1.1 %copy-start.3 = (f32[9,2,160,128]{3,2,1,0:T(8,128)}, f32[9,2,160,128]{3,2,1,0:T(8,128)S(1)}, u32[]{:S(2)}) copy-start(f32[9,2,160,128]{3,2,1,0:T(8,128)S(1)} %get-tuple-element.28.at_mid) | copy-start | bytes 4423684
  42.8 1.0 %copy-start.7 = (f32[7,2,160,128]{3,2,1,0:T(8,128)}, f32[7,2,160,128]{3,2,1,0:T(8,128)S(1)}, u32[]{:S(2)}) copy-start(f32[7,2,160,128]{3,2,1,0:T(8,128)S(1)} %get-tuple-element.27.tan) | copy-start | bytes 3440644
  43.8 1.3 %copy-start.2 = (f32[7,2,160,128]{3,2,1,0:T(8,128)S(1)}, f32[7,2,160,128]{3,2,1,0:T(8,128)}, u32[]{:S(2)}) copy-start(f32[7,2,160,128]{3,2,1,0:T(8,128)} %copy-done) | copy-start | bytes 3440644
  45.0 1.4 %copy-start.4 = (f32[9,2,160,128]{3,2,1,0:T(8,128)S(1)}, f32[9,2,160,128]{3,2,1,0:T(8,128)}, u32[]{:S(2)}) copy-start(f32[9,2,160,128]{3,2,1,0:T(8,128)} %copy-done.3) | copy-start | bytes 4423684
  46.4 1.3 %copy-start.8 = (f32[7,2,160,128]{3,2,1,0:T(8,128)S(1)}, f32[7,2,160,128]{3,2,1,0:T(8,128)}, u32[]{:S(2)}) copy-start(f32[7,2,160,128]{3,2,1,0:T(8,128)} %copy-done.7) | copy-start | bytes 3440644
  47.7 1.2 %copy-start.10 = (f32[6,2,160,128]{3,2,1,0:T(8,128)S(1)}, f32[6,2,160,128]{3,2,1,0:T(8,128)}, u32[]{:S(2)}) copy-start(f32[6,2,160,128]{3,2,1,0:T(8,128)} %copy-done.9) | copy-start | bytes 2949124
where the time goes:
time: 53.8 us; the launch traced here: 53.2 us
  local copies, waits for them, and re-layouts  22.7 us (42%)
  Pallas kernels  13.7 us (25%)
  starting transfers between devices  13.4 us (25%)
  waiting for transfers between devices  2.62 us (5%)
  between operations  0.75 us (1%)
    unnamed x44, local copies, waits for them, and re-layouts  22.7 us
    pallas_call x5, Pallas kernels, call(): pl.pallas_call(body, name=name, out_shape=outs, in_specs=[SMEM if i in sm...  13.7 us
    all_to_all x2, starting transfers between devices, share(): return lax.all_to_all(row, 'cross', 0, 0, tiled=True)  12.3 us
    all_to_all x2, waiting for transfers between devices, share(): return lax.all_to_all(row, 'cross', 0, 0, tiled=True)  2.62 us
  transfers between devices with their start and end apart: 4, of which 1 were waited for; matrix products, arithmetic and copies ran while one was open for 0% of the time, Pallas kernels for 10%

commit v1 on v0

--- a/solution.py
+++ b/solution.py
@@ -18,7 +18,7 @@
 TILE = 8
 H, Q1, Q2, FA, FB, DA, DB, DM, DX, WR, OB = range(11)
 FIELDS = 11
-UNROLL = 2
+UNROLL = 6
 
 
 def load(ref, k, col, groups):
@@ -106,42 +106,60 @@
     return inv_speed, speed, dry * height * inv_speed, turbulent * speed
 
 
-def splat_max(rows, shape):
-    return jnp.broadcast_to(jnp.max(rows, axis=0, keepdims=True), shape)
-
-
-def prepare(state, log_mu, log_xi, dir_mu, dir_xi, wet, observed, terrain, class_weight,
-            own, edge_a, edge_b, row, count_row, code, turned):
+def first_speed(state, row, held, arrived):
+    rows, cols = state.shape[1:]
+    parts = held.shape[0]
+    size = rows // parts
+    copies = []
+    for i in range(parts):
+        copies.append(pltpu.make_async_copy(state.at[:, pl.ds(i * size, size), :], held.at[i], arrived.at[i]))
+        copies[i].start()
+    top = jnp.zeros((16, cols), jnp.float32)
+    for i in range(parts):
+        copies[i].wait()
+        for j in range(0, size, 16):
+            top = jnp.maximum(top, speed_of(*(held[i, k, j : j + 16, :] for k in range(3))))
+    row[...] = jnp.full(row.shape, jnp.max(top), jnp.float32)
+
+
+def prepare(*refs):
+    sources, rest = refs[:9], refs[10:]
+    own, edge_a, edge_b, count_row, code, turned = rest[:6]
+    held, arrived = rest[6:15], rest[15]
+    copies = [pltpu.make_async_copy(src, dst, arrived.at[i]) for i, (src, dst) in enumerate(zip(sources, held))]
+    order = (6, 5, 7, 0, 3, 4, 1, 2, 8)
+    for i in order:
+        copies[i].start()
+    state, log_mu, log_xi, dir_mu, dir_xi, wet, observed, terrain, class_weight = held
     rows, cols = log_mu.shape
     groups = rows // LANES
-    step_rows = 16
-
-    def scan(i, carry):
-        top, seen = carry
-        at = pl.ds(pl.multiple_of(i * step_rows, step_rows), step_rows)
-        seen_here = observed[at, :]
-        code[at, :] = (wet[at, :] + 2 * seen_here + 4 * terrain[at, :]).astype(jnp.float32)
-        here = speed_of(state[0, at, :], state[1, at, :], state[2, at, :])
-        return jnp.maximum(top, here), seen + seen_here.astype(jnp.float32)
-
-    zero = jnp.zeros((step_rows, cols), jnp.float32)
-    top, seen = lax.fori_loop(0, rows // step_rows, scan, (zero, zero))
-    row[...] = jnp.full(row.shape, jnp.max(top), jnp.float32)
+    for i in (5, 6, 7):
+        copies[i].wait()
+    seen = jnp.zeros((16, cols), jnp.float32)
+    for i in range(0, rows, 16):
+        seen_here = observed[i : i + 16, :]
+        code[i : i + 16, :] = (wet[i : i + 16, :] + 2 * seen_here + 4 * terrain[i : i + 16, :]).astype(jnp.float32)
+        seen += seen_here.astype(jnp.float32)
     count_row[...] = jnp.full(count_row.shape, jnp.sum(seen), jnp.float32)
 
+    copies[0].wait()
     for g in range(groups):
         at = pl.ds(g * LANES, LANES)
         for k in range(3):
             own[k, g] = state[k, at, :].T
+        turned[2, g] = code[at, :].T
+    for i in (1, 2, 3, 4, 8):
+        copies[i].wait()
+    for g in range(groups):
+        at = pl.ds(g * LANES, LANES)
         own[DM, g] = dir_mu[at, :].T
         own[DX, g] = dir_xi[at, :].T
         turned[0, g] = log_mu[at, :].T
         turned[1, g] = log_xi[at, :].T
-        turned[2, g] = code[at, :].T
 
     def derive(i, carry):
-        for g in range(groups):
-            at = pl.ds(pl.multiple_of(i * TILE, TILE), TILE)
+        for g, half in ((g, half) for g in range(groups) for half in range(2)):
+            at = pl.ds(pl.multiple_of((2 * i + half) * TILE, TILE), TILE)
             bits = turned[2, g, at, :].astype(jnp.int32)
             wet_here = (bits & 1).astype(jnp.float32)
             kind = bits >> 2
@@ -158,7 +176,7 @@
             own[WR, g, at, :] = weight
         return carry
 
-    lax.fori_loop(0, cols // TILE, derive, 0)
+    lax.fori_loop(0, cols // (2 * TILE), derive, 0)
     even = lax.rem(lax.axis_index("cross"), 2) == 0
     for k in range(FIELDS):
         for g in range(groups):
@@ -224,11 +242,11 @@
 MU, MV, MZ, MW, ME, MB, MM, MH, MY = range(9)
 
 
-def middle(ends_of, top_rows, ext, xy, count_row, at_one, mid, row, work):
+def middle(ends_of, top, top_last, ext, xy, count_row, at_one, mid, row, work):
     groups, cols = ext.shape[1], ext.shape[2] - 4 * TILE
     grid = Grid(groups, cols)
     ends = ends_of()
-    dt = COURANT / splat_max(top_rows[...], grid.lane.shape)
+    dt = COURANT / jnp.broadcast_to(jnp.maximum(top[...], top_last[...]), grid.lane.shape)
     half = 0.5 * dt
 
     def first(t, col):
@@ -259,7 +277,7 @@
 
     grid.sweep(first)
 
-    def second(t, col, top):
+    def second(t, col, most):
         keep = grid.inside(t, ends)
         found = []
         for k, (value, flux) in enumerate(((0, 2), (1, 3), (2, 4))):
@@ -269,19 +287,17 @@
             found.append(jnp.where(keep, 0.5 * total, 0.0))
             grid.put(mid, k, col, found[k])
         own = (t > 0) & (t < grid.tiles - 1)
-        return jnp.maximum(top, jnp.where(own, speed_of(*found), 0.0))
-
-    top = grid.sweep(second, carry=jnp.zeros(grid.lane.shape, jnp.float32))
-    lane = lax.broadcasted_iota(jnp.int32, row.shape, 1)
-    count = jnp.broadcast_to(count_row[:1, :], row.shape)
-    row[...] = jnp.where(lane < LANES // 2, jnp.full(row.shape, jnp.max(top), jnp.float32), count)
-
-
-def tangents(ends_of, top_rows, ext, xy, at_one, mid, tan, at_mid, smooth, work):
-    groups, cols = ext.shape[1], ext.shape[2] - 4 * TILE
+        return jnp.maximum(most, jnp.where(own, speed_of(*found), 0.0))
+
+    fastest = grid.sweep(second, carry=jnp.zeros(grid.lane.shape, jnp.float32))
+    row[0:1, :] = jnp.full((1, LANES), jnp.max(fastest), jnp.float32)
+    row[1:2, :] = count_row[...]
+
+
+def tangent_one(top, top_last, xy, at_one, one):
+    groups, cols = xy.shape[1], xy.shape[2] - 4 * TILE
     grid = Grid(groups, cols)
-    ends = ends_of()
-    dt = COURANT / splat_max(top_rows[...], grid.lane.shape)
+    dt = COURANT / jnp.broadcast_to(jnp.maximum(top[...], top_last[...]), grid.lane.shape)
     half = 0.5 * dt
 
     def first(t, col):
@@ -291,27 +307,34 @@
         along = grid.get(at_one, CZ, col) * (u * tp + v * tq) + grid.get(at_one, CD, col)
         mixed = v * tp + u * tq
         for k, value in enumerate((tp, tq, mixed, 2.0 * v * tq)):
-            grid.put(work, k, col, value)
+            grid.put(one, k, col, value)
         moved = half * tp
-        grid.put(tan, 0, col, grid.rows_prev(moved) - grid.rows_next(moved))
+        grid.put(one, 4, col, grid.rows_prev(moved) - grid.rows_next(moved))
         sources = (-dt * (u * along + w * tp), -dt * (v * along + w * tq))
         for k, (value, flux) in enumerate(((tp, 2.0 * u * tp), (tq, mixed))):
             tenth, moved = 0.1 * value, half * flux
             total = 0.6 * value + sources[k]
             total += grid.rows_next(tenth - moved) + grid.rows_prev(tenth + moved)
-            grid.put(tan, 1 + k, col, total)
+            grid.put(one, 5 + k, col, total)
 
     grid.sweep(first)
+
+def tangent_mid(ends_of, top, top_last, ext, one, mid, part, at_mid, work):
+    groups, cols = ext.shape[1], ext.shape[2] - 4 * TILE
+    grid = Grid(groups, cols)
+    ends = ends_of()
+    dt = COURANT / jnp.broadcast_to(jnp.maximum(top[...], top_last[...]), grid.lane.shape)
+    half = 0.5 * dt
 
     def second(t, col):
         keep = grid.inside(t, ends)
-        qn, qp = grid.both_cols(work, 1, col)
-        pn, pp = grid.both_cols(work, 0, col)
-        gn, gp = grid.both_cols(work, 2, col)
-        fn, fp = grid.both_cols(work, 3, col)
-        th = grid.get(tan, 0, col) - half * (qn - qp)
-        tp = grid.get(tan, 1, col) + 0.1 * (pn + pp) - half * (gn - gp)
-        tq = grid.get(tan, 2, col) + 0.1 * (qn + qp) - half * (fn - fp)
+        qn, qp = grid.both_cols(one, 1, col)
+        pn, pp = grid.both_cols(one, 0, col)
+        gn, gp = grid.both_cols(one, 2, col)
+        fn, fp = grid.both_cols(one, 3, col)
+        th = grid.get(one, 4, col) - half * (qn - qp)
+        tp = grid.get(one, 5, col) + 0.1 * (pn + pp) - half * (gn - gp)
+        tq = grid.get(one, 6, col) + 0.1 * (qn + qp) - half * (fn - fp)
         th, tp, tq = (jnp.where(keep, 0.5 * x, 0.0) for x in (th, tp, tq))
         height, down, across = (grid.get(mid, k, col) for k in range(3))
         inv, u, v = velocities(height, down, across)
@@ -331,35 +354,45 @@
         flux_down = 2.0 * u * tp + eight * th - u * u * lift
         mixed = v * tp + u * tq - u * v * lift
         for k, value in enumerate((th, tp, tq, mixed, 2.0 * v * tq + eight * th - v * v * lift)):
-            grid.put(work, 4 + k, col, value)
+            grid.put(work, k, col, value)
         hn, hp = grid.both_rows(th)
         pn, pp = grid.both_rows(tp)
         qn, qp = grid.both_rows(tq)
         fn, fp = grid.both_rows(flux_down)
         gn, gp = grid.both_rows(mixed)
-        grid.put(tan, 0, col, th)
-        grid.put(tan, 1, col, 0.6 * th + 0.1 * (hn + hp))
-        grid.put(tan, 2, col, 0.6 * tp + 0.1 * (pn + pp))
-        grid.put(tan, 3, col, 0.6 * tq + 0.1 * (qn + qp))
-        grid.put(tan, 4, col, -0.5 * (pn - pp))
-        grid.put(tan, 5, col, SIN_SLOPE * th - u * along - w * tp - 0.5 * (fn - fp))
-        grid.put(tan, 6, col, -v * along - w * tq - 0.5 * (gn - gp))
+        grid.put(part, 0, col, th)
+        grid.put(part, 1, col, 0.6 * th + 0.1 * (hn + hp))
+        grid.put(part, 2, col, 0.6 * tp + 0.1 * (pn + pp))
+        grid.put(part, 3, col, 0.6 * tq + 0.1 * (qn + qp))
+        grid.put(part, 4, col, -0.5 * (pn - pp))
+        grid.put(part, 5, col, SIN_SLOPE * th - u * along - w * tp - 0.5 * (fn - fp))
+        grid.put(part, 6, col, -v * along - w * tq - 0.5 * (gn - gp))
 
     grid.sweep(second)
+
+def tangent_end(ends_of, part, work, tan):
+    groups, cols = part.shape[1], part.shape[2] - 4 * TILE
+    grid = Grid(groups, cols)
+    ends = ends_of()
 
     def third(t, col):
         keep = grid.inside(t, ends)
-        hn, hp = grid.both_cols(work, 4, col)
-        pn, pp = grid.both_cols(work, 5, col)
-        qn, qp = grid.both_cols(work, 6, col)
-        gn, gp = grid.both_cols(work, 7, col)
-        fn, fp = grid.both_cols(work, 8, col)
+        hn, hp = grid.both_cols(work, 0, col)
+        pn, pp = grid.both_cols(work, 1, col)
+        qn, qp = grid.both_cols(work, 2, col)
+        gn, gp = grid.both_cols(work, 3, col)
+        fn, fp = grid.both_cols(work, 4, col)
+        grid.put(tan, 0, col, grid.get(part, 0, col))
         for k, (n, p) in enumerate(((hn, hp), (pn, pp), (qn, qp))):
-            grid.put(tan, 1 + k, col, jnp.where(keep, grid.get(tan, 1 + k, col) + 0.1 * (n + p), 0.0))
+            grid.put(tan, 1 + k, col, jnp.where(keep, grid.get(part, 1 + k, col) + 0.1 * (n + p), 0.0))
         for k, (n, p) in enumerate(((qn, qp), (gn, gp), (fn, fp))):
-            grid.put(tan, 4 + k, col, jnp.where(keep, grid.get(tan, 4 + k, col) - 0.5 * (n - p), 0.0))
+            grid.put(tan, 4 + k, col, jnp.where(keep, grid.get(part, 4 + k, col) - 0.5 * (n - p), 0.0))
 
     grid.sweep(third)
+
+def regularize(ext, smooth, work):
+    groups, cols = ext.shape[1], ext.shape[2] - 4 * TILE
+    grid = Grid(groups, cols)
 
     def laplace(ref, k, col):
         value = grid.get(ref, k, col)
@@ -381,19 +414,14 @@
     grid.sweep(bend_again, 1, grid.tiles - 1)
 
 
-def finish(ends_of, cells, top_rows, next_rows, ext, base, at_one, tan, at_mid, smooth, out_mu, out_xi, work, total):
+def finish(ends_of, cells, top, top_last, fast, fast_last, ext, base, at_one, tan, at_mid, smooth, out_mu, out_xi, work, total):
     groups, cols = ext.shape[1], ext.shape[2] - 4 * TILE
     grid = Grid(groups, cols)
     ends = ends_of()
     shape = grid.lane.shape
-    dt0 = COURANT / splat_max(top_rows[...], shape)
-    rows = next_rows[...]
-    lane = lax.broadcasted_iota(jnp.int32, (1, LANES), 1)
-    most = jnp.max(rows, axis=0, keepdims=True)
-    added = jnp.sum(rows, axis=0, keepdims=True)
-    dt1 = COURANT / jnp.broadcast_to(jnp.where(lane < LANES // 2, most, pltpu.roll(most, LANES // 2, 1)), shape)
-    count = jnp.where(lane < LANES // 2, pltpu.roll(added, LANES // 2, 1), added)
-    weight = jnp.broadcast_to((DATA_WEIGHT * cells) / count, shape)
+    dt0 = COURANT / jnp.broadcast_to(jnp.maximum(top[...], top_last[...]), shape)
+    dt1 = COURANT / jnp.broadcast_to(jnp.maximum(fast[0:1, :], fast_last[0:1, :]), shape)
+    weight = jnp.broadcast_to((DATA_WEIGHT * cells) / (fast[1:2, :] + fast_last[1:2, :]), shape)
     half1 = 0.5 * dt1
     half0 = 0.5 * dt0
 
@@ -490,19 +518,19 @@
 
 
 VMEM = pl.BlockSpec(memory_space=pltpu.VMEM)
-SMEM = pl.BlockSpec(memory_space=pltpu.SMEM)
-
-
-def call(body, name, operands, outs, scratch, flops, small=()):
+ANY = pl.BlockSpec(memory_space=pltpu.HBM)
+
+
+def call(body, name, operands, outs, scratch, flops, spaces=None):
     outs = [jax.ShapeDtypeStruct(shape, jnp.float32) for shape in outs]
     moved = 4 * sum(x.size for x in operands) + 4 * sum(x.size for x in outs)
     return pl.pallas_call(
         body,
         name=name,
         out_shape=outs,
-        in_specs=[SMEM if i in small else VMEM for i in range(len(operands))],
+        in_specs=spaces or [VMEM] * len(operands),
         out_specs=[VMEM] * len(outs),
-        scratch_shapes=[pltpu.VMEM(shape, jnp.float32) for shape in scratch],
+        scratch_shapes=[pltpu.VMEM(x, jnp.float32) if isinstance(x, tuple) else x for x in scratch],
         compiler_params=pltpu.CompilerParams(vmem_limit_bytes=24 * 1024 * 1024),
         cost_estimate=pl.CostEstimate(flops=flops, bytes_accessed=moved, transcendentals=0),
     )(*operands)
@@ -514,8 +542,25 @@
     return lax.ppermute(edge_a, "cross", pairs_a), lax.ppermute(edge_b, "cross", pairs_b)
 
 
-def share(row):
-    return lax.all_to_all(row, "cross", 0, 0, tiled=True)
+def exchange(row, step):
+    return lax.ppermute(row, "cross", [(i, i ^ step) for i in range(lax.axis_size("cross"))])
+
+
+def share(row, combine, first=1):
+    step = first
+    while 2 * step < lax.axis_size("cross"):
+        row = combine(row, exchange(row, step))
+        step *= 2
+    return row, exchange(row, step)
+
+
+def round_beside(row, step, result):
+    arrived, result = lax.optimization_barrier((exchange(row, step), result))
+    return max_and_sum(row, arrived), result
+
+
+def max_and_sum(a, b):
+    return jnp.where(lax.broadcasted_iota(jnp.int32, a.shape, 0) == 0, jnp.maximum(a, b), a + b)
 
 
 def local(state, log_mu, log_xi, dir_mu, dir_xi, wet, observed, terrain, class_weight):
@@ -527,41 +572,65 @@
     edge = (FIELDS, groups, TILE, LANES)
     work = rows * cols
 
-    own, edge_a, edge_b, row, count_row = call(
+    inputs = (state, log_mu, log_xi, dir_mu, dir_xi, wet, observed, terrain, class_weight)
+    inputs = tuple(pltpu.with_memory_space_constraint(x, pltpu.HBM) for x in inputs)
+    (row,) = call(
+        first_speed,
+        "first_speed",
+        inputs[:1],
+        [(1, LANES)],
+        [pltpu.VMEM((4, 3, rows // 4, cols), jnp.float32), pltpu.SemaphoreType.DMA((4,))],
+        20 * work,
+        spaces=(ANY,),
+    )
+    row = jnp.maximum(row, exchange(row, 1))
+    own, edge_a, edge_b, count_row = call(
         prepare,
         "prepare",
-        (state, log_mu, log_xi, dir_mu, dir_xi, wet, observed, terrain, class_weight),
-        [(FIELDS, groups, cols, LANES), edge, edge, (count, LANES), (TILE, LANES)],
-        [(rows, cols), (3, groups, cols, LANES)],
+        inputs + (row,),
+        [(FIELDS, groups, cols, LANES), edge, edge, (1, LANES)],
+        [(rows, cols), (3, groups, cols, LANES)]
+        + [pltpu.VMEM(x.shape, x.dtype) for x in inputs[:-1]]
+        + [pltpu.SMEM(class_weight.shape, jnp.float32), pltpu.SemaphoreType.DMA((len(inputs),))],
         100 * work,
-        small=(8,),
-    )
+        spaces=(ANY,) * 9 + (VMEM,),
+    )
+    row = jnp.maximum(row, exchange(row, 2))
+    row, edge_a, edge_b = lax.optimization_barrier((row, edge_a, edge_b))
     edge_a, edge_b = swap_edges(edge_a, edge_b, count)
-    top_rows = share(row)
+    top, top_last = share(row, jnp.maximum, 4)
     ext, xy, base = call(
         open_step, "open_step", (own, edge_a, edge_b), [(FIELDS,) + wide, (8,) + wide, (6,) + wide], [], 100 * work
     )
     at_one, mid, next_row = call(
         functools.partial(middle, end_flags),
         "middle",
-        (top_rows, ext, xy, count_row),
-        [(7,) + wide, (3,) + wide, (count, LANES)],
+        (top, top_last, ext, xy, count_row),
+        [(7,) + wide, (3,) + wide, (2, LANES)],
         [(5,) + wide],
         120 * work,
     )
-    next_rows = share(next_row)
-    tan, at_mid, smooth = call(
-        functools.partial(tangents, end_flags),
-        "tangents",
-        (top_rows, ext, xy, at_one, mid),
-        [(7,) + wide, (9,) + wide, (2,) + wide],
-        [(9,) + wide],
-        200 * work,
-    )
+    (smooth,) = call(regularize, "regularize", (ext,), [(2,) + wide], [(2,) + wide], 30 * work)
+    fast, smooth = round_beside(next_row, 1, smooth)
+    (one,) = call(tangent_one, "tangent_one", (top, top_last, xy, at_one), [(7,) + wide], [], 60 * work)
+    fast, one = round_beside(fast, 2, one)
+    part, at_mid, between = call(
+        functools.partial(tangent_mid, end_flags),
+        "tangent_mid",
+        (top, top_last, ext, one, mid),
+        [(7,) + wide, (9,) + wide, (5,) + wide],
+        [],
+        120 * work,
+    )
+    fast, part = round_beside(fast, 4, part)
+    (tan,) = call(
+        functools.partial(tangent_end, end_flags), "tangent_end", (part, between), [(7,) + wide], [], 30 * work
+    )
+    fast, fast_last = share(fast, max_and_sum, 8)
     out_mu, out_xi = call(
         functools.partial(finish, end_flags, float(cells)),
         "finish",
-        (top_rows, next_rows, ext, base, at_one, tan, at_mid, smooth),
+        (top, top_last, fast, fast_last, ext, base, at_one, tan, at_mid, smooth),
         [(rows, cols), (rows, cols)],
         [(7,) + wide, (2,) + wide],
         200 * work,

time: 53.8 us -> 36.6 us (0.68)
  local copies, waits for them, and re-layouts: 22.7 us -> 0 us
  waiting for transfers between devices: 2.62 us -> 10.8 us
  Pallas kernels: 13.7 us -> 9.63 us
  starting transfers between devices: 13.4 us -> 15 us
    unnamed x44 -> x0, local copies, waits for them, and re-layouts: 22.7 us -> none
    ppermute x0 -> x8, starting transfers between devices: none -> 14.3 us  [exchange(): lax.ppermute(row, 'cross', [(i, i ^ step) for i in range(lax.axis_size('c...]
    all_to_all x2 -> x0, starting transfers between devices: 12.3 us -> none  [share(): return lax.all_to_all(row, 'cross', 0, 0, tiled=True)]
    ppermute x0 -> x8, waiting for transfers between devices: none -> 10.8 us  [exchange(): lax.ppermute(row, 'cross', [(i, i ^ step) for i in range(lax.axis_size('c...]
    pallas_call x5 -> x9, Pallas kernels: 13.7 us -> 9.63 us  [call(): pl.pallas_call(body, name=name, out_shape=outs, in_specs=spaces or [VMEM]...]
    all_to_all x2 -> x0, waiting for transfers between devices: 2.62 us -> none  [share(): return lax.all_to_all(row, 'cross', 0, 0, tiled=True)]
  transfers between devices with their start and end apart: 4 -> 10, of which waited for: 1 -> 7; matrix products, arithmetic and copies ran while one was open for 0% -> 0% of each run, Pallas kernels for 10% -> 14%
where the time goes in v1:
time: 36.6 us; the launch traced here: 36.4 us
  starting transfers between devices  15 us (41%)
  waiting for transfers between devices  10.8 us (30%)
  Pallas kernels  9.63 us (26%)
  between operations  0.73 us (2%)
    ppermute x8, starting transfers between devices, exchange(): lax.ppermute(row, 'cross', [(i, i ^ step) for i in range(lax.axis_size('c...  14.3 us
    ppermute x8, waiting for transfers between devices, exchange(): lax.ppermute(row, 'cross', [(i, i ^ step) for i in range(lax.axis_size('c...  10.8 us
    pallas_call x9, Pallas kernels, call(): pl.pallas_call(body, name=name, out_shape=outs, in_specs=spaces or [VMEM]...  9.63 us
  transfers between devices with their start and end apart: 10, of which 7 were waited for; matrix products, arithmetic and copies ran while one was open for 0% of the time, Pallas kernels for 14%

profile of v1, /device:TPU:0, one launch (start us, length us, event | category | flops | bytes accessed | tf_op | source)
XLA Modules:
  0.0 36.4 jit_solution(10569965831649053125)
XLA Ops:
  0.6 1.2 %first_speed.1 = f32[1,128]{1,0:T(1,128)S(1)} custom-call(f32[3,256,128]{2,1,0:T(8,128)} %refs_0_.1), custom_call_target="tpu_custom_call" | custom-call | flops 655360 | bytes 393728 | tf_op jit(solution)/shard_map/first_speed/pallas_call | solution.py:527
  1.9 0.5 %collective-permute-start = (f32[1,128]{1,0:T(1,128)S(1)}, f32[1,128]{1,0:T(1,128)S(1)}, u32[]{:S(2)}, u32[]{:S(2)}) collective-permute-start(f32[1,128]{1,0:T(1,128)S(1)} %first_speed.1), channel_id=1, source_target_pairs={{0,1},{1,0},{2,3},{3,2},{4,5},{5,4},{6,7},{7,6},{8,9},{9,8},{10,11... | collective-permute-start | bytes 1544 | tf_op jit(solution)/shard_map/ppermute | solution.py:546
  2.4 0.8 %collective-permute-done = f32[1,128]{1,0:T(1,128)S(1)} collective-permute-done((f32[1,128]{1,0:T(1,128)S(1)}, f32[1,128]{1,0:T(1,128)S(1)}, u32[]{:S(2)}, u32[]{:S(2)}) %collective-permute-start) | collective-permute-done | bytes 544 | tf_op jit(solution)/shard_map/ppermute | solution.py:546
  3.2 2.8 %collective-permute-start.1 = (f32[1,128]{1,0:T(1,128)S(1)}, f32[1,128]{1,0:T(1,128)S(1)}, u32[]{:S(2)}, u32[]{:S(2)}) collective-permute-start(f32[1,128]{1,0:T(1,128)S(1)} %max.18.refs_9_), channel_id=1, source_target_pairs={{0,2},{1,3},{2,0},{3,1},{4,6},{5,7},{6,4},{7,5},{8,10},{9,11},{10,... | collective-permute-start | bytes 1544 | tf_op jit(solution)/shard_map/ppermute | solution.py:546
  6.0 1.9 %prepare.1 = (f32[11,2,128,128]{3,2,1,0:T(8,128)S(1)}, f32[11,2,8,128]{3,2,1,0:T(8,128)S(1)}, f32[11,2,8,128]{3,2,1,0:T(8,128)S(1)}, f32[1,128]{1,0:T(1,128)S(1)}) custom-call(f32[3,256,128]{2,1,0:T(8,128)} %refs_0_.1, f32[256,128]{1,0:T(8,128)} %refs_1_.1, f32[256,128]{1,0:T(8,128)} %refs_2_.1, f32[256,128]{1,0:T(8,128)} %refs_3_.1, f32[256,128]{1,0:T(8,128)} %refs_4_.1, ...), custom_call_target="tpu_custom_call" | custom-call | flops 3276800 | bytes 2933792 | tf_op jit(solution)/shard_map/prepare/pallas_call | solution.py:527
  8.0 0.0 collective-permute-done.1
  8.0 0.1 collective-permute-start.4
  8.1 0.7 %collective-permute-start.5 = (f32[11,2,8,128]{3,2,1,0:T(8,128)S(1)}, f32[11,2,8,128]{3,2,1,0:T(8,128)S(1)}, u32[]{:S(2)}, u32[]{:S(2)}) collective-permute-start(f32[11,2,8,128]{3,2,1,0:T(8,128)S(1)} %get-tuple-element.29), channel_id=1, source_target_pairs={{1,2},{2,1},{3,4},{4,3},{5,6},{6,5},{7,8},{8,7},{9,10},{10,9},{11,... | collective-permute-start | bytes 270344 | tf_op jit(solution)/shard_map/ppermute | solution.py:542
  8.7 4.4 %collective-permute-start.2 = (f32[1,128]{1,0:T(1,128)S(1)}, f32[1,128]{1,0:T(1,128)S(1)}, u32[]{:S(2)}, u32[]{:S(2)}) collective-permute-start(f32[1,128]{1,0:T(1,128)S(1)} %max.19), channel_id=1, source_target_pairs={{0,4},{1,5},{2,6},{3,7},{4,0},{5,1},{6,2},{7,3},{8,12},{9,13},{10,... | collective-permute-start | bytes 1544 | tf_op jit(solution)/shard_map/ppermute | solution.py:546
  13.1 2.4 %collective-permute-done.2 = f32[1,128]{1,0:T(1,128)S(1)} collective-permute-done((f32[1,128]{1,0:T(1,128)S(1)}, f32[1,128]{1,0:T(1,128)S(1)}, u32[]{:S(2)}, u32[]{:S(2)}) %collective-permute-start.2) | collective-permute-done | bytes 544 | tf_op jit(solution)/shard_map/ppermute | solution.py:546
  15.5 2.6 %collective-permute-start.3 = (f32[1,128]{1,0:T(1,128)S(1)}, f32[1,128]{1,0:T(1,128)S(1)}, u32[]{:S(2)}, u32[]{:S(2)}) collective-permute-start(f32[1,128]{1,0:T(1,128)S(1)} %max.20.top), channel_id=1, source_target_pairs={{0,8},{1,9},{2,10},{3,11},{4,12},{5,13},{6,14},{7,15},{8,0},{9,1},... | collective-permute-start | bytes 1544 | tf_op jit(solution)/shard_map/ppermute | solution.py:546
  18.1 0.0 collective-permute-done.4.edge_a
  18.1 0.0 collective-permute-done.5.edge_b
  18.1 0.9 %open_step.1 = (f32[11,2,160,128]{3,2,1,0:T(8,128)S(1)}, f32[8,2,160,128]{3,2,1,0:T(8,128)S(1)}, f32[6,2,160,128]{3,2,1,0:T(8,128)S(1)}) custom-call(f32[11,2,128,128]{3,2,1,0:T(8,128)S(1)} %get-tuple-element.27.own, f32[11,2,8,128]{3,2,1,0:T(8,128)S(1)} %collective-permute-done.4.edge_a, f32[11,2,8,128]{3,2,1,0:T(8,128)S(1)} %collective-permute-done.5.edge_b), custom_call_target="tpu_custom_call" | custom-call | flops 3276800 | bytes 5718016 | tf_op jit(solution)/shard_map/open_step/pallas_call | solution.py:527
  19.0 0.9 %collective-permute-done.3.top_last = f32[1,128]{1,0:T(1,128)S(1)} collective-permute-done((f32[1,128]{1,0:T(1,128)S(1)}, f32[1,128]{1,0:T(1,128)S(1)}, u32[]{:S(2)}, u32[]{:S(2)}) %collective-permute-start.3) | collective-permute-done | bytes 544 | tf_op jit(solution)/shard_map/ppermute | solution.py:546
  19.9 0.9 %middle.1 = (f32[7,2,160,128]{3,2,1,0:T(8,128)S(1)}, f32[3,2,160,128]{3,2,1,0:T(8,128)S(1)}, f32[2,128]{1,0:T(2,128)S(1)}) custom-call(f32[1,128]{1,0:T(1,128)S(1)} %max.20.top, f32[1,128]{1,0:T(1,128)S(1)} %collective-permute-done.3.top_last, f32[11,2,160,128]{3,2,1,0:T(8,128)S(1)} %get-tuple-element.30.ext, f32[8,2,160,128]{3,2,1,0:T(8,128)S(1)} %get-tuple-element.31.xy, ...), custom_call_target="tpu_custom_call" | custom-call | flops 3932160 | bytes 4753920 | tf_op jit(solution)/shard_map/middle/pallas_call | solution.py:527
  20.9 0.1 collective-permute-start.6
  20.9 0.7 %regularize.1.smooth = f32[2,2,160,128]{3,2,1,0:T(8,128)S(1)} custom-call(f32[11,2,160,128]{3,2,1,0:T(8,128)S(1)} %get-tuple-element.30.ext), custom_call_target="tpu_custom_call" | custom-call | flops 983040 | bytes 2129920 | tf_op jit(solution)/shard_map/regularize/pallas_call | solution.py:527
  21.7 0.4 %collective-permute-done.6 = f32[2,128]{1,0:T(2,128)S(1)} collective-permute-done((f32[2,128]{1,0:T(2,128)S(1)}, f32[2,128]{1,0:T(2,128)S(1)}, u32[]{:S(2)}, u32[]{:S(2)}) %collective-permute-start.6) | collective-permute-done | bytes 1056 | tf_op jit(solution)/shard_map/ppermute | solution.py:546
  22.1 0.1 add_select_fusion.2
  22.1 0.2 collective-permute-start.7
  22.3 0.5 %tangent_one.1.one = f32[7,2,160,128]{3,2,1,0:T(8,128)S(1)} custom-call(f32[1,128]{1,0:T(1,128)S(1)} %max.20.top, f32[1,128]{1,0:T(1,128)S(1)} %collective-permute-done.3.top_last, f32[8,2,160,128]{3,2,1,0:T(8,128)S(1)} %get-tuple-element.31.xy, f32[7,2,160,128]{3,2,1,0:T(8,128)S(1)} %get-tuple-element.35.at_one), custom_call_target="tpu_custom_call" | custom-call | flops 1966080 | bytes 3605504 | tf_op jit(solution)/shard_map/tangent_one/pallas_call | solution.py:527
  22.8 2.9 %collective-permute-done.7 = f32[2,128]{1,0:T(2,128)S(1)} collective-permute-done((f32[2,128]{1,0:T(2,128)S(1)}, f32[2,128]{1,0:T(2,128)S(1)}, u32[]{:S(2)}, u32[]{:S(2)}) %collective-permute-start.7) | collective-permute-done | bytes 1056 | tf_op jit(solution)/shard_map/ppermute | solution.py:546
  25.7 0.1 add_select_fusion.1
  25.8 1.1 %collective-permute-start.8 = (f32[2,128]{1,0:T(2,128)S(1)}, f32[2,128]{1,0:T(2,128)S(1)}, u32[]{:S(2)}, u32[]{:S(2)}) collective-permute-start(f32[2,128]{1,0:T(2,128)S(1)} %add_select_fusion.1), channel_id=1, source_target_pairs={{0,4},{1,5},{2,6},{3,7},{4,0},{5,1},{6,2},{7,3},{8,12},{9,13},{10,... | collective-permute-start | bytes 3080 | tf_op jit(solution)/shard_map/ppermute | solution.py:546
  26.9 0.8 %tangent_mid.1 = (f32[7,2,160,128]{3,2,1,0:T(8,128)S(1)}, f32[9,2,160,128]{3,2,1,0:T(8,128)S(1)}, f32[5,2,160,128]{3,2,1,0:T(8,128)S(1)}) custom-call(f32[1,128]{1,0:T(1,128)S(1)} %max.20.top, f32[1,128]{1,0:T(1,128)S(1)} %collective-permute-done.3.top_last, f32[11,2,160,128]{3,2,1,0:T(8,128)S(1)} %get-tuple-element.30.ext, ...), custom_call_target="tpu_custom_call" | custom-call | flops 3932160 | bytes 6882304 | tf_op jit(solution)/shard_map/tangent_mid/pallas_call | solution.py:527
  27.7 1.7 %collective-permute-done.8 = f32[2,128]{1,0:T(2,128)S(1)} collective-permute-done((f32[2,128]{1,0:T(2,128)S(1)}, f32[2,128]{1,0:T(2,128)S(1)}, u32[]{:S(2)}, u32[]{:S(2)}) %collective-permute-start.8) | collective-permute-done | bytes 1056 | tf_op jit(solution)/shard_map/ppermute | solution.py:546
  29.3 0.1 add_select_fusion.fast
  29.4 2.6 %collective-permute-start.9 = (f32[2,128]{1,0:T(2,128)S(1)}, f32[2,128]{1,0:T(2,128)S(1)}, u32[]{:S(2)}, u32[]{:S(2)}) collective-permute-start(f32[2,128]{1,0:T(2,128)S(1)} %add_select_fusion.fast), channel_id=1, source_target_pairs={{0,8},{1,9},{2,10},{3,11},{4,12},{5,13},{6,14},{7,15},{8,0},{9,1},... | collective-permute-start | bytes 3080 | tf_op jit(solution)/shard_map/ppermute | solution.py:546
  32.0 0.2 tangent_end.1.tan
  32.2 1.6 %collective-permute-done.9.fast_last = f32[2,128]{1,0:T(2,128)S(1)} collective-permute-done((f32[2,128]{1,0:T(2,128)S(1)}, f32[2,128]{1,0:T(2,128)S(1)}, u32[]{:S(2)}, u32[]{:S(2)}) %collective-permute-start.9) | collective-permute-done | bytes 1056 | tf_op jit(solution)/shard_map/ppermute | solution.py:546
  33.9 2.5 %finish.1 = (f32[256,128]{1,0:T(8,128)}, f32[256,128]{1,0:T(8,128)}) custom-call(f32[1,128]{1,0:T(1,128)S(1)} %max.20.top, f32[1,128]{1,0:T(1,128)S(1)} %collective-permute-done.3.top_last, f32[2,128]{1,0:T(2,128)S(1)} %add_select_fusion.fast, f32[2,128]{1,0:T(2,128)S(1)} %collective-permute-done.9.fast_last, f32[11,2,160,128]{3,2,1,0:T(8,128)S(1)} %get-tuple-element.30.ext, ...), custom_call_target="tpu_custom_call" | custom-call | flops 6553600 | bytes 7146496 | tf_op jit(solution)/shard_map/finish/pallas_call | solution.py:527
  (4 shorter events, 0.0 us)
Async XLA Ops:
  1.9 1.3 %collective-permute-start = (f32[1,128]{1,0:T(1,128)S(1)}, f32[1,128]{1,0:T(1,128)S(1)}, u32[]{:S(2)}, u32[]{:S(2)}) collective-permute-start(f32[1,128]{1,0:T(1,128)S(1)} %first_speed.1), channel_id=1, source_target_pairs={{0,1},{1,0},{2,3},{3,2},{4,5},{5,4},{6,7},{7,6},{8,9},{9,8},{10,11... | collective-permute-start | bytes 1544 | tf_op jit(solution)/shard_map/ppermute | solution.py:546
  3.2 4.8 %collective-permute-start.1 = (f32[1,128]{1,0:T(1,128)S(1)}, f32[1,128]{1,0:T(1,128)S(1)}, u32[]{:S(2)}, u32[]{:S(2)}) collective-permute-start(f32[1,128]{1,0:T(1,128)S(1)} %max.18.refs_9_), channel_id=1, source_target_pairs={{0,2},{1,3},{2,0},{3,1},{4,6},{5,7},{6,4},{7,5},{8,10},{9,11},{10,... | collective-permute-start | bytes 1544 | tf_op jit(solution)/shard_map/ppermute | solution.py:546
  8.0 10.1 %collective-permute-start.4 = (f32[11,2,8,128]{3,2,1,0:T(8,128)S(1)}, f32[11,2,8,128]{3,2,1,0:T(8,128)S(1)}, u32[]{:S(2)}, u32[]{:S(2)}) collective-permute-start(f32[11,2,8,128]{3,2,1,0:T(8,128)S(1)} %get-tuple-element.28), channel_id=1, source_target_pairs={{0,1},{1,0},{2,3},{3,2},{4,5},{5,4},{6,7},{7,6},{8,9},{9,8},{10,11... | collective-permute-start | bytes 270344 | tf_op jit(solution)/shard_map/ppermute | solution.py:542
  8.1 10.0 %collective-permute-start.5 = (f32[11,2,8,128]{3,2,1,0:T(8,128)S(1)}, f32[11,2,8,128]{3,2,1,0:T(8,128)S(1)}, u32[]{:S(2)}, u32[]{:S(2)}) collective-permute-start(f32[11,2,8,128]{3,2,1,0:T(8,128)S(1)} %get-tuple-element.29), channel_id=1, source_target_pairs={{1,2},{2,1},{3,4},{4,3},{5,6},{6,5},{7,8},{8,7},{9,10},{10,9},{11,... | collective-permute-start | bytes 270344 | tf_op jit(solution)/shard_map/ppermute | solution.py:542
  8.7 6.8 %collective-permute-start.2 = (f32[1,128]{1,0:T(1,128)S(1)}, f32[1,128]{1,0:T(1,128)S(1)}, u32[]{:S(2)}, u32[]{:S(2)}) collective-permute-start(f32[1,128]{1,0:T(1,128)S(1)} %max.19), channel_id=1, source_target_pairs={{0,4},{1,5},{2,6},{3,7},{4,0},{5,1},{6,2},{7,3},{8,12},{9,13},{10,... | collective-permute-start | bytes 1544 | tf_op jit(solution)/shard_map/ppermute | solution.py:546
  15.5 4.4 %collective-permute-start.3 = (f32[1,128]{1,0:T(1,128)S(1)}, f32[1,128]{1,0:T(1,128)S(1)}, u32[]{:S(2)}, u32[]{:S(2)}) collective-permute-start(f32[1,128]{1,0:T(1,128)S(1)} %max.20.top), channel_id=1, source_target_pairs={{0,8},{1,9},{2,10},{3,11},{4,12},{5,13},{6,14},{7,15},{8,0},{9,1},... | collective-permute-start | bytes 1544 | tf_op jit(solution)/shard_map/ppermute | solution.py:546
  20.9 1.2 %collective-permute-start.6 = (f32[2,128]{1,0:T(2,128)S(1)}, f32[2,128]{1,0:T(2,128)S(1)}, u32[]{:S(2)}, u32[]{:S(2)}) collective-permute-start(f32[2,128]{1,0:T(2,128)S(1)} %get-tuple-element.33), channel_id=1, source_target_pairs={{0,1},{1,0},{2,3},{3,2},{4,5},{5,4},{6,7},{7,6},{8,9},{9,8},{10,11... | collective-permute-start | bytes 3080 | tf_op jit(solution)/shard_map/ppermute | solution.py:546
  22.1 3.6 %collective-permute-start.7 = (f32[2,128]{1,0:T(2,128)S(1)}, f32[2,128]{1,0:T(2,128)S(1)}, u32[]{:S(2)}, u32[]{:S(2)}) collective-permute-start(f32[2,128]{1,0:T(2,128)S(1)} %add_select_fusion.2), channel_id=1, source_target_pairs={{0,2},{1,3},{2,0},{3,1},{4,6},{5,7},{6,4},{7,5},{8,10},{9,11},{10,... | collective-permute-start | bytes 3080 | tf_op jit(solution)/shard_map/ppermute | solution.py:546
  25.8 3.6 %collective-permute-start.8 = (f32[2,128]{1,0:T(2,128)S(1)}, f32[2,128]{1,0:T(2,128)S(1)}, u32[]{:S(2)}, u32[]{:S(2)}) collective-permute-start(f32[2,128]{1,0:T(2,128)S(1)} %add_select_fusion.1), channel_id=1, source_target_pairs={{0,4},{1,5},{2,6},{3,7},{4,0},{5,1},{6,2},{7,3},{8,12},{9,13},{10,... | collective-permute-start | bytes 3080 | tf_op jit(solution)/shard_map/ppermute | solution.py:546
  29.4 4.5 %collective-permute-start.9 = (f32[2,128]{1,0:T(2,128)S(1)}, f32[2,128]{1,0:T(2,128)S(1)}, u32[]{:S(2)}, u32[]{:S(2)}) collective-permute-start(f32[2,128]{1,0:T(2,128)S(1)} %add_select_fusion.fast), channel_id=1, source_target_pairs={{0,8},{1,9},{2,10},{3,11},{4,12},{5,13},{6,14},{7,15},{8,0},{9,1},... | collective-permute-start | bytes 3080 | tf_op jit(solution)/shard_map/ppermute | solution.py:546

commit v2 on v0

v2 whole, which is shorter than its diff:
```python
import functools

import jax
import jax.numpy as jnp
from jax import lax
from jax.experimental import pallas as pl
from jax.experimental.pallas import tpu as pltpu
from jax.sharding import PartitionSpec as P

COS_SLOPE = 0.8
SIN_SLOPE = 0.6
DEPTH_FLOOR = 0.05
SPEED_EPS = 0.01
COURANT = 0.2
DATA_WEIGHT = 100000.0

LANES = 128
TILE = 8
H, Q1, Q2, FA, FB, DM, DX, OB, WR = range(9)
KEPT = 8
SHARED = 9
UNROLL = 6


class Grid:
    def __init__(self, groups, wide):
        self.groups = groups
        self.tiles = wide // TILE
        self.lane = lax.broadcasted_iota(jnp.int32, (groups * TILE, LANES), 1)
        self.blank = jnp.zeros((TILE, LANES), jnp.float32)
        me = lax.axis_index("cross")
        self.ends = (me == 0, me == lax.axis_size("cross") - 1)

    def rows_next(self, v):
        turned = pltpu.roll(v, LANES - 1, 1)
        after = jnp.concatenate([turned[TILE:], self.blank], axis=0)
        return jnp.where(self.lane == LANES - 1, after, turned)

    def rows_prev(self, v):
        turned = pltpu.roll(v, 1, 1)
        before = jnp.concatenate([self.blank, turned[:-TILE]], axis=0)
        return jnp.where(self.lane == 0, before, turned)

    def both_rows(self, v):
        return self.rows_next(v), self.rows_prev(v)

    def get(self, ref, k, col):
        return jnp.concatenate([ref[k, g, pl.ds(col, TILE), :] for g in range(self.groups)], axis=0)

    def put(self, ref, k, col, value):
        for g in range(self.groups):
            ref[k, g, pl.ds(col, TILE), :] = value[g * TILE : (g + 1) * TILE]

    def spare_get(self, ref, k, col, off=0):
        return self.get(ref, k, col + TILE + off)

    def spare_put(self, ref, k, col, value):
        self.put(ref, k, col + TILE, value)

    def both_cols(self, ref, k, col):
        return self.spare_get(ref, k, col, 1), self.spare_get(ref, k, col, -1)

    def sweep(self, body, first=0, last=None, carry=None):
        last = self.tiles if last is None else last
        steps, rest = divmod(last - first, UNROLL)

        def visit(t, col, carry):
            return body(t, col) if carry is None else body(t, col, carry)

        def step(i, carry):
            for u in range(UNROLL):
                t = first + i * UNROLL + u
                carry = visit(t, pl.multiple_of(t * TILE, TILE), carry)
            return carry

        carry = lax.fori_loop(0, steps, step, carry)
        for t in range(last - rest, last):
            carry = visit(t, t * TILE, carry)
        return carry

    def sweep_own(self, body):
        self.sweep(body, 1, self.tiles - 1)

    def inside(self, t):
        return jnp.logical_not(((t == 0) & self.ends[0]) | ((t == self.tiles - 1) & self.ends[1]))


def speed_of(height, down, across):
    inv = 1.0 / jnp.maximum(height, DEPTH_FLOOR)
    vel_down = down * inv
    vel_across = across * inv
    return jnp.sqrt(vel_down * vel_down + vel_across * vel_across) + jnp.sqrt(COS_SLOPE * jnp.maximum(height, 0.0))


def velocities(height, down, across):
    inv = 1.0 / jnp.maximum(height, DEPTH_FLOOR)
    return inv, down * inv, across * inv


def friction(height, vel_down, vel_across, dry, turbulent):
    squared = vel_down * vel_down + vel_across * vel_across + SPEED_EPS
    inv_speed = lax.rsqrt(squared)
    return inv_speed, dry * height * inv_speed, turbulent * (squared * inv_speed)


def step_length(rows, shape):
    return COURANT / jnp.broadcast_to(jnp.max(rows[...], axis=0, keepdims=True), shape)


def prepare(*refs):
    sources = refs[:9]
    kept, weights, edge_a, edge_b, row, count_row, code, turned = refs[9:17]
    held, arrived = refs[17:26], refs[26]
    copies = [pltpu.make_async_copy(src, dst, arrived.at[i]) for i, (src, dst) in enumerate(zip(sources, held))]
    for i in (0, 6, 5, 7, 3, 4, 1, 2, 8):
        copies[i].start()
    state, log_mu, log_xi, dir_mu, dir_xi, wet, observed, terrain, class_weight = held
    rows, cols = log_mu.shape
    groups = rows // LANES
    own = pl.ds(TILE, cols)

    copies[0].wait()
    top = jnp.zeros((16, cols), jnp.float32)
    for i in range(0, rows, 16):
        top = jnp.maximum(top, speed_of(*(state[k, i : i + 16, :] for k in range(3))))
    row[...] = jnp.full(row.shape, jnp.max(top), jnp.float32)
    for g in range(groups):
        for k in range(3):
            kept[k, g, own, :] = state[k, pl.ds(g * LANES, LANES), :].T

    for i in (6, 5, 7):
        copies[i].wait()
    seen = jnp.zeros((16, cols), jnp.float32)
    for i in range(0, rows, 16):
        seen_here = observed[i : i + 16, :]
        code[i : i + 16, :] = (wet[i : i + 16, :] + 2 * seen_here + 4 * terrain[i : i + 16, :]).astype(jnp.float32)
        seen += seen_here.astype(jnp.float32)
    count_row[...] = jnp.full(count_row.shape, jnp.sum(seen), jnp.float32)

    for i in (3, 4, 1, 2, 8):
        copies[i].wait()
    for g in range(groups):
        at = pl.ds(g * LANES, LANES)
        turned[2, g] = code[at, :].T
        kept[DM, g, own, :] = dir_mu[at, :].T
        kept[DX, g, own, :] = dir_xi[at, :].T
        turned[0, g] = log_mu[at, :].T
        turned[1, g] = log_xi[at, :].T

    def derive(i, carry):
        for g, half in ((g, half) for g in range(groups) for half in range(2)):
            at = pl.ds(pl.multiple_of((2 * i + half) * TILE, TILE), TILE)
            to = pl.ds(pl.multiple_of((2 * i + half + 1) * TILE, TILE), TILE)
            bits = turned[2, g, at, :].astype(jnp.int32)
            wet_here = (bits & 1).astype(jnp.float32)
            kind = bits >> 2
            kept[FA, g, to, :] = wet_here * jnp.exp(turned[0, g, at, :]) * COS_SLOPE
            kept[FB, g, to, :] = wet_here * jnp.exp(-turned[1, g, at, :])
            kept[OB, g, to, :] = ((bits >> 1) & 1).astype(jnp.float32)
            weight = jnp.zeros((TILE, LANES), jnp.float32)
            for c in range(class_weight.shape[0]):
                weight = jnp.where(kind == c, class_weight[c], weight)
            weights[0, g, to, :] = weight
        return carry

    lax.fori_loop(0, cols // (2 * TILE), derive, 0)
    even = lax.rem(lax.axis_index("cross"), 2) == 0
    for k in range(SHARED):
        ref, j = (kept, k) if k < KEPT else (weights, 0)
        for g in range(groups):
            left = ref[j, g, TILE : 2 * TILE, :]
            right = ref[j, g, cols : cols + TILE, :]
            edge_a[k, g] = jnp.where(even, right, left)
            edge_b[k, g] = jnp.where(even, left, right)


def fill_halo(source, ref, j, k, edge_a, edge_b):
    even = lax.rem(lax.axis_index("cross"), 2) == 0
    wide = ref.shape[2]
    for g in range(ref.shape[1]):
        ref[j, g, TILE : wide - TILE, :] = source[j, g, TILE : wide - TILE, :]
        ref[j, g, :TILE, :] = jnp.where(even, edge_b[k, g], edge_a[k, g])
        ref[j, g, wide - TILE :, :] = jnp.where(even, edge_a[k, g], edge_b[k, g])


def open_step(kept_in, weights_in, edge_a, edge_b, kept, weights, xy, change, work):
    grid = Grid(kept.shape[1], kept.shape[2])
    for k in range(KEPT):
        fill_halo(kept_in, kept, k, k, edge_a, edge_b)
    fill_halo(weights_in, weights, 0, WR, edge_a, edge_b)

    def first(t, col):
        height, down, across = (grid.get(kept, k, col) for k in (H, Q1, Q2))
        _, u, v = velocities(height, down, across)
        _, dry, turb = friction(height, u, v, grid.get(kept, FA, col), grid.get(kept, FB, col))
        moved = dry * grid.get(kept, DM, col) - turb * grid.get(kept, DX, col)
        grid.put(change, 0, col, -u * moved)
        grid.put(change, 1, col, -v * moved)
        drag = dry + turb
        pressure = 0.5 * COS_SLOPE * height * height
        mixed = down * v
        for k, value in enumerate((height, down, across, mixed, across * v + pressure)):
            grid.spare_put(work, k, col, value)
        hn, hp = grid.both_rows(height)
        pn, pp = grid.both_rows(down)
        qn, qp = grid.both_rows(across)
        fn, fp = grid.both_rows(down * u + pressure)
        gn, gp = grid.both_rows(mixed)
        grid.put(xy, 0, col, 0.6 * height + 0.1 * (hn + hp))
        grid.put(xy, 1, col, 0.6 * down + 0.1 * (pn + pp))
        grid.put(xy, 2, col, 0.6 * across + 0.1 * (qn + qp))
        grid.put(xy, 3, col, -0.5 * (pn - pp))
        grid.put(xy, 4, col, SIN_SLOPE * height - drag * u - 0.5 * (fn - fp))
        grid.put(xy, 5, col, -drag * v - 0.5 * (gn - gp))

    grid.sweep(first)

    def second(t, col):
        hn, hp = grid.both_cols(work, 0, col)
        pn, pp = grid.both_cols(work, 1, col)
        qn, qp = grid.both_cols(work, 2, col)
        gn, gp = grid.both_cols(work, 3, col)
        fn, fp = grid.both_cols(work, 4, col)
        for k, (n, p) in enumerate(((hn, hp), (pn, pp), (qn, qp))):
            grid.put(xy, k, col, grid.get(xy, k, col) + 0.1 * (n + p))
        for k, (n, p) in enumerate(((qn, qp), (gn, gp), (fn, fp))):
            grid.put(xy, 3 + k, col, grid.get(xy, 3 + k, col) - 0.5 * (n - p))

    grid.sweep(second)


CU, CV, CZ, CW, CE, CB = range(6)
MU, MV, MZ, MW, ME, MB, MM, MH, MY = range(9)


def middle(top_rows, kept, xy, count_row, at_one, mid, row, work):
    grid = Grid(kept.shape[1], kept.shape[2])
    dt = step_length(top_rows, grid.lane.shape)
    half = 0.5 * dt

    def first(t, col):
        keep = grid.inside(t)
        height, down, across = (
            jnp.where(keep, grid.get(xy, k, col) + dt * grid.get(xy, 3 + k, col), 0.0) for k in range(3)
        )
        inv, u, v = velocities(height, down, across)
        turb_of = grid.get(kept, FB, col)
        inv_speed, dry, turb = friction(height, u, v, grid.get(kept, FA, col), turb_of)
        drag = dry + turb
        grid.put(at_one, CU, col, u)
        grid.put(at_one, CV, col, v)
        grid.put(at_one, CZ, col, (turb_of - dry * inv_speed) * inv_speed * inv)
        grid.put(at_one, CW, col, drag * inv)
        grid.put(at_one, CE, col, dry)
        grid.put(at_one, CB, col, turb)
        pressure = 0.5 * COS_SLOPE * height * height
        mixed = down * v
        for k, value in enumerate((height, down, across, mixed, across * v + pressure)):
            grid.spare_put(work, k, col, value)
        sources = (0.0, dt * (SIN_SLOPE * height - drag * u), -dt * drag * v)
        for k, (value, flux) in enumerate(((height, down), (down, down * u + pressure), (across, mixed))):
            tenth, moved = 0.1 * value, half * flux
            total = grid.get(kept, k, col) + 0.6 * value + sources[k]
            total += grid.rows_next(tenth - moved) + grid.rows_prev(tenth + moved)
            grid.put(mid, k, col, total)

    grid.sweep(first)

    def second(t, col, most):
        keep = grid.inside(t)
        found = []
        for k, (value, flux) in enumerate(((0, 2), (1, 3), (2, 4))):
            vn, vp = grid.both_cols(work, value, col)
            fn, fp = grid.both_cols(work, flux, col)
            total = grid.get(mid, k, col) + 0.1 * (vn + vp) - half * (fn - fp)
            found.append(jnp.where(keep, 0.5 * total, 0.0))
            grid.put(mid, k, col, found[k])
        own = (t > 0) & (t < grid.tiles - 1)
        return jnp.maximum(most, jnp.where(own, speed_of(*found), 0.0))

    fastest = grid.sweep(second, carry=jnp.zeros(grid.lane.shape, jnp.float32))
    lane = lax.broadcasted_iota(jnp.int32, row.shape, 1)
    count = jnp.broadcast_to(count_row[...], row.shape)
    row[...] = jnp.where(lane < LANES // 2, jnp.full(row.shape, jnp.max(fastest), jnp.float32), count)


def between(top_rows, kept, weights, change, at_one, smooth, tan, work, bent):
    grid = Grid(kept.shape[1], kept.shape[2])
    dt = step_length(top_rows, grid.lane.shape)
    half = 0.5 * dt

    def first(t, col):
        tp, tq = dt * grid.get(change, 0, col), dt * grid.get(change, 1, col)
        u, v = grid.get(at_one, CU, col), grid.get(at_one, CV, col)
        w = grid.get(at_one, CW, col)
        moved = grid.get(at_one, CE, col) * grid.get(kept, DM, col) - grid.get(at_one, CB, col) * grid.get(kept, DX, col)
        along = grid.get(at_one, CZ, col) * (u * tp + v * tq) + moved
        mixed = v * tp + u * tq
        for k, value in enumerate((tp, tq, mixed, 2.0 * v * tq)):
            grid.spare_put(work, k, col, value)
        for k, field in enumerate((DM, DX)):
            grid.spare_put(bent, k, col, grid.get(kept, field, col))
        moved = half * tp
        grid.put(tan, 0, col, grid.rows_prev(moved) - grid.rows_next(moved))
        sources = (-dt * (u * along + w * tp), -dt * (v * along + w * tq))
        for k, (value, flux) in enumerate(((tp, 2.0 * u * tp), (tq, mixed))):
            tenth, moved = 0.1 * value, half * flux
            total = 0.6 * value + sources[k]
            total += grid.rows_next(tenth - moved) + grid.rows_prev(tenth + moved)
            grid.put(tan, 1 + k, col, total)

    grid.sweep(first)

    def laplace(k, col):
        value = grid.spare_get(bent, k, col)
        rn, rp = grid.both_rows(value)
        cn, cp = grid.both_cols(bent, k, col)
        return 4.0 * value - rn - rp - cn - cp

    def second(t, col):
        keep = grid.inside(t)
        qn, qp = grid.both_cols(work, 1, col)
        pn, pp = grid.both_cols(work, 0, col)
        gn, gp = grid.both_cols(work, 2, col)
        fn, fp = grid.both_cols(work, 3, col)
        th = grid.get(tan, 0, col) - half * (qn - qp)
        tp = grid.get(tan, 1, col) + 0.1 * (pn + pp) - half * (gn - gp)
        tq = grid.get(tan, 2, col) + 0.1 * (qn + qp) - half * (fn - fp)
        for k, value in enumerate((th, tp, tq)):
            grid.put(tan, k, col, jnp.where(keep, 0.5 * value, 0.0))
        weight = grid.get(weights, 0, col)
        for k in range(2):
            grid.spare_put(bent, 2 + k, col, weight * laplace(k, col))

    grid.sweep(second)

    def third(t, col):
        for k in range(2):
            grid.put(smooth, k, col - TILE, laplace(2 + k, col))

    grid.sweep_own(third)


def finish(cells, top_rows, next_rows, kept, at_one, mid, tan, smooth, out_mu, out_xi, at_mid, end, work, total):
    grid = Grid(kept.shape[1], kept.shape[2])
    shape = grid.lane.shape
    dt0 = step_length(top_rows, shape)
    rows = next_rows[...]
    lane = lax.broadcasted_iota(jnp.int32, (1, LANES), 1)
    most = jnp.max(rows, axis=0, keepdims=True)
    added = jnp.sum(rows, axis=0, keepdims=True)
    dt1 = COURANT / jnp.broadcast_to(jnp.where(lane < LANES // 2, most, pltpu.roll(most, LANES // 2, 1)), shape)
    count = jnp.where(lane < LANES // 2, pltpu.roll(added, LANES // 2, 1), added)
    weight = jnp.broadcast_to((DATA_WEIGHT * cells) / count, shape)
    half1 = 0.5 * dt1
    half0 = 0.5 * dt0

    def open_end(t, col):
        th, tp, tq = (grid.get(tan, k, col) for k in range(3))
        height, down, across = (grid.get(mid, k, col) for k in range(3))
        inv, u, v = velocities(height, down, across)
        above = jnp.where(height > DEPTH_FLOOR, 1.0, jnp.where(height == DEPTH_FLOOR, 0.5, 0.0))
        turb_of = grid.get(kept, FB, col)
        dry_of = grid.get(kept, FA, col)
        inv_speed, dry, turb = friction(height, u, v, dry_of, turb_of)
        z = (turb_of - dry * inv_speed) * inv_speed * inv
        w = (dry + turb) * inv
        y = dry_of * inv_speed - above * (z * (u * u + v * v) + w)
        eight = COS_SLOPE * height
        for k, value in ((MU, u), (MV, v), (MZ, z), (MW, w), (ME, dry), (MB, turb), (MM, above), (MH, eight), (MY, y)):
            grid.put(at_mid, k, col, value)
        along = z * (u * tp + v * tq) + y * th
        along += dry * grid.get(kept, DM, col) - turb * grid.get(kept, DX, col)
        lift = above * th
        flux_down = 2.0 * u * tp + eight * th - u * u * lift
        mixed = v * tp + u * tq - u * v * lift
        for k, value in enumerate((th, tp, tq, mixed, 2.0 * v * tq + eight * th - v * v * lift)):
            grid.spare_put(work, k, col, value)
        tenths = (0.1 * th, 0.1 * tp, 0.1 * tq)
        moves = (half1 * tp, half1 * flux_down, half1 * mixed)
        sources = (0.0, dt1 * (SIN_SLOPE * th - u * along - w * tp), -dt1 * (v * along + w * tq))
        for k, value in enumerate((th, tp, tq)):
            total_k = 0.6 * value + sources[k]
            total_k += grid.rows_next(tenths[k] - moves[k]) + grid.rows_prev(tenths[k] + moves[k])
            grid.spare_put(end, k, col, total_k)

    grid.sweep(open_end)

    def close_end(t, col):
        keep = grid.inside(t)
        for k, (value, flux) in enumerate(((0, 2), (1, 3), (2, 4))):
            vn, vp = grid.both_cols(work, value, col)
            fn, fp = grid.both_cols(work, flux, col)
            found = grid.spare_get(end, k, col) + 0.1 * (vn + vp) - half1 * (fn - fp)
            grid.spare_put(end, k, col, jnp.where(keep, found, 0.0))

    grid.sweep(close_end)

    def seed_end(t, col):
        th, tp = grid.spare_get(end, 0, col), grid.spare_get(end, 1, col)
        tenth, moved = 0.1 * th, half1 * tp
        hn, hp = grid.both_cols(end, 0, col)
        qn, qp = grid.both_cols(end, 2, col)
        value = grid.get(tan, 0, col) + 0.6 * th + grid.rows_next(tenth - moved) + grid.rows_prev(tenth + moved)
        value += 0.1 * (hn + hp) - half1 * (qn - qp)
        grid.spare_put(work, 0, col, weight * grid.get(kept, OB, col) * (0.5 * value))

    grid.sweep(seed_end)

    def back_second(t, col):
        keep = grid.inside(t)
        seed = grid.spare_get(work, 0, col)
        rn, rp = grid.both_rows(seed)
        cn, cp = grid.both_cols(work, 0, col)
        grid.spare_put(work, 1, col, jnp.where(keep, 0.3 * seed + 0.05 * (rn + rp + cn + cp), 0.0))
        grid.spare_put(work, 2, col, jnp.where(keep, 0.5 * half1 * (rn - rp), 0.0))
        grid.spare_put(work, 3, col, jnp.where(keep, 0.5 * half1 * (cn - cp), 0.0))

    grid.sweep(back_second)

    def back_first(t, col):
        keep = grid.inside(t)
        g0, g1, g2 = (grid.spare_get(work, 1 + k, col) for k in range(3))
        r0n, r0p = grid.both_rows(g0)
        r1n, r1p = grid.both_rows(g1)
        r2n, r2p = grid.both_rows(g2)
        c0n, c0p = grid.both_cols(work, 1, col)
        c1n, c1p = grid.both_cols(work, 2, col)
        c2n, c2p = grid.both_cols(work, 3, col)
        u, v = grid.get(at_mid, MU, col), grid.get(at_mid, MV, col)
        z, w = grid.get(at_mid, MZ, col), grid.get(at_mid, MW, col)
        down = half1 * (r1n - r1p)
        cross = half1 * ((r2n - r2p) + (c1n - c1p))
        side = half1 * (c2n - c2p)
        h1, h2 = dt1 * g1, dt1 * g2
        along = u * h1 + v * h2
        grid.put(total, 0, col, -grid.get(at_mid, ME, col) * along)
        grid.put(total, 1, col, grid.get(at_mid, MB, col) * along)
        pull = z * along
        part_u = u * down + v * cross
        part_v = v * side
        m0 = 0.5 * grid.spare_get(work, 0, col) + 0.6 * g0 + 0.1 * (r0n + r0p + c0n + c0p)
        m0 += SIN_SLOPE * h1 - grid.get(at_mid, MY, col) * along + grid.get(at_mid, MH, col) * (down + side)
        m0 -= grid.get(at_mid, MM, col) * (u * part_u + v * part_v)
        m1 = 0.6 * g1 + 0.1 * (r1n + r1p + c1n + c1p)
        m1 += half1 * (r0n - r0p) + u * (down - pull) + part_u - w * h1
        m2 = 0.6 * g2 + 0.1 * (r2n + r2p + c2n + c2p)
        m2 += half1 * (c0n - c0p) + u * cross + 2.0 * part_v - v * pull - w * h2
        for k, value in enumerate((m0, m1, m2)):
            grid.spare_put(work, 4 + k, col, jnp.where(keep, value, 0.0))

    grid.sweep(back_first)

    def early(t, col):
        m0, m1, m2 = (grid.spare_get(work, 4 + k, col) for k in range(3))
        r0n, r0p = grid.both_rows(m0)
        r1n, r1p = grid.both_rows(m1)
        r2n, r2p = grid.both_rows(m2)
        c0n, c0p = grid.both_cols(work, 4, col)
        c1n, c1p = grid.both_cols(work, 5, col)
        c2n, c2p = grid.both_cols(work, 6, col)
        u, v = grid.get(at_one, CU, col), grid.get(at_one, CV, col)
        z, w = grid.get(at_one, CZ, col), grid.get(at_one, CW, col)
        quarter = 0.5 * half0
        down = quarter * (r1n - r1p)
        cross = quarter * ((r2n - r2p) + (c1n - c1p))
        side = quarter * (c2n - c2p)
        p1, p2 = half0 * m1, half0 * m2
        along = u * p1 + v * p2
        pull = z * along
        f1 = 0.3 * m1 + 0.05 * (r1n + r1p + c1n + c1p)
        f1 += quarter * (r0n - r0p) + 2.0 * u * down + v * cross - u * pull - w * p1
        f2 = 0.3 * m2 + 0.05 * (r2n + r2p + c2n + c2p)
        f2 += quarter * (c0n - c0p) + u * cross + 2.0 * v * side - v * pull - w * p2
        height, down, across = (grid.get(kept, k, col) for k in (H, Q1, Q2))
        _, u, v = velocities(height, down, across)
        _, dry, turb = friction(height, u, v, grid.get(kept, FA, col), grid.get(kept, FB, col))
        start = dt0 * (u * f1 + v * f2)
        mu = grid.get(total, 0, col) + grid.get(smooth, 0, col - TILE)
        xi = grid.get(total, 1, col) + grid.get(smooth, 1, col - TILE)
        grid.put(total, 0, col, mu - grid.get(at_one, CE, col) * along - dry * start)
        grid.put(total, 1, col, xi + grid.get(at_one, CB, col) * along + turb * start)

    grid.sweep_own(early)

    cols = out_mu.shape[1]
    for g in range(grid.groups):
        at = pl.ds(g * LANES, LANES)
        out_mu[at, :] = total[0, g, TILE : TILE + cols, :].T
        out_xi[at, :] = total[1, g, TILE : TILE + cols, :].T


VMEM = pl.BlockSpec(memory_space=pltpu.VMEM)
ANY = pl.BlockSpec(memory_space=pltpu.HBM)


def call(body, name, operands, outs, scratch, flops, spaces=None, aliases=None):
    outs = [jax.ShapeDtypeStruct(shape, jnp.float32) for shape in outs]
    moved = 4 * sum(x.size for x in operands) + 4 * sum(x.size for x in outs)
    return pl.pallas_call(
        body,
        name=name,
        out_shape=outs,
        in_specs=spaces or [VMEM] * len(operands),
        out_specs=[VMEM] * len(outs),
        scratch_shapes=[pltpu.VMEM(x, jnp.float32) if isinstance(x, tuple) else x for x in scratch],
        input_output_aliases=aliases or {},
        compiler_params=pltpu.CompilerParams(vmem_limit_bytes=24 * 1024 * 1024),
        cost_estimate=pl.CostEstimate(flops=flops, bytes_accessed=moved, transcendentals=0),
    )(*operands)


def swap_edges(edge_a, edge_b, count):
    pairs_a = [(i, i ^ 1) for i in range(count)]
    pairs_b = [(i, i - 1 if i % 2 == 0 else i + 1) for i in range(1, count - 1)]
    return lax.ppermute(edge_a, "cross", pairs_a), lax.ppermute(edge_b, "cross", pairs_b)


def share(row):
    return lax.all_to_all(row, "cross", 0, 0, tiled=True)


def local(state, log_mu, log_xi, dir_mu, dir_xi, wet, observed, terrain, class_weight):
    rows, cols = log_mu.shape
    groups = rows // LANES
    count = lax.axis_size("cross")
    own = (groups, cols, LANES)
    wide = (groups, cols + 2 * TILE, LANES)
    spare = (groups, cols + 4 * TILE, LANES)
    edge = (SHARED, groups, TILE, LANES)
    work = rows * cols

    inputs = (state, log_mu, log_xi, dir_mu, dir_xi, wet, observed, terrain, class_weight)
    inputs = tuple(pltpu.with_memory_space_constraint(x, pltpu.HBM) for x in inputs)
    kept, weights, edge_a, edge_b, row, count_row = call(
        prepare,
        "prepare",
        inputs,
        [(KEPT,) + wide, (1,) + wide, edge, edge, (count, LANES), (1, LANES)],
        [(rows, cols), (3,) + own]
        + [pltpu.VMEM(x.shape, x.dtype) for x in inputs[:-1]]
        + [pltpu.SMEM(class_weight.shape, jnp.float32), pltpu.SemaphoreType.DMA((len(inputs),))],
        100 * work,
        spaces=[ANY] * len(inputs),
    )
    edge_a, edge_b = swap_edges(edge_a, edge_b, count)
    top_rows = share(row)
    kept, weights, xy, change = call(
        open_step,
        "open_step",
        (kept, weights, edge_a, edge_b),
        [(KEPT,) + wide, (1,) + wide, (6,) + wide, (3,) + wide],
        [(5,) + spare],
        100 * work,
        aliases={0: 0, 1: 1},
    )
    at_one, mid, next_row = call(
        middle,
        "middle",
        (top_rows, kept, xy, count_row),
        [(6,) + wide, (3,) + wide, (count, LANES)],
        [(5,) + spare],
        120 * work,
    )
    next_rows = share(next_row)
    smooth, tan = call(
        between,
        "between",
        (top_rows, kept, weights, change, at_one),
        [(2,) + own, (3,) + wide],
        [(4,) + spare, (4,) + spare],
        100 * work,
        aliases={3: 1},
    )
    return call(
        functools.partial(finish, float(rows * cols * count)),
        "finish",
        (top_rows, next_rows, kept, at_one, mid, tan, smooth),
        [(rows, cols), (rows, cols)],
        [(9,) + wide, (3,) + spare, (7,) + spare, (2,) + wide],
        300 * work,
    )


def solution(mesh):
    return jax.shard_map(
        local,
        mesh=mesh,
        in_specs=(
            P(None, "grp", "cross"),
            P("grp", "cross"),
            P("grp", "cross"),
            P("grp", "cross"),
            P("grp", "cross"),
            P("grp", "cross"),
            P("grp", "cross"),
            P("grp", "cross"),
            P(),
        ),
        out_specs=(P("grp", "cross"), P("grp", "cross")),
        check_vma=False,
    )
```

time: 53.8 us -> 35 us (0.65)
  local copies, waits for them, and re-layouts: 22.7 us -> 0.76 us
  waiting for transfers between devices: 2.62 us -> 9.34 us
  Pallas kernels: 13.7 us -> 10.5 us
    unnamed x44 -> x4, local copies, waits for them, and re-layouts: 22.7 us -> 0.76 us
    all_to_all x2, waiting for transfers between devices: 2.62 us -> 9.34 us  [share(): return lax.all_to_all(row, 'cross', 0, 0, tiled=True)]
    pallas_call x5, Pallas kernels: 13.7 us -> 10.5 us  [call(): pl.pallas_call(body, name=name, out_shape=outs, in_specs=spaces or [VMEM]...]
  transfers between devices with their start and end apart: 4 -> 4, of which waited for: 1 -> 2; matrix products, arithmetic and copies ran while one was open for 0% -> 0% of each run, Pallas kernels for 10% -> 9%
where the time goes in v2:
time: 35 us; the launch traced here: 34.8 us
  starting transfers between devices  13.5 us (39%)
  Pallas kernels  10.5 us (30%)
  waiting for transfers between devices  9.34 us (27%)
  local copies, waits for them, and re-layouts  0.76 us (2%)
  between operations  0.71 us (2%)
    all_to_all x2, starting transfers between devices, share(): return lax.all_to_all(row, 'cross', 0, 0, tiled=True)  12.3 us
    pallas_call x5, Pallas kernels, call(): pl.pallas_call(body, name=name, out_shape=outs, in_specs=spaces or [VMEM]...  10.5 us
    all_to_all x2, waiting for transfers between devices, share(): return lax.all_to_all(row, 'cross', 0, 0, tiled=True)  9.34 us
    unnamed x4, local copies, waits for them, and re-layouts  0.76 us
  transfers between devices with their start and end apart: 4, of which 2 were waited for; matrix products, arithmetic and copies ran while one was open for 0% of the time, Pallas kernels for 9%

profile of v2, /device:TPU:0, one launch (start us, length us, event | category | flops | bytes accessed | tf_op | source)
XLA Modules:
  0.0 34.8 jit_solution(13784085851431637790)
XLA Ops:
  0.6 2.6 %prepare.1 = (f32[8,2,144,128]{3,2,1,0:T(8,128)S(1)}, f32[1,2,144,128]{3,2,1,0:T(8,128)S(1)}, f32[9,2,8,128]{3,2,1,0:T(8,128)S(1)}, f32[9,2,8,128]{3,2,1,0:T(8,1...) custom-call(f32[3,256,128]{2,1,0:T(8,128)} %refs_0_.1, f32[256,128]{1,0:T(8,128)} %refs_1_.1, f32[256,128]{1,0:T(8,128)} %refs_2_.1, ...), custom_call_target="tpu_custom_call" | custom-call | flops 3276800 | bytes 2794016 | tf_op jit(solution)/shard_map/prepare/pallas_call | solution.py:500
  3.2 0.5 %collective-permute-start = (f32[9,2,8,128]{3,2,1,0:T(8,128)S(1)}, f32[9,2,8,128]{3,2,1,0:T(8,128)S(1)}, u32[]{:S(2)}, u32[]{:S(2)}) collective-permute-start(f32[9,2,8,128]{3,2,1,0:T(8,128)S(1)} %get-tuple-element.20), channel_id=1, source_target_pairs={{0,1},{1,0},{2,3},{3,2},{4,5},{5,4},{6,7},{7,6},{8,9},{9,8},{10,11... | collective-permute-start | bytes 221192 | tf_op jit(solution)/shard_map/ppermute | solution.py:516
  3.7 0.7 %collective-permute-start.1 = (f32[9,2,8,128]{3,2,1,0:T(8,128)S(1)}, f32[9,2,8,128]{3,2,1,0:T(8,128)S(1)}, u32[]{:S(2)}, u32[]{:S(2)}) collective-permute-start(f32[9,2,8,128]{3,2,1,0:T(8,128)S(1)} %get-tuple-element.21), channel_id=1, source_target_pairs={{1,2},{2,1},{3,4},{4,3},{5,6},{6,5},{7,8},{8,7},{9,10},{10,9},{11,... | collective-permute-start | bytes 221192 | tf_op jit(solution)/shard_map/ppermute | solution.py:516
  4.4 8.8 %all-to-all-start = ((f32[16,1,128]{2,1,0:T(1,128)}), f32[16,1,128]{2,1,0:T(1,128)S(1)}, u32[]{:S(2)}, u32[]{:S(2)}) async-start(f32[16,1,128]{2,1,0:T(1,128)} %bitcast.1), calls=%async_computation | async-start | bytes 16384 | tf_op jit(solution)/shard_map/all_to_all | solution.py:520
  13.2 0.0 collective-permute-done.edge_a
  13.2 0.0 collective-permute-done.1.edge_b
  13.2 0.9 %open_step.1 = (f32[8,2,144,128]{3,2,1,0:T(8,128)S(1)}, f32[1,2,144,128]{3,2,1,0:T(8,128)S(1)}, f32[6,2,144,128]{3,2,1,0:T(8,128)S(1)}, f32[3,2,144,128]{3,2,1,0:T(8,128)S(1)}) custom-call(f32[8,2,144,128]{3,2,1,0:T(8,128)S(1)} %get-tuple-element.18.kept_in, ...), custom_call_target="tpu_custom_call", output_to_operand_aliasing={{0}: (0, {}), {1}: (1, {})} | custom-call | flops 3276800 | bytes 4128768 | tf_op jit(solution)/shard_map/open_step/pallas_call | solution.py:500
  14.1 5.4 %all-to-all-done = f32[16,1,128]{2,1,0:T(1,128)S(1)} async-done(((f32[16,1,128]{2,1,0:T(1,128)}), f32[16,1,128]{2,1,0:T(1,128)S(1)}, u32[]{:S(2)}, u32[]{:S(2)}) %all-to-all-start) | async-done | bytes 8224 | tf_op jit(solution)/shard_map/all_to_all | solution.py:520
  19.5 1.5 %middle.1 = (f32[6,2,144,128]{3,2,1,0:T(8,128)S(1)}, f32[3,2,144,128]{3,2,1,0:T(8,128)S(1)}, f32[16,128]{1,0:T(8,128)}) custom-call(f32[16,128]{1,0:T(8,128)S(1)} %bitcast.8, f32[8,2,144,128]{3,2,1,0:T(8,128)S(1)} %get-tuple-element.22.kept, f32[6,2,144,128]{3,2,1,0:T(8,128)S(1)} %get-tuple-element.23.xy, f32[1,128]{1,0:T(1,128)S(1)} %get-tuple-element.24.count_row), custom_call_target="tpu_custom_call" | custom-call | flops 3932160 | bytes 3408384 | tf_op jit(solution)/shard_map/middle/pallas_call | solution.py:500
  21.0 0.0 copy-start
  21.0 0.8 %copy-done = f32[3,2,144,128]{3,2,1,0:T(8,128)} copy-done((f32[3,2,144,128]{3,2,1,0:T(8,128)}, f32[3,2,144,128]{3,2,1,0:T(8,128)S(1)}, u32[]{:S(2)}) %copy-start) | copy-done | bytes 442392
  21.8 3.5 %all-to-all-start.1 = ((f32[16,1,128]{2,1,0:T(1,128)}), f32[16,1,128]{2,1,0:T(1,128)S(1)}, u32[]{:S(2)}, u32[]{:S(2)}) async-start(f32[16,1,128]{2,1,0:T(1,128)} %bitcast.4), calls=%async_computation.1 | async-start | bytes 16384 | tf_op jit(solution)/shard_map/all_to_all | solution.py:520
  25.3 0.0 copy-start.1
  25.3 2.3 %between.1 = (f32[2,2,128,128]{3,2,1,0:T(8,128)S(1)}, f32[3,2,144,128]{3,2,1,0:T(8,128)S(1)}) custom-call(f32[16,128]{1,0:T(8,128)S(1)} %bitcast.9, f32[8,2,144,128]{3,2,1,0:T(8,128)S(1)} %get-tuple-element.22.kept, f32[1,2,144,128]{3,2,1,0:T(8,128)S(1)} %get-tuple-element.28.weights, ...), custom_call_target="tpu_custom_call", output_to_operand_aliasing={{1}: (3, {})} | custom-call | flops 3276800 | bytes 3366912 | tf_op jit(solution)/shard_map/between/pallas_call | solution.py:500
  27.6 4.0 %all-to-all-done.1 = f32[16,1,128]{2,1,0:T(1,128)S(1)} async-done(((f32[16,1,128]{2,1,0:T(1,128)}), f32[16,1,128]{2,1,0:T(1,128)S(1)}, u32[]{:S(2)}, u32[]{:S(2)}) %all-to-all-start.1) | async-done | bytes 8224 | tf_op jit(solution)/shard_map/all_to_all | solution.py:520
  31.6 0.0 copy-done.1
  31.6 3.2 %finish.1 = (f32[256,128]{1,0:T(8,128)}, f32[256,128]{1,0:T(8,128)}) custom-call(f32[16,128]{1,0:T(8,128)S(1)} %bitcast.10, f32[16,128]{1,0:T(8,128)S(1)} %bitcast.11, f32[8,2,144,128]{3,2,1,0:T(8,128)S(1)} %get-tuple-element.22.kept, f32[6,2,144,128]{3,2,1,0:T(8,128)S(1)} %get-tuple-element.26.at_one, f32[3,2,144,128]{3,2,1,0:T(8,128)S(1)} %copy-done.1, ...), custom_call_target="tpu_custom_call" | custom-call | flops 9830400 | bytes 3489792 | tf_op jit(solution)/shard_map/finish/pallas_call | solution.py:500
Async XLA Ops:
  3.2 10.0 %collective-permute-start = (f32[9,2,8,128]{3,2,1,0:T(8,128)S(1)}, f32[9,2,8,128]{3,2,1,0:T(8,128)S(1)}, u32[]{:S(2)}, u32[]{:S(2)}) collective-permute-start(f32[9,2,8,128]{3,2,1,0:T(8,128)S(1)} %get-tuple-element.20), channel_id=1, source_target_pairs={{0,1},{1,0},{2,3},{3,2},{4,5},{5,4},{6,7},{7,6},{8,9},{9,8},{10,11... | collective-permute-start | bytes 221192 | tf_op jit(solution)/shard_map/ppermute | solution.py:516
  3.7 9.5 %collective-permute-start.1 = (f32[9,2,8,128]{3,2,1,0:T(8,128)S(1)}, f32[9,2,8,128]{3,2,1,0:T(8,128)S(1)}, u32[]{:S(2)}, u32[]{:S(2)}) collective-permute-start(f32[9,2,8,128]{3,2,1,0:T(8,128)S(1)} %get-tuple-element.21), channel_id=1, source_target_pairs={{1,2},{2,1},{3,4},{4,3},{5,6},{6,5},{7,8},{8,7},{9,10},{10,9},{11,... | collective-permute-start | bytes 221192 | tf_op jit(solution)/shard_map/ppermute | solution.py:516
  4.4 15.1 %all-to-all-start = ((f32[16,1,128]{2,1,0:T(1,128)}), f32[16,1,128]{2,1,0:T(1,128)S(1)}, u32[]{:S(2)}, u32[]{:S(2)}) async-start(f32[16,1,128]{2,1,0:T(1,128)} %bitcast.1), calls=%async_computation | async-start | bytes 16384 | tf_op jit(solution)/shard_map/all_to_all | solution.py:520
  21.0 0.8 %copy-start = (f32[3,2,144,128]{3,2,1,0:T(8,128)}, f32[3,2,144,128]{3,2,1,0:T(8,128)S(1)}, u32[]{:S(2)}) copy-start(f32[3,2,144,128]{3,2,1,0:T(8,128)S(1)} %get-tuple-element.27.mid) | copy-start | bytes 1327108
  21.8 9.8 %all-to-all-start.1 = ((f32[16,1,128]{2,1,0:T(1,128)}), f32[16,1,128]{2,1,0:T(1,128)S(1)}, u32[]{:S(2)}, u32[]{:S(2)}) async-start(f32[16,1,128]{2,1,0:T(1,128)} %bitcast.4), calls=%async_computation.1 | async-start | bytes 16384 | tf_op jit(solution)/shard_map/all_to_all | solution.py:520
  25.3 6.3 %copy-start.1 = (f32[3,2,144,128]{3,2,1,0:T(8,128)S(1)}, f32[3,2,144,128]{3,2,1,0:T(8,128)}, u32[]{:S(2)}) copy-start(f32[3,2,144,128]{3,2,1,0:T(8,128)} %copy-done) | copy-start | bytes 1327108

commit v3 on v2

--- a/solution.py
+++ b/solution.py
@@ -516,8 +516,15 @@
     return lax.ppermute(edge_a, "cross", pairs_a), lax.ppermute(edge_b, "cross", pairs_b)
 
 
-def share(row):
-    return lax.all_to_all(row, "cross", 0, 0, tiled=True)
+def share(row, combine):
+    count = lax.axis_size("cross")
+    row = combine(row, lax.ppermute(row, "cross", [(i, i ^ 1) for i in range(count)]))
+    parity = [list(range(first, count, 2)) for first in (0, 1)]
+    return lax.all_to_all(row, "cross", 0, 0, axis_index_groups=parity, tiled=True)
+
+
+def max_and_sum(a, b):
+    return jnp.where(lax.broadcasted_iota(jnp.int32, a.shape, 1) < LANES // 2, jnp.maximum(a, b), a + b)
 
 
 def local(state, log_mu, log_xi, dir_mu, dir_xi, wet, observed, terrain, class_weight):
@@ -536,7 +543,7 @@
         prepare,
         "prepare",
         inputs,
-        [(KEPT,) + wide, (1,) + wide, edge, edge, (count, LANES), (1, LANES)],
+        [(KEPT,) + wide, (1,) + wide, edge, edge, (count // 2, LANES), (1, LANES)],
         [(rows, cols), (3,) + own]
         + [pltpu.VMEM(x.shape, x.dtype) for x in inputs[:-1]]
         + [pltpu.SMEM(class_weight.shape, jnp.float32), pltpu.SemaphoreType.DMA((len(inputs),))],
@@ -544,7 +551,7 @@
         spaces=[ANY] * len(inputs),
     )
     edge_a, edge_b = swap_edges(edge_a, edge_b, count)
-    top_rows = share(row)
+    top_rows = share(row, jnp.maximum)
     kept, weights, xy, change = call(
         open_step,
         "open_step",
@@ -558,11 +565,11 @@
         middle,
         "middle",
         (top_rows, kept, xy, count_row),
-        [(6,) + wide, (3,) + wide, (count, LANES)],
+        [(6,) + wide, (3,) + wide, (count // 2, LANES)],
         [(5,) + spare],
         120 * work,
     )
-    next_rows = share(next_row)
+    next_rows = share(next_row, max_and_sum)
     smooth, tan = call(
         between,
         "between",

time: 35 us -> 37.3 us (1.066)
  waiting for transfers between devices: 9.34 us -> 11.4 us
  other arithmetic: 0 us -> 1.2 us
  Pallas kernels: 10.5 us -> 9.38 us
    ppermute x0 -> x2, starting transfers between devices: none -> 3.97 us  [share(): lax.ppermute(row, 'cross', [(i, i ^ 1) for i in range(count)])]
    all_to_all x2, starting transfers between devices: 12.3 us -> 8.45 us  [share(): lax.all_to_all(row, 'cross', 0, 0, axis_index_groups=parity, tiled=True)]
    ppermute x0 -> x2, waiting for transfers between devices: none -> 1.98 us  [share(): lax.ppermute(row, 'cross', [(i, i ^ 1) for i in range(count)])]
    pallas_call x5, Pallas kernels: 10.5 us -> 9.38 us  [call(): pl.pallas_call(body, name=name, out_shape=outs, in_specs=spaces or [VMEM]...]
    select_n x0 -> x1, other arithmetic: none -> 0.6 us  [max_and_sum(): jnp.where(lax.broadcasted_iota(jnp.int32, a.shape, 1) < LANES // 2, jnp.m...]
    max x0 -> x1, other arithmetic: none -> 0.59 us  [share(): combine(row, lax.ppermute(row, 'cross', [(i, i ^ 1) for i in range(count)]))]
  transfers between devices with their start and end apart: 4 -> 6, of which waited for: 2 -> 4; matrix products, arithmetic and copies ran while one was open for 0% -> 2% of each run, Pallas kernels for 9% -> 9%
where the time goes in v3:
time: 37.3 us; the launch traced here: 37.1 us
  starting transfers between devices  13.6 us (36%)
  waiting for transfers between devices  11.4 us (31%)
  Pallas kernels  9.38 us (25%)
  other arithmetic  1.2 us (3%)
  local copies, waits for them, and re-layouts  0.77 us (2%)
  between operations  0.71 us (2%)
    all_to_all x2, waiting for transfers between devices, share(): lax.all_to_all(row, 'cross', 0, 0, axis_index_groups=parity, tiled=True)  9.44 us
    pallas_call x5, Pallas kernels, call(): pl.pallas_call(body, name=name, out_shape=outs, in_specs=spaces or [VMEM]...  9.38 us
    all_to_all x2, starting transfers between devices, share(): lax.all_to_all(row, 'cross', 0, 0, axis_index_groups=parity, tiled=True)  8.45 us
    ppermute x2, starting transfers between devices, share(): lax.ppermute(row, 'cross', [(i, i ^ 1) for i in range(count)])  3.97 us
    ppermute x2, waiting for transfers between devices, share(): lax.ppermute(row, 'cross', [(i, i ^ 1) for i in range(count)])  1.98 us
    unnamed x4, local copies, waits for them, and re-layouts  0.77 us
  transfers between devices with their start and end apart: 6, of which 4 were waited for; matrix products, arithmetic and copies ran while one was open for 2% of the time, Pallas kernels for 9%

profile of v3, /device:TPU:0, one launch (start us, length us, event | category | flops | bytes accessed | tf_op | source)
XLA Modules:
  0.0 37.1 jit_solution(14944180714730380775)
XLA Ops:
  0.6 2.0 %prepare.1 = (f32[8,2,144,128]{3,2,1,0:T(8,128)S(1)}, f32[1,2,144,128]{3,2,1,0:T(8,128)S(1)}, f32[9,2,8,128]{3,2,1,0:T(8,128)S(1)}, f32[9,2,8,128]{3,2,1,0:T(8,1...) custom-call(f32[3,256,128]{2,1,0:T(8,128)} %refs_0_.1, f32[256,128]{1,0:T(8,128)} %refs_1_.1, f32[256,128]{1,0:T(8,128)} %refs_2_.1, ...), custom_call_target="tpu_custom_call" | custom-call | flops 3276800 | bytes 2789920 | tf_op jit(solution)/shard_map/prepare/pallas_call | solution.py:500
  2.6 0.5 %collective-permute-start.1 = (f32[9,2,8,128]{3,2,1,0:T(8,128)S(1)}, f32[9,2,8,128]{3,2,1,0:T(8,128)S(1)}, u32[]{:S(2)}, u32[]{:S(2)}) collective-permute-start(f32[9,2,8,128]{3,2,1,0:T(8,128)S(1)} %get-tuple-element.20), channel_id=1, source_target_pairs={{0,1},{1,0},{2,3},{3,2},{4,5},{5,4},{6,7},{7,6},{8,9},{9,8},{10,11... | collective-permute-start | bytes 221192 | tf_op jit(solution)/shard_map/ppermute | solution.py:516
  3.2 0.7 %collective-permute-start.2 = (f32[9,2,8,128]{3,2,1,0:T(8,128)S(1)}, f32[9,2,8,128]{3,2,1,0:T(8,128)S(1)}, u32[]{:S(2)}, u32[]{:S(2)}) collective-permute-start(f32[9,2,8,128]{3,2,1,0:T(8,128)S(1)} %get-tuple-element.21), channel_id=1, source_target_pairs={{1,2},{2,1},{3,4},{4,3},{5,6},{6,5},{7,8},{8,7},{9,10},{10,9},{11,... | collective-permute-start | bytes 221192 | tf_op jit(solution)/shard_map/ppermute | solution.py:516
  3.8 4.0 %collective-permute-start = (f32[8,128]{1,0:T(8,128)S(1)}, f32[8,128]{1,0:T(8,128)S(1)}, u32[]{:S(2)}, u32[]{:S(2)}) collective-permute-start(f32[8,128]{1,0:T(8,128)S(1)} %get-tuple-element.17), channel_id=1, source_target_pairs={{0,1},{1,0},{2,3},{3,2},{4,5},{5,4},{6,7},{7,6},{8,9},{9,8},{10,11... | collective-permute-start | bytes 12296 | tf_op jit(solution)/shard_map/ppermute | solution.py:521
  7.8 0.8 %collective-permute-done = f32[8,128]{1,0:T(8,128)S(1)} collective-permute-done((f32[8,128]{1,0:T(8,128)S(1)}, f32[8,128]{1,0:T(8,128)S(1)}, u32[]{:S(2)}, u32[]{:S(2)}) %collective-permute-start) | collective-permute-done | bytes 4128 | tf_op jit(solution)/shard_map/ppermute | solution.py:521
  8.6 0.6 %max.6 = f32[8,128]{1,0:T(8,128)} maximum(f32[8,128]{1,0:T(8,128)S(1)} %get-tuple-element.17, f32[8,128]{1,0:T(8,128)S(1)} %collective-permute-done) | non-fusion elementwise | flops 1024 | bytes 12288 | tf_op jit(solution)/shard_map/max | solution.py:521
  9.2 5.1 %all-to-all-start = ((f32[8,1,128]{2,1,0:T(1,128)}), f32[8,1,128]{2,1,0:T(1,128)S(1)}, u32[]{:S(2)}, u32[]{:S(2)}) async-start(f32[8,1,128]{2,1,0:T(1,128)} %bitcast.1), calls=%async_computation | async-start | bytes 8192 | tf_op jit(solution)/shard_map/all_to_all | solution.py:523
  14.3 0.0 collective-permute-done.1.edge_a
  14.3 0.0 collective-permute-done.2.edge_b
  14.4 0.9 %open_step.1 = (f32[8,2,144,128]{3,2,1,0:T(8,128)S(1)}, f32[1,2,144,128]{3,2,1,0:T(8,128)S(1)}, f32[6,2,144,128]{3,2,1,0:T(8,128)S(1)}, f32[3,2,144,128]{3,2,1,0:T(8,128)S(1)}) custom-call(f32[8,2,144,128]{3,2,1,0:T(8,128)S(1)} %get-tuple-element.18.kept_in, ...), custom_call_target="tpu_custom_call", output_to_operand_aliasing={{0}: (0, {}), {1}: (1, {})} | custom-call | flops 3276800 | bytes 4128768 | tf_op jit(solution)/shard_map/open_step/pallas_call | solution.py:500
  15.3 5.4 %all-to-all-done = f32[8,1,128]{2,1,0:T(1,128)S(1)} async-done(((f32[8,1,128]{2,1,0:T(1,128)}), f32[8,1,128]{2,1,0:T(1,128)S(1)}, u32[]{:S(2)}, u32[]{:S(2)}) %all-to-all-start) | async-done | bytes 4128 | tf_op jit(solution)/shard_map/all_to_all | solution.py:523
  20.7 0.9 %middle.1 = (f32[6,2,144,128]{3,2,1,0:T(8,128)S(1)}, f32[3,2,144,128]{3,2,1,0:T(8,128)S(1)}, f32[8,128]{1,0:T(8,128)S(1)}) custom-call(f32[8,128]{1,0:T(8,128)S(1)} %bitcast.8, f32[8,2,144,128]{3,2,1,0:T(8,128)S(1)} %get-tuple-element.22.kept, f32[6,2,144,128]{3,2,1,0:T(8,128)S(1)} %get-tuple-element.23.xy, f32[1,128]{1,0:T(1,128)S(1)} %get-tuple-element.24.count_row), custom_call_target="tpu_custom_call" | custom-call | flops 3932160 | bytes 3400192 | tf_op jit(solution)/shard_map/middle/pallas_call | solution.py:500
  21.6 0.0 copy-start
  21.6 0.8 %copy-done = f32[3,2,144,128]{3,2,1,0:T(8,128)} copy-done((f32[3,2,144,128]{3,2,1,0:T(8,128)}, f32[3,2,144,128]{3,2,1,0:T(8,128)S(1)}, u32[]{:S(2)}) %copy-start) | copy-done | bytes 442392
  22.4 0.0 collective-permute-start.3
  22.4 1.2 %collective-permute-done.3 = f32[8,128]{1,0:T(8,128)S(1)} collective-permute-done((f32[8,128]{1,0:T(8,128)S(1)}, f32[8,128]{1,0:T(8,128)S(1)}, u32[]{:S(2)}, u32[]{:S(2)}) %collective-permute-start.3) | collective-permute-done | bytes 4128 | tf_op jit(solution)/shard_map/ppermute | solution.py:521
  23.6 0.6 %add_select_fusion = f32[8,128]{1,0:T(8,128)} fusion(f32[8,128]{1,0:T(8,128)S(1)} %get-tuple-element.25, f32[8,128]{1,0:T(8,128)S(1)} %collective-permute-done.3, pred[128]{0:T(512)(128)(4,1)S(1)} %iota_compare_fusion), kind=kLoop, calls=%fused_computation | loop fusion | flops 3072 | bytes 12416 | tf_op jit(solution)/shard_map/jit(_where)/select_n | solution.py:527
  24.2 3.3 %all-to-all-start.1 = ((f32[8,1,128]{2,1,0:T(1,128)}), f32[8,1,128]{2,1,0:T(1,128)S(1)}, u32[]{:S(2)}, u32[]{:S(2)}) async-start(f32[8,1,128]{2,1,0:T(1,128)} %bitcast.4), calls=%async_computation.1 | async-start | bytes 8192 | tf_op jit(solution)/shard_map/all_to_all | solution.py:523
  27.5 0.0 copy-start.1
  27.5 2.3 %between.1 = (f32[2,2,128,128]{3,2,1,0:T(8,128)S(1)}, f32[3,2,144,128]{3,2,1,0:T(8,128)S(1)}) custom-call(f32[8,128]{1,0:T(8,128)S(1)} %bitcast.9, f32[8,2,144,128]{3,2,1,0:T(8,128)S(1)} %get-tuple-element.22.kept, f32[1,2,144,128]{3,2,1,0:T(8,128)S(1)} %get-tuple-element.28.weights, ...), custom_call_target="tpu_custom_call", output_to_operand_aliasing={{1}: (3, {})} | custom-call | flops 3276800 | bytes 3362816 | tf_op jit(solution)/shard_map/between/pallas_call | solution.py:500
  29.8 4.0 %all-to-all-done.1 = f32[8,1,128]{2,1,0:T(1,128)S(1)} async-done(((f32[8,1,128]{2,1,0:T(1,128)}), f32[8,1,128]{2,1,0:T(1,128)S(1)}, u32[]{:S(2)}, u32[]{:S(2)}) %all-to-all-start.1) | async-done | bytes 4128 | tf_op jit(solution)/shard_map/all_to_all | solution.py:523
  33.8 0.0 copy-done.1
  33.8 3.2 %finish.1 = (f32[256,128]{1,0:T(8,128)}, f32[256,128]{1,0:T(8,128)}) custom-call(f32[8,128]{1,0:T(8,128)S(1)} %bitcast.10, f32[8,128]{1,0:T(8,128)S(1)} %bitcast.11, f32[8,2,144,128]{3,2,1,0:T(8,128)S(1)} %get-tuple-element.22.kept, f32[6,2,144,128]{3,2,1,0:T(8,128)S(1)} %get-tuple-element.26.at_one, f32[3,2,144,128]{3,2,1,0:T(8,128)S(1)} %copy-done.1, ...), custom_call_target="tpu_custom_call" | custom-call | flops 9830400 | bytes 3481600 | tf_op jit(solution)/shard_map/finish/pallas_call | solution.py:500
  (1 shorter events, 0.0 us)
Async XLA Ops:
  2.6 11.7 %collective-permute-start.1 = (f32[9,2,8,128]{3,2,1,0:T(8,128)S(1)}, f32[9,2,8,128]{3,2,1,0:T(8,128)S(1)}, u32[]{:S(2)}, u32[]{:S(2)}) collective-permute-start(f32[9,2,8,128]{3,2,1,0:T(8,128)S(1)} %get-tuple-element.20), channel_id=1, source_target_pairs={{0,1},{1,0},{2,3},{3,2},{4,5},{5,4},{6,7},{7,6},{8,9},{9,8},{10,11... | collective-permute-start | bytes 221192 | tf_op jit(solution)/shard_map/ppermute | solution.py:516
  3.2 11.2 %collective-permute-start.2 = (f32[9,2,8,128]{3,2,1,0:T(8,128)S(1)}, f32[9,2,8,128]{3,2,1,0:T(8,128)S(1)}, u32[]{:S(2)}, u32[]{:S(2)}) collective-permute-start(f32[9,2,8,128]{3,2,1,0:T(8,128)S(1)} %get-tuple-element.21), channel_id=1, source_target_pairs={{1,2},{2,1},{3,4},{4,3},{5,6},{6,5},{7,8},{8,7},{9,10},{10,9},{11,... | collective-permute-start | bytes 221192 | tf_op jit(solution)/shard_map/ppermute | solution.py:516
  3.8 4.8 %collective-permute-start = (f32[8,128]{1,0:T(8,128)S(1)}, f32[8,128]{1,0:T(8,128)S(1)}, u32[]{:S(2)}, u32[]{:S(2)}) collective-permute-start(f32[8,128]{1,0:T(8,128)S(1)} %get-tuple-element.17), channel_id=1, source_target_pairs={{0,1},{1,0},{2,3},{3,2},{4,5},{5,4},{6,7},{7,6},{8,9},{9,8},{10,11... | collective-permute-start | bytes 12296 | tf_op jit(solution)/shard_map/ppermute | solution.py:521
  9.2 11.5 %all-to-all-start = ((f32[8,1,128]{2,1,0:T(1,128)}), f32[8,1,128]{2,1,0:T(1,128)S(1)}, u32[]{:S(2)}, u32[]{:S(2)}) async-start(f32[8,1,128]{2,1,0:T(1,128)} %bitcast.1), calls=%async_computation | async-start | bytes 8192 | tf_op jit(solution)/shard_map/all_to_all | solution.py:523
  21.6 0.8 %copy-start = (f32[3,2,144,128]{3,2,1,0:T(8,128)}, f32[3,2,144,128]{3,2,1,0:T(8,128)S(1)}, u32[]{:S(2)}) copy-start(f32[3,2,144,128]{3,2,1,0:T(8,128)S(1)} %get-tuple-element.27.mid) | copy-start | bytes 1327108
  22.4 1.2 %collective-permute-start.3 = (f32[8,128]{1,0:T(8,128)S(1)}, f32[8,128]{1,0:T(8,128)S(1)}, u32[]{:S(2)}, u32[]{:S(2)}) collective-permute-start(f32[8,128]{1,0:T(8,128)S(1)} %get-tuple-element.25), channel_id=1, source_target_pairs={{0,1},{1,0},{2,3},{3,2},{4,5},{5,4},{6,7},{7,6},{8,9},{9,8},{10,11... | collective-permute-start | bytes 12296 | tf_op jit(solution)/shard_map/ppermute | solution.py:521
  24.2 9.6 %all-to-all-start.1 = ((f32[8,1,128]{2,1,0:T(1,128)}), f32[8,1,128]{2,1,0:T(1,128)S(1)}, u32[]{:S(2)}, u32[]{:S(2)}) async-start(f32[8,1,128]{2,1,0:T(1,128)} %bitcast.4), calls=%async_computation.1 | async-start | bytes 8192 | tf_op jit(solution)/shard_map/all_to_all | solution.py:523
  27.5 6.3 %copy-start.1 = (f32[3,2,144,128]{3,2,1,0:T(8,128)S(1)}, f32[3,2,144,128]{3,2,1,0:T(8,128)}, u32[]{:S(2)}) copy-start(f32[3,2,144,128]{3,2,1,0:T(8,128)} %copy-done) | copy-start | bytes 1327108

commit v4 on v2

--- a/solution.py
+++ b/solution.py
@@ -103,8 +103,8 @@
     return inv_speed, dry * height * inv_speed, turbulent * (squared * inv_speed)
 
 
-def step_length(rows, shape):
-    return COURANT / jnp.broadcast_to(jnp.max(rows[...], axis=0, keepdims=True), shape)
+def step_length(row, last, shape):
+    return COURANT / jnp.broadcast_to(jnp.maximum(row[:1, :], last[:1, :]), shape)
 
 
 def prepare(*refs):
@@ -233,9 +233,9 @@
 MU, MV, MZ, MW, ME, MB, MM, MH, MY = range(9)
 
 
-def middle(top_rows, kept, xy, count_row, at_one, mid, row, work):
+def middle(top, last, kept, xy, count_row, at_one, mid, row, work):
     grid = Grid(kept.shape[1], kept.shape[2])
-    dt = step_length(top_rows, grid.lane.shape)
+    dt = step_length(top, last, grid.lane.shape)
     half = 0.5 * dt
 
     def first(t, col):
@@ -279,14 +279,42 @@
         return jnp.maximum(most, jnp.where(own, speed_of(*found), 0.0))
 
     fastest = grid.sweep(second, carry=jnp.zeros(grid.lane.shape, jnp.float32))
-    lane = lax.broadcasted_iota(jnp.int32, row.shape, 1)
-    count = jnp.broadcast_to(count_row[...], row.shape)
-    row[...] = jnp.where(lane < LANES // 2, jnp.full(row.shape, jnp.max(fastest), jnp.float32), count)
-
-
-def between(top_rows, kept, weights, change, at_one, smooth, tan, work, bent):
+    row[0:1, :] = jnp.full((1, LANES), jnp.max(fastest), jnp.float32)
+    row[1:2, :] = count_row[...]
+
+
+def regularize(kept, weights, smooth, bent):
     grid = Grid(kept.shape[1], kept.shape[2])
-    dt = step_length(top_rows, grid.lane.shape)
+
+    def spread(t, col):
+        for k, field in enumerate((DM, DX)):
+            grid.spare_put(bent, k, col, grid.get(kept, field, col))
+
+    grid.sweep(spread)
+
+    def laplace(k, col):
+        value = grid.spare_get(bent, k, col)
+        rn, rp = grid.both_rows(value)
+        cn, cp = grid.both_cols(bent, k, col)
+        return 4.0 * value - rn - rp - cn - cp
+
+    def bend(t, col):
+        weight = grid.get(weights, 0, col)
+        for k in range(2):
+            grid.spare_put(bent, 2 + k, col, weight * laplace(k, col))
+
+    grid.sweep(bend)
+
+    def bend_again(t, col):
+        for k in range(2):
+            grid.put(smooth, k, col - TILE, laplace(2 + k, col))
+
+    grid.sweep_own(bend_again)
+
+
+def tangent_one(top, last, kept, change, at_one, one, part):
+    grid = Grid(kept.shape[1], kept.shape[2])
+    dt = step_length(top, last, grid.lane.shape)
     half = 0.5 * dt
 
     def first(t, col):
@@ -297,66 +325,34 @@
         along = grid.get(at_one, CZ, col) * (u * tp + v * tq) + moved
         mixed = v * tp + u * tq
         for k, value in enumerate((tp, tq, mixed, 2.0 * v * tq)):
-            grid.spare_put(work, k, col, value)
-        for k, field in enumerate((DM, DX)):
-            grid.spare_put(bent, k, col, grid.get(kept, field, col))
+            grid.spare_put(one, k, col, value)
         moved = half * tp
-        grid.put(tan, 0, col, grid.rows_prev(moved) - grid.rows_next(moved))
+        grid.put(part, 0, col, grid.rows_prev(moved) - grid.rows_next(moved))
         sources = (-dt * (u * along + w * tp), -dt * (v * along + w * tq))
         for k, (value, flux) in enumerate(((tp, 2.0 * u * tp), (tq, mixed))):
             tenth, moved = 0.1 * value, half * flux
             total = 0.6 * value + sources[k]
             total += grid.rows_next(tenth - moved) + grid.rows_prev(tenth + moved)
-            grid.put(tan, 1 + k, col, total)
+            grid.put(part, 1 + k, col, total)
 
     grid.sweep(first)
 
-    def laplace(k, col):
-        value = grid.spare_get(bent, k, col)
-        rn, rp = grid.both_rows(value)
-        cn, cp = grid.both_cols(bent, k, col)
-        return 4.0 * value - rn - rp - cn - cp
+
+def tangent_mid(top, last, kept, mid, one, part_one, part, at_mid, work):
+    grid = Grid(kept.shape[1], kept.shape[2])
+    dt = step_length(top, last, grid.lane.shape)
+    half = 0.5 * dt
 
     def second(t, col):
         keep = grid.inside(t)
-        qn, qp = grid.both_cols(work, 1, col)
-        pn, pp = grid.both_cols(work, 0, col)
-        gn, gp = grid.both_cols(work, 2, col)
-        fn, fp = grid.both_cols(work, 3, col)
-        th = grid.get(tan, 0, col) - half * (qn - qp)
-        tp = grid.get(tan, 1, col) + 0.1 * (pn + pp) - half * (gn - gp)
-        tq = grid.get(tan, 2, col) + 0.1 * (qn + qp) - half * (fn - fp)
-        for k, value in enumerate((th, tp, tq)):
-            grid.put(tan, k, col, jnp.where(keep, 0.5 * value, 0.0))
-        weight = grid.get(weights, 0, col)
-        for k in range(2):
-            grid.spare_put(bent, 2 + k, col, weight * laplace(k, col))
-
-    grid.sweep(second)
-
-    def third(t, col):
-        for k in range(2):
-            grid.put(smooth, k, col - TILE, laplace(2 + k, col))
-
-    grid.sweep_own(third)
-
-
-def finish(cells, top_rows, next_rows, kept, at_one, mid, tan, smooth, out_mu, out_xi, at_mid, end, work, total):
-    grid = Grid(kept.shape[1], kept.shape[2])
-    shape = grid.lane.shape
-    dt0 = step_length(top_rows, shape)
-    rows = next_rows[...]
-    lane = lax.broadcasted_iota(jnp.int32, (1, LANES), 1)
-    most = jnp.max(rows, axis=0, keepdims=True)
-    added = jnp.sum(rows, axis=0, keepdims=True)
-    dt1 = COURANT / jnp.broadcast_to(jnp.where(lane < LANES // 2, most, pltpu.roll(most, LANES // 2, 1)), shape)
-    count = jnp.where(lane < LANES // 2, pltpu.roll(added, LANES // 2, 1), added)
-    weight = jnp.broadcast_to((DATA_WEIGHT * cells) / count, shape)
-    half1 = 0.5 * dt1
-    half0 = 0.5 * dt0
-
-    def open_end(t, col):
-        th, tp, tq = (grid.get(tan, k, col) for k in range(3))
+        qn, qp = grid.both_cols(one, 1, col)
+        pn, pp = grid.both_cols(one, 0, col)
+        gn, gp = grid.both_cols(one, 2, col)
+        fn, fp = grid.both_cols(one, 3, col)
+        th = grid.get(part_one, 0, col) - half * (qn - qp)
+        tp = grid.get(part_one, 1, col) + 0.1 * (pn + pp) - half * (gn - gp)
+        tq = grid.get(part_one, 2, col) + 0.1 * (qn + qp) - half * (fn - fp)
+        th, tp, tq = (jnp.where(keep, 0.5 * x, 0.0) for x in (th, tp, tq))
         height, down, across = (grid.get(mid, k, col) for k in range(3))
         inv, u, v = velocities(height, down, across)
         above = jnp.where(height > DEPTH_FLOOR, 1.0, jnp.where(height == DEPTH_FLOOR, 0.5, 0.0))
@@ -376,33 +372,57 @@
         mixed = v * tp + u * tq - u * v * lift
         for k, value in enumerate((th, tp, tq, mixed, 2.0 * v * tq + eight * th - v * v * lift)):
             grid.spare_put(work, k, col, value)
-        tenths = (0.1 * th, 0.1 * tp, 0.1 * tq)
-        moves = (half1 * tp, half1 * flux_down, half1 * mixed)
-        sources = (0.0, dt1 * (SIN_SLOPE * th - u * along - w * tp), -dt1 * (v * along + w * tq))
-        for k, value in enumerate((th, tp, tq)):
-            total_k = 0.6 * value + sources[k]
-            total_k += grid.rows_next(tenths[k] - moves[k]) + grid.rows_prev(tenths[k] + moves[k])
-            grid.spare_put(end, k, col, total_k)
-
-    grid.sweep(open_end)
-
-    def close_end(t, col):
+        hn, hp = grid.both_rows(th)
+        pn, pp = grid.both_rows(tp)
+        qn, qp = grid.both_rows(tq)
+        fn, fp = grid.both_rows(flux_down)
+        gn, gp = grid.both_rows(mixed)
+        grid.put(part, 0, col, 0.6 * th + 0.1 * (hn + hp))
+        grid.put(part, 1, col, 0.6 * tp + 0.1 * (pn + pp))
+        grid.put(part, 2, col, 0.6 * tq + 0.1 * (qn + qp))
+        grid.put(part, 3, col, -0.5 * (pn - pp))
+        grid.put(part, 4, col, SIN_SLOPE * th - u * along - w * tp - 0.5 * (fn - fp))
+        grid.put(part, 5, col, -v * along - w * tq - 0.5 * (gn - gp))
+
+    grid.sweep(second)
+
+
+def tangent_end(part, work, tan):
+    grid = Grid(part.shape[1], part.shape[2])
+
+    def third(t, col):
         keep = grid.inside(t)
-        for k, (value, flux) in enumerate(((0, 2), (1, 3), (2, 4))):
-            vn, vp = grid.both_cols(work, value, col)
-            fn, fp = grid.both_cols(work, flux, col)
-            found = grid.spare_get(end, k, col) + 0.1 * (vn + vp) - half1 * (fn - fp)
-            grid.spare_put(end, k, col, jnp.where(keep, found, 0.0))
-
-    grid.sweep(close_end)
+        hn, hp = grid.both_cols(work, 0, col)
+        pn, pp = grid.both_cols(work, 1, col)
+        qn, qp = grid.both_cols(work, 2, col)
+        gn, gp = grid.both_cols(work, 3, col)
+        fn, fp = grid.both_cols(work, 4, col)
+        for k, (n, p) in enumerate(((hn, hp), (pn, pp), (qn, qp))):
+            grid.spare_put(tan, k, col, jnp.where(keep, grid.get(part, k, col) + 0.1 * (n + p), 0.0))
+        for k, (n, p) in enumerate(((qn, qp), (gn, gp), (fn, fp))):
+            grid.spare_put(tan, 3 + k, col, jnp.where(keep, grid.get(part, 3 + k, col) - 0.5 * (n - p), 0.0))
+
+    grid.sweep(third)
+
+
+def finish(cells, top, last, fast, fast_last, kept, at_one, at_mid, between, tan, smooth, out_mu, out_xi, work, total):
+    grid = Grid(kept.shape[1], kept.shape[2])
+    shape = grid.lane.shape
+    dt0 = step_length(top, last, shape)
+    dt1 = step_length(fast, fast_last, shape)
+    weight = jnp.broadcast_to((DATA_WEIGHT * cells) / jnp.maximum(fast[1:2, :], fast_last[1:2, :]), shape)
+    half1 = 0.5 * dt1
+    half0 = 0.5 * dt0
 
     def seed_end(t, col):
-        th, tp = grid.spare_get(end, 0, col), grid.spare_get(end, 1, col)
+        def section(k, off):
+            return grid.spare_get(tan, k, col, off) + dt1 * grid.spare_get(tan, 3 + k, col, off)
+
+        th, tp = section(0, 0), section(1, 0)
         tenth, moved = 0.1 * th, half1 * tp
-        hn, hp = grid.both_cols(end, 0, col)
-        qn, qp = grid.both_cols(end, 2, col)
-        value = grid.get(tan, 0, col) + 0.6 * th + grid.rows_next(tenth - moved) + grid.rows_prev(tenth + moved)
-        value += 0.1 * (hn + hp) - half1 * (qn - qp)
+        value = grid.spare_get(between, 0, col) + 0.6 * th
+        value += grid.rows_next(tenth - moved) + grid.rows_prev(tenth + moved)
+        value += 0.1 * (section(0, 1) + section(0, -1)) - half1 * (section(2, 1) - section(2, -1))
         grid.spare_put(work, 0, col, weight * grid.get(kept, OB, col) * (0.5 * value))
 
     grid.sweep(seed_end)
@@ -510,14 +530,37 @@
     )(*operands)
 
 
-def swap_edges(edge_a, edge_b, count):
-    pairs_a = [(i, i ^ 1) for i in range(count)]
-    pairs_b = [(i, i - 1 if i % 2 == 0 else i + 1) for i in range(1, count - 1)]
-    return lax.ppermute(edge_a, "cross", pairs_a), lax.ppermute(edge_b, "cross", pairs_b)
-
-
-def share(row):
-    return lax.all_to_all(row, "cross", 0, 0, tiled=True)
+def swap(value, other):
+    count = lax.axis_size("cross")
+    pairs = [(i, other(i)) for i in range(count) if other(i) is not None and 0 <= other(i) < count]
+    return lax.ppermute(value, "cross", pairs)
+
+
+def other_core(i):
+    return i ^ 1
+
+
+def next_chip(i):
+    return i - 1 if i % 2 == 0 else i + 1
+
+
+def odd_far(step):
+    return lambda i: i ^ step if i % 2 == 1 else None
+
+
+def to_even(i):
+    return i - 1 if i % 2 == 1 else None
+
+
+def max_and_sum(a, b):
+    return jnp.where(lax.broadcasted_iota(jnp.int32, a.shape, 0) == 0, jnp.maximum(a, b), a + b)
+
+
+def round_beside(row, other, result=None):
+    arrived = swap(row, other)
+    if result is not None:
+        arrived, result = lax.optimization_barrier((arrived, result))
+    return max_and_sum(row, arrived), result
 
 
 def local(state, log_mu, log_xi, dir_mu, dir_xi, wet, observed, terrain, class_weight):
@@ -536,48 +579,66 @@
         prepare,
         "prepare",
         inputs,
-        [(KEPT,) + wide, (1,) + wide, edge, edge, (count, LANES), (1, LANES)],
+        [(KEPT,) + wide, (1,) + wide, edge, edge, (1, LANES), (1, LANES)],
         [(rows, cols), (3,) + own]
         + [pltpu.VMEM(x.shape, x.dtype) for x in inputs[:-1]]
         + [pltpu.SMEM(class_weight.shape, jnp.float32), pltpu.SemaphoreType.DMA((len(inputs),))],
         100 * work,
         spaces=[ANY] * len(inputs),
     )
-    edge_a, edge_b = swap_edges(edge_a, edge_b, count)
-    top_rows = share(row)
+    steps = [2**k for k in range(1, count.bit_length() - 1)]
+    edge_a = swap(edge_a, other_core)
+    row = jnp.maximum(row, swap(row, other_core))
+    for step in steps[:-1]:
+        row = jnp.maximum(row, swap(row, odd_far(step)))
+        if step == 2:
+            row, edge_b = lax.optimization_barrier((row, edge_b))
+            edge_b = swap(edge_b, next_chip)
     kept, weights, xy, change = call(
         open_step,
         "open_step",
         (kept, weights, edge_a, edge_b),
-        [(KEPT,) + wide, (1,) + wide, (6,) + wide, (3,) + wide],
+        [(KEPT,) + wide, (1,) + wide, (6,) + wide, (2,) + wide],
         [(5,) + spare],
         100 * work,
         aliases={0: 0, 1: 1},
     )
-    at_one, mid, next_row = call(
+    arrived, xy = lax.optimization_barrier((swap(row, odd_far(steps[-1])), xy))
+    top = jnp.maximum(row, arrived)
+    last = swap(top, to_even)
+    at_one, mid, row = call(
         middle,
         "middle",
-        (top_rows, kept, xy, count_row),
-        [(6,) + wide, (3,) + wide, (count, LANES)],
+        (top, last, kept, xy, count_row),
+        [(6,) + wide, (3,) + wide, (2, LANES)],
         [(5,) + spare],
         120 * work,
     )
-    next_rows = share(next_row)
-    smooth, tan = call(
-        between,
-        "between",
-        (top_rows, kept, weights, change, at_one),
-        [(2,) + own, (3,) + wide],
-        [(4,) + spare, (4,) + spare],
-        100 * work,
-        aliases={3: 1},
+    (smooth,) = call(regularize, "regularize", (kept, weights), [(2,) + own], [(4,) + spare], 30 * work)
+    row, smooth = round_beside(row, other_core, smooth)
+    one, part = call(
+        tangent_one, "tangent_one", (top, last, kept, change, at_one), [(4,) + spare, (3,) + wide], [], 60 * work
     )
+    row, one = round_beside(row, odd_far(steps[0]), one)
+    part, at_mid, between = call(
+        tangent_mid,
+        "tangent_mid",
+        (top, last, kept, mid, one, part),
+        [(6,) + wide, (9,) + wide, (5,) + spare],
+        [],
+        120 * work,
+    )
+    row, part = round_beside(row, odd_far(steps[1]), part)
+    (tan,) = call(tangent_end, "tangent_end", (part, between), [(6,) + spare], [], 30 * work)
+    row, tan = round_beside(row, odd_far(steps[2]), tan)
+    for step in steps[3:]:
+        row, _ = round_beside(row, odd_far(step))
     return call(
         functools.partial(finish, float(rows * cols * count)),
         "finish",
-        (top_rows, next_rows, kept, at_one, mid, tan, smooth),
+        (top, last, row, swap(row, to_even), kept, at_one, at_mid, between, tan, smooth),
         [(rows, cols), (rows, cols)],
-        [(9,) + wide, (3,) + spare, (7,) + spare, (2,) + wide],
+        [(7,) + spare, (2,) + wide],
         300 * work,
     )
 

time: 35 us -> 44.7 us (1.28)
  waiting for transfers between devices: 9.34 us -> 22.6 us
  Pallas kernels: 10.5 us -> 8.62 us
  starting transfers between devices: 13.5 us -> 12 us
  local copies, waits for them, and re-layouts: 0.76 us -> 0 us
    ppermute x2 -> x12, waiting for transfers between devices: 0.01 us -> 22.6 us  [swap(): return lax.ppermute(value, 'cross', pairs)]
    all_to_all x2 -> x0, starting transfers between devices: 12.3 us -> none  [share(): return lax.all_to_all(row, 'cross', 0, 0, tiled=True)]
    ppermute x2 -> x12, starting transfers between devices: 1.17 us -> 12 us  [swap(): return lax.ppermute(value, 'cross', pairs)]
    all_to_all x2 -> x0, waiting for transfers between devices: 9.34 us -> none  [share(): return lax.all_to_all(row, 'cross', 0, 0, tiled=True)]
    pallas_call x5 -> x8, Pallas kernels: 10.5 us -> 8.62 us  [call(): pl.pallas_call(body, name=name, out_shape=outs, in_specs=spaces or [VMEM]...]
    unnamed x4 -> x0, local copies, waits for them, and re-layouts: 0.76 us -> none
  transfers between devices with their start and end apart: 4 -> 12, of which waited for: 2 -> 4; matrix products, arithmetic and copies ran while one was open for 0% -> 0% of each run, Pallas kernels for 9% -> 7%
where the time goes in v4:
time: 44.7 us; the launch traced here: 44.3 us
  waiting for transfers between devices  22.6 us (51%)
  starting transfers between devices  12 us (27%)
  Pallas kernels  8.62 us (19%)
  between operations  0.82 us (2%)
    ppermute x12, waiting for transfers between devices, swap(): return lax.ppermute(value, 'cross', pairs)  22.6 us
    ppermute x12, starting transfers between devices, swap(): return lax.ppermute(value, 'cross', pairs)  12 us
    pallas_call x8, Pallas kernels, call(): pl.pallas_call(body, name=name, out_shape=outs, in_specs=spaces or [VMEM]...  8.62 us
  transfers between devices with their start and end apart: 12, of which 4 were waited for; matrix products, arithmetic and copies ran while one was open for 0% of the time, Pallas kernels for 7%

profile of v4, /device:TPU:0, one launch (start us, length us, event | category | flops | bytes accessed | tf_op | source)
XLA Modules:
  0.0 44.3 jit_solution(14512253790292567634)
XLA Ops:
  0.6 2.0 %prepare.1 = (f32[8,2,144,128]{3,2,1,0:T(8,128)S(1)}, f32[1,2,144,128]{3,2,1,0:T(8,128)S(1)}, f32[9,2,8,128]{3,2,1,0:T(8,128)S(1)}, f32[9,2,8,128]{3,2,1,0:T(8,1...) custom-call(f32[3,256,128]{2,1,0:T(8,128)} %refs_0_.1, f32[256,128]{1,0:T(8,128)} %refs_1_.1, f32[256,128]{1,0:T(8,128)} %refs_2_.1, ...), custom_call_target="tpu_custom_call" | custom-call | flops 3276800 | bytes 2786336 | tf_op jit(solution)/shard_map/prepare/pallas_call | solution.py:520
  2.6 0.5 %collective-permute-start = (f32[1,128]{1,0:T(1,128)S(1)}, f32[1,128]{1,0:T(1,128)S(1)}, u32[]{:S(2)}, u32[]{:S(2)}) collective-permute-start(f32[1,128]{1,0:T(1,128)S(1)} %get-tuple-element.32), channel_id=1, source_target_pairs={{0,1},{1,0},{2,3},{3,2},{4,5},{5,4},{6,7},{7,6},{8,9},{9,8},{10,11... | collective-permute-start | bytes 1544 | tf_op jit(solution)/shard_map/ppermute | solution.py:536
  3.2 0.8 %collective-permute-done = f32[1,128]{1,0:T(1,128)S(1)} collective-permute-done((f32[1,128]{1,0:T(1,128)S(1)}, f32[1,128]{1,0:T(1,128)S(1)}, u32[]{:S(2)}, u32[]{:S(2)}) %collective-permute-start) | collective-permute-done | bytes 544 | tf_op jit(solution)/shard_map/ppermute | solution.py:536
  4.0 0.6 %collective-permute-start.1 = (f32[1,128]{1,0:T(1,128)S(1)}, f32[1,128]{1,0:T(1,128)S(1)}, u32[]{:S(2)}, u32[]{:S(2)}) collective-permute-start(f32[1,128]{1,0:T(1,128)S(1)} %max.24), channel_id=1, source_target_pairs={{1,3},{3,1},{5,7},{7,5},{9,11},{11,9},{13,15},{15,13},{17,19},{19,... | collective-permute-start | bytes 1544 | tf_op jit(solution)/shard_map/ppermute | solution.py:536
  4.6 4.1 %collective-permute-start.4 = (f32[9,2,8,128]{3,2,1,0:T(8,128)S(1)}, f32[9,2,8,128]{3,2,1,0:T(8,128)S(1)}, u32[]{:S(2)}, u32[]{:S(2)}) collective-permute-start(f32[9,2,8,128]{3,2,1,0:T(8,128)S(1)} %get-tuple-element.37), channel_id=1, source_target_pairs={{0,1},{1,0},{2,3},{3,2},{4,5},{5,4},{6,7},{7,6},{8,9},{9,8},{10,11... | collective-permute-start | bytes 221192 | tf_op jit(solution)/shard_map/ppermute | solution.py:536
  8.7 0.7 %collective-permute-start.5 = (f32[9,2,8,128]{3,2,1,0:T(8,128)S(1)}, f32[9,2,8,128]{3,2,1,0:T(8,128)S(1)}, u32[]{:S(2)}, u32[]{:S(2)}) collective-permute-start(f32[9,2,8,128]{3,2,1,0:T(8,128)S(1)} %get-tuple-element.38), channel_id=1, source_target_pairs={{1,2},{2,1},{3,4},{4,3},{5,6},{6,5},{7,8},{8,7},{9,10},{10,9},{11,... | collective-permute-start | bytes 221192 | tf_op jit(solution)/shard_map/ppermute | solution.py:536
  9.4 0.7 %collective-permute-start.2 = (f32[1,128]{1,0:T(1,128)S(1)}, f32[1,128]{1,0:T(1,128)S(1)}, u32[]{:S(2)}, u32[]{:S(2)}) collective-permute-start(f32[1,128]{1,0:T(1,128)S(1)} %max.25), channel_id=1, source_target_pairs={{1,5},{3,7},{5,1},{7,3},{9,13},{11,15},{13,9},{15,11},{17,21},{19,... | collective-permute-start | bytes 1544 | tf_op jit(solution)/shard_map/ppermute | solution.py:536
  10.1 0.7 %collective-permute-start.3 = (f32[1,128]{1,0:T(1,128)S(1)}, f32[1,128]{1,0:T(1,128)S(1)}, u32[]{:S(2)}, u32[]{:S(2)}) collective-permute-start(f32[1,128]{1,0:T(1,128)S(1)} %max.26), channel_id=1, source_target_pairs={{1,9},{3,11},{5,13},{7,15},{9,1},{11,3},{13,5},{15,7},{17,25},{19,... | collective-permute-start | bytes 1544 | tf_op jit(solution)/shard_map/ppermute | solution.py:536
  10.7 0.0 collective-permute-done.4.edge_a
  10.7 0.0 collective-permute-done.5.edge_b
  10.7 0.9 %open_step.1 = (f32[8,2,144,128]{3,2,1,0:T(8,128)S(1)}, f32[1,2,144,128]{3,2,1,0:T(8,128)S(1)}, f32[6,2,144,128]{3,2,1,0:T(8,128)S(1)}, f32[2,2,144,128]{3,2,1,0:T(8,128)S(1)}) custom-call(f32[8,2,144,128]{3,2,1,0:T(8,128)S(1)} %get-tuple-element.35.kept_in, ...), custom_call_target="tpu_custom_call", output_to_operand_aliasing={{0}: (0, {}), {1}: (1, {})} | custom-call | flops 3276800 | bytes 3981312 | tf_op jit(solution)/shard_map/open_step/pallas_call | solution.py:520
  11.7 0.0 collective-permute-done.3
  11.7 1.3 %collective-permute-start.6 = (f32[1,128]{1,0:T(1,128)S(1)}, f32[1,128]{1,0:T(1,128)S(1)}, u32[]{:S(2)}, u32[]{:S(2)}) collective-permute-start(f32[1,128]{1,0:T(1,128)S(1)} %max.27.top), channel_id=1, source_target_pairs={{1,0},{3,2},{5,4},{7,6},{9,8},{11,10},{13,12},{15,14},{17,16},{19,... | collective-permute-start | bytes 1544 | tf_op jit(solution)/shard_map/ppermute | solution.py:536
  13.0 10.1 %collective-permute-done.6.last = f32[1,128]{1,0:T(1,128)S(1)} collective-permute-done((f32[1,128]{1,0:T(1,128)S(1)}, f32[1,128]{1,0:T(1,128)S(1)}, u32[]{:S(2)}, u32[]{:S(2)}) %collective-permute-start.6) | collective-permute-done | bytes 544 | tf_op jit(solution)/shard_map/ppermute | solution.py:536
  23.0 0.9 %middle.1 = (f32[6,2,144,128]{3,2,1,0:T(8,128)S(1)}, f32[3,2,144,128]{3,2,1,0:T(8,128)S(1)}, f32[2,128]{1,0:T(2,128)S(1)}) custom-call(f32[1,128]{1,0:T(1,128)S(1)} %max.27.top, f32[1,128]{1,0:T(1,128)S(1)} %collective-permute-done.6.last, f32[8,2,144,128]{3,2,1,0:T(8,128)S(1)} %get-tuple-element.41.kept, f32[6,2,144,128]{3,2,1,0:T(8,128)S(1)} %get-tuple-element.42.xy, ...), custom_call_target="tpu_custom_call" | custom-call | flops 3932160 | bytes 3394048 | tf_op jit(solution)/shard_map/middle/pallas_call | solution.py:520
  24.0 0.3 collective-permute-start.7
  24.3 0.7 %regularize.1.smooth = f32[2,2,128,128]{3,2,1,0:T(8,128)S(1)} custom-call(f32[8,2,144,128]{3,2,1,0:T(8,128)S(1)} %get-tuple-element.41.kept, f32[1,2,144,128]{3,2,1,0:T(8,128)S(1)} %get-tuple-element.45.weights), custom_call_target="tpu_custom_call" | custom-call | flops 983040 | bytes 1589248 | tf_op jit(solution)/shard_map/regularize/pallas_call | solution.py:520
  25.0 0.2 collective-permute-done.7
  25.2 0.1 add_select_fusion.3
  25.3 0.7 %collective-permute-start.8 = (f32[2,128]{1,0:T(2,128)S(1)}, f32[2,128]{1,0:T(2,128)S(1)}, u32[]{:S(2)}, u32[]{:S(2)}) collective-permute-start(f32[2,128]{1,0:T(2,128)S(1)} %add_select_fusion.3), channel_id=1, source_target_pairs={{1,3},{3,1},{5,7},{7,5},{9,11},{11,9},{13,15},{15,13},{17,19},{19,... | collective-permute-start | bytes 3080 | tf_op jit(solution)/shard_map/ppermute | solution.py:536
  25.9 0.5 %tangent_one.1 = (f32[4,2,160,128]{3,2,1,0:T(8,128)S(1)}, f32[3,2,144,128]{3,2,1,0:T(8,128)S(1)}) custom-call(f32[1,128]{1,0:T(1,128)S(1)} %max.27.top, f32[1,128]{1,0:T(1,128)S(1)} %collective-permute-done.6.last, f32[8,2,144,128]{3,2,1,0:T(8,128)S(1)} %get-tuple-element.41.kept, f32[2,2,144,128]{3,2,1,0:T(8,128)S(1)} %get-tuple-element.47.change, ...), custom_call_target="tpu_custom_call" | custom-call | flops 1966080 | bytes 3458048 | tf_op jit(solution)/shard_map/tangent_one/pallas_call | solution.py:520
  26.4 0.1 add_select_fusion.2
  26.5 0.7 %collective-permute-start.9 = (f32[2,128]{1,0:T(2,128)S(1)}, f32[2,128]{1,0:T(2,128)S(1)}, u32[]{:S(2)}, u32[]{:S(2)}) collective-permute-start(f32[2,128]{1,0:T(2,128)S(1)} %add_select_fusion.2), channel_id=1, source_target_pairs={{1,5},{3,7},{5,1},{7,3},{9,13},{11,15},{13,9},{15,11},{17,21},{19,... | collective-permute-start | bytes 3080 | tf_op jit(solution)/shard_map/ppermute | solution.py:536
  27.1 0.7 %tangent_mid.1 = (f32[6,2,144,128]{3,2,1,0:T(8,128)S(1)}, f32[9,2,144,128]{3,2,1,0:T(8,128)S(1)}, f32[5,2,160,128]{3,2,1,0:T(8,128)S(1)}) custom-call(f32[1,128]{1,0:T(1,128)S(1)} %max.27.top, f32[1,128]{1,0:T(1,128)S(1)} %collective-permute-done.6.last, f32[8,2,144,128]{3,2,1,0:T(8,128)S(1)} %get-tuple-element.41.kept, ...), custom_call_target="tpu_custom_call" | custom-call | flops 3932160 | bytes 5751808 | tf_op jit(solution)/shard_map/tangent_mid/pallas_call | solution.py:520
  27.8 0.1 add_select_fusion.1
  27.9 0.7 %collective-permute-start.10 = (f32[2,128]{1,0:T(2,128)S(1)}, f32[2,128]{1,0:T(2,128)S(1)}, u32[]{:S(2)}, u32[]{:S(2)}) collective-permute-start(f32[2,128]{1,0:T(2,128)S(1)} %add_select_fusion.1), channel_id=1, source_target_pairs={{1,9},{3,11},{5,13},{7,15},{9,1},{11,3},{13,5},{15,7},{17,25},{19,... | collective-permute-start | bytes 3080 | tf_op jit(solution)/shard_map/ppermute | solution.py:536
  28.6 0.3 tangent_end.1.tan
  28.8 0.0 collective-permute-done.10
  28.8 0.1 add_select_fusion.fast
  28.9 1.3 %collective-permute-start.11 = (f32[2,128]{1,0:T(2,128)S(1)}, f32[2,128]{1,0:T(2,128)S(1)}, u32[]{:S(2)}, u32[]{:S(2)}) collective-permute-start(f32[2,128]{1,0:T(2,128)S(1)} %add_select_fusion.fast), channel_id=1, source_target_pairs={{1,0},{3,2},{5,4},{7,6},{9,8},{11,10},{13,12},{15,14},{17,16},{19,... | collective-permute-start | bytes 3080 | tf_op jit(solution)/shard_map/ppermute | solution.py:536
  30.2 11.5 %collective-permute-done.11.fast_last = f32[2,128]{1,0:T(2,128)S(1)} collective-permute-done((f32[2,128]{1,0:T(2,128)S(1)}, f32[2,128]{1,0:T(2,128)S(1)}, u32[]{:S(2)}, u32[]{:S(2)}) %collective-permute-start.11) | collective-permute-done | bytes 1056 | tf_op jit(solution)/shard_map/ppermute | solution.py:536
  41.7 2.6 %finish.1 = (f32[256,128]{1,0:T(8,128)}, f32[256,128]{1,0:T(8,128)}) custom-call(f32[1,128]{1,0:T(1,128)S(1)} %max.27.top, f32[1,128]{1,0:T(1,128)S(1)} %collective-permute-done.6.last, f32[2,128]{1,0:T(2,128)S(1)} %add_select_fusion.fast, f32[2,128]{1,0:T(2,128)S(1)} %collective-permute-done.11.fast_last, f32[8,2,144,128]{3,2,1,0:T(8,128)S(1)} %get-tuple-element.41.kept, ...), custom_call_target="tpu_custom_call" | custom-call | flops 9830400 | bytes 5721088 | tf_op jit(solution)/shard_map/finish/pallas_call | solution.py:520
  (9 shorter events, 0.0 us)
Async XLA Ops:
  2.6 1.3 %collective-permute-start = (f32[1,128]{1,0:T(1,128)S(1)}, f32[1,128]{1,0:T(1,128)S(1)}, u32[]{:S(2)}, u32[]{:S(2)}) collective-permute-start(f32[1,128]{1,0:T(1,128)S(1)} %get-tuple-element.32), channel_id=1, source_target_pairs={{0,1},{1,0},{2,3},{3,2},{4,5},{5,4},{6,7},{7,6},{8,9},{9,8},{10,11... | collective-permute-start | bytes 1544 | tf_op jit(solution)/shard_map/ppermute | solution.py:536
  4.0 4.7 %collective-permute-start.1 = (f32[1,128]{1,0:T(1,128)S(1)}, f32[1,128]{1,0:T(1,128)S(1)}, u32[]{:S(2)}, u32[]{:S(2)}) collective-permute-start(f32[1,128]{1,0:T(1,128)S(1)} %max.24), channel_id=1, source_target_pairs={{1,3},{3,1},{5,7},{7,5},{9,11},{11,9},{13,15},{15,13},{17,19},{19,... | collective-permute-start | bytes 1544 | tf_op jit(solution)/shard_map/ppermute | solution.py:536
  4.6 6.1 %collective-permute-start.4 = (f32[9,2,8,128]{3,2,1,0:T(8,128)S(1)}, f32[9,2,8,128]{3,2,1,0:T(8,128)S(1)}, u32[]{:S(2)}, u32[]{:S(2)}) collective-permute-start(f32[9,2,8,128]{3,2,1,0:T(8,128)S(1)} %get-tuple-element.37), channel_id=1, source_target_pairs={{0,1},{1,0},{2,3},{3,2},{4,5},{5,4},{6,7},{7,6},{8,9},{9,8},{10,11... | collective-permute-start | bytes 221192 | tf_op jit(solution)/shard_map/ppermute | solution.py:536
  8.7 2.0 %collective-permute-start.5 = (f32[9,2,8,128]{3,2,1,0:T(8,128)S(1)}, f32[9,2,8,128]{3,2,1,0:T(8,128)S(1)}, u32[]{:S(2)}, u32[]{:S(2)}) collective-permute-start(f32[9,2,8,128]{3,2,1,0:T(8,128)S(1)} %get-tuple-element.38), channel_id=1, source_target_pairs={{1,2},{2,1},{3,4},{4,3},{5,6},{6,5},{7,8},{8,7},{9,10},{10,9},{11,... | collective-permute-start | bytes 221192 | tf_op jit(solution)/shard_map/ppermute | solution.py:536
  9.4 0.7 %collective-permute-start.2 = (f32[1,128]{1,0:T(1,128)S(1)}, f32[1,128]{1,0:T(1,128)S(1)}, u32[]{:S(2)}, u32[]{:S(2)}) collective-permute-start(f32[1,128]{1,0:T(1,128)S(1)} %max.25), channel_id=1, source_target_pairs={{1,5},{3,7},{5,1},{7,3},{9,13},{11,15},{13,9},{15,11},{17,21},{19,... | collective-permute-start | bytes 1544 | tf_op jit(solution)/shard_map/ppermute | solution.py:536
  10.1 1.6 %collective-permute-start.3 = (f32[1,128]{1,0:T(1,128)S(1)}, f32[1,128]{1,0:T(1,128)S(1)}, u32[]{:S(2)}, u32[]{:S(2)}) collective-permute-start(f32[1,128]{1,0:T(1,128)S(1)} %max.26), channel_id=1, source_target_pairs={{1,9},{3,11},{5,13},{7,15},{9,1},{11,3},{13,5},{15,7},{17,25},{19,... | collective-permute-start | bytes 1544 | tf_op jit(solution)/shard_map/ppermute | solution.py:536
  11.7 11.3 %collective-permute-start.6 = (f32[1,128]{1,0:T(1,128)S(1)}, f32[1,128]{1,0:T(1,128)S(1)}, u32[]{:S(2)}, u32[]{:S(2)}) collective-permute-start(f32[1,128]{1,0:T(1,128)S(1)} %max.27.top), channel_id=1, source_target_pairs={{1,0},{3,2},{5,4},{7,6},{9,8},{11,10},{13,12},{15,14},{17,16},{19,... | collective-permute-start | bytes 1544 | tf_op jit(solution)/shard_map/ppermute | solution.py:536
  24.0 1.2 %collective-permute-start.7 = (f32[2,128]{1,0:T(2,128)S(1)}, f32[2,128]{1,0:T(2,128)S(1)}, u32[]{:S(2)}, u32[]{:S(2)}) collective-permute-start(f32[2,128]{1,0:T(2,128)S(1)} %get-tuple-element.44), channel_id=1, source_target_pairs={{0,1},{1,0},{2,3},{3,2},{4,5},{5,4},{6,7},{7,6},{8,9},{9,8},{10,11... | collective-permute-start | bytes 3080 | tf_op jit(solution)/shard_map/ppermute | solution.py:536
  25.3 1.2 %collective-permute-start.8 = (f32[2,128]{1,0:T(2,128)S(1)}, f32[2,128]{1,0:T(2,128)S(1)}, u32[]{:S(2)}, u32[]{:S(2)}) collective-permute-start(f32[2,128]{1,0:T(2,128)S(1)} %add_select_fusion.3), channel_id=1, source_target_pairs={{1,3},{3,1},{5,7},{7,5},{9,11},{11,9},{13,15},{15,13},{17,19},{19,... | collective-permute-start | bytes 3080 | tf_op jit(solution)/shard_map/ppermute | solution.py:536
  26.5 1.3 %collective-permute-start.9 = (f32[2,128]{1,0:T(2,128)S(1)}, f32[2,128]{1,0:T(2,128)S(1)}, u32[]{:S(2)}, u32[]{:S(2)}) collective-permute-start(f32[2,128]{1,0:T(2,128)S(1)} %add_select_fusion.2), channel_id=1, source_target_pairs={{1,5},{3,7},{5,1},{7,3},{9,13},{11,15},{13,9},{15,11},{17,21},{19,... | collective-permute-start | bytes 3080 | tf_op jit(solution)/shard_map/ppermute | solution.py:536
  27.9 0.9 %collective-permute-start.10 = (f32[2,128]{1,0:T(2,128)S(1)}, f32[2,128]{1,0:T(2,128)S(1)}, u32[]{:S(2)}, u32[]{:S(2)}) collective-permute-start(f32[2,128]{1,0:T(2,128)S(1)} %add_select_fusion.1), channel_id=1, source_target_pairs={{1,9},{3,11},{5,13},{7,15},{9,1},{11,3},{13,5},{15,7},{17,25},{19,... | collective-permute-start | bytes 3080 | tf_op jit(solution)/shard_map/ppermute | solution.py:536
  28.9 12.8 %collective-permute-start.11 = (f32[2,128]{1,0:T(2,128)S(1)}, f32[2,128]{1,0:T(2,128)S(1)}, u32[]{:S(2)}, u32[]{:S(2)}) collective-permute-start(f32[2,128]{1,0:T(2,128)S(1)} %add_select_fusion.fast), channel_id=1, source_target_pairs={{1,0},{3,2},{5,4},{7,6},{9,8},{11,10},{13,12},{15,14},{17,16},{19,... | collective-permute-start | bytes 3080 | tf_op jit(solution)/shard_map/ppermute | solution.py:536

commit v5 on v4

--- a/solution.py
+++ b/solution.py
@@ -103,8 +103,12 @@
     return inv_speed, dry * height * inv_speed, turbulent * (squared * inv_speed)
 
 
+def known(row, last, k):
+    return jnp.where(lax.rem(lax.axis_index("cross"), 2) == 0, last[k : k + 1, :], row[k : k + 1, :])
+
+
 def step_length(row, last, shape):
-    return COURANT / jnp.broadcast_to(jnp.maximum(row[:1, :], last[:1, :]), shape)
+    return COURANT / jnp.broadcast_to(known(row, last, 0), shape)
 
 
 def prepare(*refs):
@@ -175,12 +179,14 @@
 
 
 def fill_halo(source, ref, j, k, edge_a, edge_b):
-    even = lax.rem(lax.axis_index("cross"), 2) == 0
+    me = lax.axis_index("cross")
+    even = lax.rem(me, 2) == 0
+    first, last = me == 0, me == lax.axis_size("cross") - 1
     wide = ref.shape[2]
     for g in range(ref.shape[1]):
         ref[j, g, TILE : wide - TILE, :] = source[j, g, TILE : wide - TILE, :]
-        ref[j, g, :TILE, :] = jnp.where(even, edge_b[k, g], edge_a[k, g])
-        ref[j, g, wide - TILE :, :] = jnp.where(even, edge_a[k, g], edge_b[k, g])
+        ref[j, g, :TILE, :] = jnp.where(first, 0.0, jnp.where(even, edge_b[k, g], edge_a[k, g]))
+        ref[j, g, wide - TILE :, :] = jnp.where(last, 0.0, jnp.where(even, edge_a[k, g], edge_b[k, g]))
 
 
 def open_step(kept_in, weights_in, edge_a, edge_b, kept, weights, xy, change, work):
@@ -410,7 +416,7 @@
     shape = grid.lane.shape
     dt0 = step_length(top, last, shape)
     dt1 = step_length(fast, fast_last, shape)
-    weight = jnp.broadcast_to((DATA_WEIGHT * cells) / jnp.maximum(fast[1:2, :], fast_last[1:2, :]), shape)
+    weight = jnp.broadcast_to((DATA_WEIGHT * cells) / known(fast, fast_last, 1), shape)
     half1 = 0.5 * dt1
     half0 = 0.5 * dt0
 
@@ -532,8 +538,7 @@
 
 def swap(value, other):
     count = lax.axis_size("cross")
-    pairs = [(i, other(i)) for i in range(count) if other(i) is not None and 0 <= other(i) < count]
-    return lax.ppermute(value, "cross", pairs)
+    return lax.ppermute(value, "cross", [(i, other(i) if 0 <= other(i) < count else i) for i in range(count)])
 
 
 def other_core(i):
@@ -545,11 +550,7 @@
 
 
 def odd_far(step):
-    return lambda i: i ^ step if i % 2 == 1 else None
-
-
-def to_even(i):
-    return i - 1 if i % 2 == 1 else None
+    return lambda i: i ^ step if i % 2 == 1 else i
 
 
 def max_and_sum(a, b):
@@ -605,7 +606,7 @@
     )
     arrived, xy = lax.optimization_barrier((swap(row, odd_far(steps[-1])), xy))
     top = jnp.maximum(row, arrived)
-    last = swap(top, to_even)
+    last = swap(top, other_core)
     at_one, mid, row = call(
         middle,
         "middle",
@@ -636,7 +637,7 @@
     return call(
         functools.partial(finish, float(rows * cols * count)),
         "finish",
-        (top, last, row, swap(row, to_even), kept, at_one, at_mid, between, tan, smooth),
+        (top, last, row, swap(row, other_core), kept, at_one, at_mid, between, tan, smooth),
         [(rows, cols), (rows, cols)],
         [(7,) + spare, (2,) + wide],
         300 * work,

time: 44.7 us -> 42.6 us (0.953)
  waiting for transfers between devices: 22.6 us -> 2.58 us
  starting transfers between devices: 12 us -> 30 us
    ppermute x12, waiting for transfers between devices: 22.6 us -> 2.58 us  [swap(): lax.ppermute(value, 'cross', [(i, other(i) if 0 <= other(i) < count else...]
    ppermute x12, starting transfers between devices: 12 us -> 30 us  [swap(): lax.ppermute(value, 'cross', [(i, other(i) if 0 <= other(i) < count else...]
where the time goes in v5:
time: 42.6 us; the launch traced here: 42.4 us
  starting transfers between devices  30 us (70%)
  Pallas kernels  8.63 us (20%)
  waiting for transfers between devices  2.58 us (6%)
  between operations  0.81 us (2%)
    ppermute x12, starting transfers between devices, swap(): lax.ppermute(value, 'cross', [(i, other(i) if 0 <= other(i) < count else...  30 us
    pallas_call x8, Pallas kernels, call(): pl.pallas_call(body, name=name, out_shape=outs, in_specs=spaces or [VMEM]...  8.63 us
    ppermute x12, waiting for transfers between devices, swap(): lax.ppermute(value, 'cross', [(i, other(i) if 0 <= other(i) < count else...  2.58 us
  transfers between devices with their start and end apart: 12, of which 4 were waited for; matrix products, arithmetic and copies ran while one was open for 0% of the time, Pallas kernels for 7%

profile of v5, /device:TPU:0, one launch (start us, length us, event | category | flops | bytes accessed | tf_op | source)
XLA Modules:
  0.0 42.4 jit_solution(1976484214805109890)
XLA Ops:
  0.6 2.0 %prepare.1 = (f32[8,2,144,128]{3,2,1,0:T(8,128)S(1)}, f32[1,2,144,128]{3,2,1,0:T(8,128)S(1)}, f32[9,2,8,128]{3,2,1,0:T(8,128)S(1)}, f32[9,2,8,128]{3,2,1,0:T(8,1...) custom-call(f32[3,256,128]{2,1,0:T(8,128)} %refs_0_.1, f32[256,128]{1,0:T(8,128)} %refs_1_.1, f32[256,128]{1,0:T(8,128)} %refs_2_.1, ...), custom_call_target="tpu_custom_call" | custom-call | flops 3276800 | bytes 2786336 | tf_op jit(solution)/shard_map/prepare/pallas_call | solution.py:526
  2.6 0.5 %collective-permute-start = (f32[1,128]{1,0:T(1,128)S(1)}, f32[1,128]{1,0:T(1,128)S(1)}, u32[]{:S(2)}, u32[]{:S(2)}) collective-permute-start(f32[1,128]{1,0:T(1,128)S(1)} %get-tuple-element.32), channel_id=1, source_target_pairs={{0,1},{1,0},{2,3},{3,2},{4,5},{5,4},{6,7},{7,6},{8,9},{9,8},{10,11... | collective-permute-start | bytes 1544 | tf_op jit(solution)/shard_map/ppermute | solution.py:541
  3.2 0.8 %collective-permute-done = f32[1,128]{1,0:T(1,128)S(1)} collective-permute-done((f32[1,128]{1,0:T(1,128)S(1)}, f32[1,128]{1,0:T(1,128)S(1)}, u32[]{:S(2)}, u32[]{:S(2)}) %collective-permute-start) | collective-permute-done | bytes 544 | tf_op jit(solution)/shard_map/ppermute | solution.py:541
  4.0 0.6 %collective-permute-start.1 = (f32[1,128]{1,0:T(1,128)S(1)}, f32[1,128]{1,0:T(1,128)S(1)}, u32[]{:S(2)}, u32[]{:S(2)}) collective-permute-start(f32[1,128]{1,0:T(1,128)S(1)} %max.24), channel_id=1, source_target_pairs={{0,0},{1,3},{2,2},{3,1},{4,4},{5,7},{6,6},{7,5},{8,8},{9,11},{10,1... | collective-permute-start | bytes 1544 | tf_op jit(solution)/shard_map/ppermute | solution.py:541
  4.6 4.1 %collective-permute-start.4 = (f32[9,2,8,128]{3,2,1,0:T(8,128)S(1)}, f32[9,2,8,128]{3,2,1,0:T(8,128)S(1)}, u32[]{:S(2)}, u32[]{:S(2)}) collective-permute-start(f32[9,2,8,128]{3,2,1,0:T(8,128)S(1)} %get-tuple-element.37), channel_id=1, source_target_pairs={{0,1},{1,0},{2,3},{3,2},{4,5},{5,4},{6,7},{7,6},{8,9},{9,8},{10,11... | collective-permute-start | bytes 221192 | tf_op jit(solution)/shard_map/ppermute | solution.py:541
  8.7 0.0 collective-permute-done.1
  8.7 0.7 %collective-permute-start.5 = (f32[9,2,8,128]{3,2,1,0:T(8,128)S(1)}, f32[9,2,8,128]{3,2,1,0:T(8,128)S(1)}, u32[]{:S(2)}, u32[]{:S(2)}) collective-permute-start(f32[9,2,8,128]{3,2,1,0:T(8,128)S(1)} %get-tuple-element.38), channel_id=1, source_target_pairs={{0,0},{1,2},{2,1},{3,4},{4,3},{5,6},{6,5},{7,8},{8,7},{9,10},{10,9... | collective-permute-start | bytes 221192 | tf_op jit(solution)/shard_map/ppermute | solution.py:541
  9.4 0.7 %collective-permute-start.2 = (f32[1,128]{1,0:T(1,128)S(1)}, f32[1,128]{1,0:T(1,128)S(1)}, u32[]{:S(2)}, u32[]{:S(2)}) collective-permute-start(f32[1,128]{1,0:T(1,128)S(1)} %max.25), channel_id=1, source_target_pairs={{0,0},{1,5},{2,2},{3,7},{4,4},{5,1},{6,6},{7,3},{8,8},{9,13},{10,1... | collective-permute-start | bytes 1544 | tf_op jit(solution)/shard_map/ppermute | solution.py:541
  10.0 0.0 collective-permute-done.2
  10.1 0.7 %collective-permute-start.3 = (f32[1,128]{1,0:T(1,128)S(1)}, f32[1,128]{1,0:T(1,128)S(1)}, u32[]{:S(2)}, u32[]{:S(2)}) collective-permute-start(f32[1,128]{1,0:T(1,128)S(1)} %max.26), channel_id=1, source_target_pairs={{0,0},{1,9},{2,2},{3,11},{4,4},{5,13},{6,6},{7,15},{8,8},{9,1},{10... | collective-permute-start | bytes 1544 | tf_op jit(solution)/shard_map/ppermute | solution.py:541
  10.7 0.0 collective-permute-done.4.edge_a
  10.7 0.9 %open_step.1 = (f32[8,2,144,128]{3,2,1,0:T(8,128)S(1)}, f32[1,2,144,128]{3,2,1,0:T(8,128)S(1)}, f32[6,2,144,128]{3,2,1,0:T(8,128)S(1)}, f32[2,2,144,128]{3,2,1,0:T(8,128)S(1)}) custom-call(f32[8,2,144,128]{3,2,1,0:T(8,128)S(1)} %get-tuple-element.35.kept_in, ...), custom_call_target="tpu_custom_call", output_to_operand_aliasing={{0}: (0, {}), {1}: (1, {})} | custom-call | flops 3276800 | bytes 3981312 | tf_op jit(solution)/shard_map/open_step/pallas_call | solution.py:526
  11.7 9.5 %collective-permute-start.6 = (f32[1,128]{1,0:T(1,128)S(1)}, f32[1,128]{1,0:T(1,128)S(1)}, u32[]{:S(2)}, u32[]{:S(2)}) collective-permute-start(f32[1,128]{1,0:T(1,128)S(1)} %max.27.top), channel_id=1, source_target_pairs={{0,1},{1,0},{2,3},{3,2},{4,5},{5,4},{6,7},{7,6},{8,9},{9,8},{10,11... | collective-permute-start | bytes 1544 | tf_op jit(solution)/shard_map/ppermute | solution.py:541
  21.2 0.8 %collective-permute-done.6.last = f32[1,128]{1,0:T(1,128)S(1)} collective-permute-done((f32[1,128]{1,0:T(1,128)S(1)}, f32[1,128]{1,0:T(1,128)S(1)}, u32[]{:S(2)}, u32[]{:S(2)}) %collective-permute-start.6) | collective-permute-done | bytes 544 | tf_op jit(solution)/shard_map/ppermute | solution.py:541
  22.0 0.9 %middle.1 = (f32[6,2,144,128]{3,2,1,0:T(8,128)S(1)}, f32[3,2,144,128]{3,2,1,0:T(8,128)S(1)}, f32[2,128]{1,0:T(2,128)S(1)}) custom-call(f32[1,128]{1,0:T(1,128)S(1)} %max.27.top, f32[1,128]{1,0:T(1,128)S(1)} %collective-permute-done.6.last, f32[8,2,144,128]{3,2,1,0:T(8,128)S(1)} %get-tuple-element.41.kept, f32[6,2,144,128]{3,2,1,0:T(8,128)S(1)} %get-tuple-element.42.xy, ...), custom_call_target="tpu_custom_call" | custom-call | flops 3932160 | bytes 3394048 | tf_op jit(solution)/shard_map/middle/pallas_call | solution.py:526
  23.0 0.4 collective-permute-start.7
  23.3 0.7 %regularize.1.smooth = f32[2,2,128,128]{3,2,1,0:T(8,128)S(1)} custom-call(f32[8,2,144,128]{3,2,1,0:T(8,128)S(1)} %get-tuple-element.41.kept, f32[1,2,144,128]{3,2,1,0:T(8,128)S(1)} %get-tuple-element.45.weights), custom_call_target="tpu_custom_call" | custom-call | flops 983040 | bytes 1589248 | tf_op jit(solution)/shard_map/regularize/pallas_call | solution.py:526
  24.1 0.1 collective-permute-done.7
  24.2 0.1 add_select_fusion.3
  24.2 0.7 %collective-permute-start.8 = (f32[2,128]{1,0:T(2,128)S(1)}, f32[2,128]{1,0:T(2,128)S(1)}, u32[]{:S(2)}, u32[]{:S(2)}) collective-permute-start(f32[2,128]{1,0:T(2,128)S(1)} %add_select_fusion.3), channel_id=1, source_target_pairs={{0,0},{1,3},{2,2},{3,1},{4,4},{5,7},{6,6},{7,5},{8,8},{9,11},{10,1... | collective-permute-start | bytes 3080 | tf_op jit(solution)/shard_map/ppermute | solution.py:541
  24.9 0.5 %tangent_one.1 = (f32[4,2,160,128]{3,2,1,0:T(8,128)S(1)}, f32[3,2,144,128]{3,2,1,0:T(8,128)S(1)}) custom-call(f32[1,128]{1,0:T(1,128)S(1)} %max.27.top, f32[1,128]{1,0:T(1,128)S(1)} %collective-permute-done.6.last, f32[8,2,144,128]{3,2,1,0:T(8,128)S(1)} %get-tuple-element.41.kept, f32[2,2,144,128]{3,2,1,0:T(8,128)S(1)} %get-tuple-element.47.change, ...), custom_call_target="tpu_custom_call" | custom-call | flops 1966080 | bytes 3458048 | tf_op jit(solution)/shard_map/tangent_one/pallas_call | solution.py:526
  25.4 0.1 add_select_fusion.2
  25.5 0.7 %collective-permute-start.9 = (f32[2,128]{1,0:T(2,128)S(1)}, f32[2,128]{1,0:T(2,128)S(1)}, u32[]{:S(2)}, u32[]{:S(2)}) collective-permute-start(f32[2,128]{1,0:T(2,128)S(1)} %add_select_fusion.2), channel_id=1, source_target_pairs={{0,0},{1,5},{2,2},{3,7},{4,4},{5,1},{6,6},{7,3},{8,8},{9,13},{10,1... | collective-permute-start | bytes 3080 | tf_op jit(solution)/shard_map/ppermute | solution.py:541
  26.1 0.7 %tangent_mid.1 = (f32[6,2,144,128]{3,2,1,0:T(8,128)S(1)}, f32[9,2,144,128]{3,2,1,0:T(8,128)S(1)}, f32[5,2,160,128]{3,2,1,0:T(8,128)S(1)}) custom-call(f32[1,128]{1,0:T(1,128)S(1)} %max.27.top, f32[1,128]{1,0:T(1,128)S(1)} %collective-permute-done.6.last, f32[8,2,144,128]{3,2,1,0:T(8,128)S(1)} %get-tuple-element.41.kept, ...), custom_call_target="tpu_custom_call" | custom-call | flops 3932160 | bytes 5751808 | tf_op jit(solution)/shard_map/tangent_mid/pallas_call | solution.py:526
  26.8 0.0 collective-permute-done.9
  26.9 0.1 add_select_fusion.1
  26.9 0.7 %collective-permute-start.10 = (f32[2,128]{1,0:T(2,128)S(1)}, f32[2,128]{1,0:T(2,128)S(1)}, u32[]{:S(2)}, u32[]{:S(2)}) collective-permute-start(f32[2,128]{1,0:T(2,128)S(1)} %add_select_fusion.1), channel_id=1, source_target_pairs={{0,0},{1,9},{2,2},{3,11},{4,4},{5,13},{6,6},{7,15},{8,8},{9,1},{10... | collective-permute-start | bytes 3080 | tf_op jit(solution)/shard_map/ppermute | solution.py:541
  27.6 0.3 tangent_end.1.tan
  27.9 0.1 add_select_fusion.fast
  27.9 11.0 %collective-permute-start.11 = (f32[2,128]{1,0:T(2,128)S(1)}, f32[2,128]{1,0:T(2,128)S(1)}, u32[]{:S(2)}, u32[]{:S(2)}) collective-permute-start(f32[2,128]{1,0:T(2,128)S(1)} %add_select_fusion.fast), channel_id=1, source_target_pairs={{0,1},{1,0},{2,3},{3,2},{4,5},{5,4},{6,7},{7,6},{8,9},{9,8},{10,11... | collective-permute-start | bytes 3080 | tf_op jit(solution)/shard_map/ppermute | solution.py:541
  38.9 0.8 %collective-permute-done.11.fast_last = f32[2,128]{1,0:T(2,128)S(1)} collective-permute-done((f32[2,128]{1,0:T(2,128)S(1)}, f32[2,128]{1,0:T(2,128)S(1)}, u32[]{:S(2)}, u32[]{:S(2)}) %collective-permute-start.11) | collective-permute-done | bytes 1056 | tf_op jit(solution)/shard_map/ppermute | solution.py:541
  39.7 2.6 %finish.1 = (f32[256,128]{1,0:T(8,128)}, f32[256,128]{1,0:T(8,128)}) custom-call(f32[1,128]{1,0:T(1,128)S(1)} %max.27.top, f32[1,128]{1,0:T(1,128)S(1)} %collective-permute-done.6.last, f32[2,128]{1,0:T(2,128)S(1)} %add_select_fusion.fast, f32[2,128]{1,0:T(2,128)S(1)} %collective-permute-done.11.fast_last, f32[8,2,144,128]{3,2,1,0:T(8,128)S(1)} %get-tuple-element.41.kept, ...), custom_call_target="tpu_custom_call" | custom-call | flops 9830400 | bytes 5721088 | tf_op jit(solution)/shard_map/finish/pallas_call | solution.py:526
  (9 shorter events, 0.0 us)
Async XLA Ops:
  2.6 1.3 %collective-permute-start = (f32[1,128]{1,0:T(1,128)S(1)}, f32[1,128]{1,0:T(1,128)S(1)}, u32[]{:S(2)}, u32[]{:S(2)}) collective-permute-start(f32[1,128]{1,0:T(1,128)S(1)} %get-tuple-element.32), channel_id=1, source_target_pairs={{0,1},{1,0},{2,3},{3,2},{4,5},{5,4},{6,7},{7,6},{8,9},{9,8},{10,11... | collective-permute-start | bytes 1544 | tf_op jit(solution)/shard_map/ppermute | solution.py:541
  4.0 4.7 %collective-permute-start.1 = (f32[1,128]{1,0:T(1,128)S(1)}, f32[1,128]{1,0:T(1,128)S(1)}, u32[]{:S(2)}, u32[]{:S(2)}) collective-permute-start(f32[1,128]{1,0:T(1,128)S(1)} %max.24), channel_id=1, source_target_pairs={{0,0},{1,3},{2,2},{3,1},{4,4},{5,7},{6,6},{7,5},{8,8},{9,11},{10,1... | collective-permute-start | bytes 1544 | tf_op jit(solution)/shard_map/ppermute | solution.py:541
  4.6 6.1 %collective-permute-start.4 = (f32[9,2,8,128]{3,2,1,0:T(8,128)S(1)}, f32[9,2,8,128]{3,2,1,0:T(8,128)S(1)}, u32[]{:S(2)}, u32[]{:S(2)}) collective-permute-start(f32[9,2,8,128]{3,2,1,0:T(8,128)S(1)} %get-tuple-element.37), channel_id=1, source_target_pairs={{0,1},{1,0},{2,3},{3,2},{4,5},{5,4},{6,7},{7,6},{8,9},{9,8},{10,11... | collective-permute-start | bytes 221192 | tf_op jit(solution)/shard_map/ppermute | solution.py:541
  8.7 2.0 %collective-permute-start.5 = (f32[9,2,8,128]{3,2,1,0:T(8,128)S(1)}, f32[9,2,8,128]{3,2,1,0:T(8,128)S(1)}, u32[]{:S(2)}, u32[]{:S(2)}) collective-permute-start(f32[9,2,8,128]{3,2,1,0:T(8,128)S(1)} %get-tuple-element.38), channel_id=1, source_target_pairs={{0,0},{1,2},{2,1},{3,4},{4,3},{5,6},{6,5},{7,8},{8,7},{9,10},{10,9... | collective-permute-start | bytes 221192 | tf_op jit(solution)/shard_map/ppermute | solution.py:541
  9.4 0.7 %collective-permute-start.2 = (f32[1,128]{1,0:T(1,128)S(1)}, f32[1,128]{1,0:T(1,128)S(1)}, u32[]{:S(2)}, u32[]{:S(2)}) collective-permute-start(f32[1,128]{1,0:T(1,128)S(1)} %max.25), channel_id=1, source_target_pairs={{0,0},{1,5},{2,2},{3,7},{4,4},{5,1},{6,6},{7,3},{8,8},{9,13},{10,1... | collective-permute-start | bytes 1544 | tf_op jit(solution)/shard_map/ppermute | solution.py:541
  10.1 1.6 %collective-permute-start.3 = (f32[1,128]{1,0:T(1,128)S(1)}, f32[1,128]{1,0:T(1,128)S(1)}, u32[]{:S(2)}, u32[]{:S(2)}) collective-permute-start(f32[1,128]{1,0:T(1,128)S(1)} %max.26), channel_id=1, source_target_pairs={{0,0},{1,9},{2,2},{3,11},{4,4},{5,13},{6,6},{7,15},{8,8},{9,1},{10... | collective-permute-start | bytes 1544 | tf_op jit(solution)/shard_map/ppermute | solution.py:541
  11.7 10.3 %collective-permute-start.6 = (f32[1,128]{1,0:T(1,128)S(1)}, f32[1,128]{1,0:T(1,128)S(1)}, u32[]{:S(2)}, u32[]{:S(2)}) collective-permute-start(f32[1,128]{1,0:T(1,128)S(1)} %max.27.top), channel_id=1, source_target_pairs={{0,1},{1,0},{2,3},{3,2},{4,5},{5,4},{6,7},{7,6},{8,9},{9,8},{10,11... | collective-permute-start | bytes 1544 | tf_op jit(solution)/shard_map/ppermute | solution.py:541
  23.0 1.2 %collective-permute-start.7 = (f32[2,128]{1,0:T(2,128)S(1)}, f32[2,128]{1,0:T(2,128)S(1)}, u32[]{:S(2)}, u32[]{:S(2)}) collective-permute-start(f32[2,128]{1,0:T(2,128)S(1)} %get-tuple-element.44), channel_id=1, source_target_pairs={{0,1},{1,0},{2,3},{3,2},{4,5},{5,4},{6,7},{7,6},{8,9},{9,8},{10,11... | collective-permute-start | bytes 3080 | tf_op jit(solution)/shard_map/ppermute | solution.py:541
  24.2 1.2 %collective-permute-start.8 = (f32[2,128]{1,0:T(2,128)S(1)}, f32[2,128]{1,0:T(2,128)S(1)}, u32[]{:S(2)}, u32[]{:S(2)}) collective-permute-start(f32[2,128]{1,0:T(2,128)S(1)} %add_select_fusion.3), channel_id=1, source_target_pairs={{0,0},{1,3},{2,2},{3,1},{4,4},{5,7},{6,6},{7,5},{8,8},{9,11},{10,1... | collective-permute-start | bytes 3080 | tf_op jit(solution)/shard_map/ppermute | solution.py:541
  25.5 1.4 %collective-permute-start.9 = (f32[2,128]{1,0:T(2,128)S(1)}, f32[2,128]{1,0:T(2,128)S(1)}, u32[]{:S(2)}, u32[]{:S(2)}) collective-permute-start(f32[2,128]{1,0:T(2,128)S(1)} %add_select_fusion.2), channel_id=1, source_target_pairs={{0,0},{1,5},{2,2},{3,7},{4,4},{5,1},{6,6},{7,3},{8,8},{9,13},{10,1... | collective-permute-start | bytes 3080 | tf_op jit(solution)/shard_map/ppermute | solution.py:541
  26.9 0.9 %collective-permute-start.10 = (f32[2,128]{1,0:T(2,128)S(1)}, f32[2,128]{1,0:T(2,128)S(1)}, u32[]{:S(2)}, u32[]{:S(2)}) collective-permute-start(f32[2,128]{1,0:T(2,128)S(1)} %add_select_fusion.1), channel_id=1, source_target_pairs={{0,0},{1,9},{2,2},{3,11},{4,4},{5,13},{6,6},{7,15},{8,8},{9,1},{10... | collective-permute-start | bytes 3080 | tf_op jit(solution)/shard_map/ppermute | solution.py:541
  27.9 11.8 %collective-permute-start.11 = (f32[2,128]{1,0:T(2,128)S(1)}, f32[2,128]{1,0:T(2,128)S(1)}, u32[]{:S(2)}, u32[]{:S(2)}) collective-permute-start(f32[2,128]{1,0:T(2,128)S(1)} %add_select_fusion.fast), channel_id=1, source_target_pairs={{0,1},{1,0},{2,3},{3,2},{4,5},{5,4},{6,7},{7,6},{8,9},{9,8},{10,11... | collective-permute-start | bytes 3080 | tf_op jit(solution)/shard_map/ppermute | solution.py:541

commit v6 on v5

--- a/solution.py
+++ b/solution.py
@@ -103,17 +103,29 @@
     return inv_speed, dry * height * inv_speed, turbulent * (squared * inv_speed)
 
 
-def known(row, last, k):
-    return jnp.where(lax.rem(lax.axis_index("cross"), 2) == 0, last[k : k + 1, :], row[k : k + 1, :])
-
-
 def step_length(row, last, shape):
-    return COURANT / jnp.broadcast_to(known(row, last, 0), shape)
+    return COURANT / jnp.broadcast_to(jnp.maximum(row[:1, :], last[:1, :]), shape)
+
+
+def first_speed(state, row, held, arrived):
+    rows, cols = state.shape[1:]
+    parts = held.shape[0]
+    size = rows // parts
+    copies = []
+    for i in range(parts):
+        copies.append(pltpu.make_async_copy(state.at[:, pl.ds(i * size, size), :], held.at[i], arrived.at[i]))
+        copies[i].start()
+    top = jnp.zeros((16, cols), jnp.float32)
+    for i in range(parts):
+        copies[i].wait()
+        for j in range(0, size, 16):
+            top = jnp.maximum(top, speed_of(*(held[i, k, j : j + 16, :] for k in range(3))))
+    row[...] = jnp.full(row.shape, jnp.max(top), jnp.float32)
 
 
 def prepare(*refs):
     sources = refs[:9]
-    kept, weights, edge_a, edge_b, row, count_row, code, turned = refs[9:17]
+    kept, weights, edge_a, edge_b, count_row, code, turned = refs[10:17]
     held, arrived = refs[17:26], refs[26]
     copies = [pltpu.make_async_copy(src, dst, arrived.at[i]) for i, (src, dst) in enumerate(zip(sources, held))]
     for i in (0, 6, 5, 7, 3, 4, 1, 2, 8):
@@ -124,10 +136,6 @@
     own = pl.ds(TILE, cols)
 
     copies[0].wait()
-    top = jnp.zeros((16, cols), jnp.float32)
-    for i in range(0, rows, 16):
-        top = jnp.maximum(top, speed_of(*(state[k, i : i + 16, :] for k in range(3))))
-    row[...] = jnp.full(row.shape, jnp.max(top), jnp.float32)
     for g in range(groups):
         for k in range(3):
             kept[k, g, own, :] = state[k, pl.ds(g * LANES, LANES), :].T
@@ -416,7 +424,7 @@
     shape = grid.lane.shape
     dt0 = step_length(top, last, shape)
     dt1 = step_length(fast, fast_last, shape)
-    weight = jnp.broadcast_to((DATA_WEIGHT * cells) / known(fast, fast_last, 1), shape)
+    weight = jnp.broadcast_to((DATA_WEIGHT * cells) / (fast[1:2, :] + fast_last[1:2, :]), shape)
     half1 = 0.5 * dt1
     half0 = 0.5 * dt0
 
@@ -538,7 +546,7 @@
 
 def swap(value, other):
     count = lax.axis_size("cross")
-    return lax.ppermute(value, "cross", [(i, other(i) if 0 <= other(i) < count else i) for i in range(count)])
+    return lax.ppermute(value, "cross", [(i, other(i) % count) for i in range(count)])
 
 
 def other_core(i):
@@ -549,8 +557,8 @@
     return i - 1 if i % 2 == 0 else i + 1
 
 
-def odd_far(step):
-    return lambda i: i ^ step if i % 2 == 1 else i
+def other_chip(step):
+    return lambda i: i ^ (step + 1)
 
 
 def max_and_sum(a, b):
@@ -576,25 +584,34 @@
 
     inputs = (state, log_mu, log_xi, dir_mu, dir_xi, wet, observed, terrain, class_weight)
     inputs = tuple(pltpu.with_memory_space_constraint(x, pltpu.HBM) for x in inputs)
-    kept, weights, edge_a, edge_b, row, count_row = call(
+    (row,) = call(
+        first_speed,
+        "first_speed",
+        inputs[:1],
+        [(1, LANES)],
+        [pltpu.VMEM((4, 3, rows // 4, cols), jnp.float32), pltpu.SemaphoreType.DMA((4,))],
+        20 * work,
+        spaces=[ANY],
+    )
+    row = jnp.maximum(row, swap(row, other_core))
+    kept, weights, edge_a, edge_b, count_row = call(
         prepare,
         "prepare",
-        inputs,
-        [(KEPT,) + wide, (1,) + wide, edge, edge, (1, LANES), (1, LANES)],
+        inputs + (row,),
+        [(KEPT,) + wide, (1,) + wide, edge, edge, (1, LANES)],
         [(rows, cols), (3,) + own]
         + [pltpu.VMEM(x.shape, x.dtype) for x in inputs[:-1]]
         + [pltpu.SMEM(class_weight.shape, jnp.float32), pltpu.SemaphoreType.DMA((len(inputs),))],
         100 * work,
-        spaces=[ANY] * len(inputs),
+        spaces=[ANY] * len(inputs) + [VMEM],
     )
     steps = [2**k for k in range(1, count.bit_length() - 1)]
     edge_a = swap(edge_a, other_core)
-    row = jnp.maximum(row, swap(row, other_core))
-    for step in steps[:-1]:
-        row = jnp.maximum(row, swap(row, odd_far(step)))
-        if step == 2:
-            row, edge_b = lax.optimization_barrier((row, edge_b))
-            edge_b = swap(edge_b, next_chip)
+    row = jnp.maximum(row, swap(row, other_chip(steps[0])))
+    row, edge_b = lax.optimization_barrier((row, edge_b))
+    edge_b = swap(edge_b, next_chip)
+    for step in steps[1:-1]:
+        row = jnp.maximum(row, swap(row, other_chip(step)))
     kept, weights, xy, change = call(
         open_step,
         "open_step",
@@ -604,9 +621,7 @@
         100 * work,
         aliases={0: 0, 1: 1},
     )
-    arrived, xy = lax.optimization_barrier((swap(row, odd_far(steps[-1])), xy))
-    top = jnp.maximum(row, arrived)
-    last = swap(top, other_core)
+    top, last = row, swap(row, other_chip(steps[-1]))
     at_one, mid, row = call(
         middle,
         "middle",
@@ -620,7 +635,7 @@
     one, part = call(
         tangent_one, "tangent_one", (top, last, kept, change, at_one), [(4,) + spare, (3,) + wide], [], 60 * work
     )
-    row, one = round_beside(row, odd_far(steps[0]), one)
+    row, one = round_beside(row, other_chip(steps[0]), one)
     part, at_mid, between = call(
         tangent_mid,
         "tangent_mid",
@@ -629,15 +644,14 @@
         [],
         120 * work,
     )
-    row, part = round_beside(row, odd_far(steps[1]), part)
+    row, part = round_beside(row, other_chip(steps[1]), part)
+    for step in steps[2:-1]:
+        row, _ = round_beside(row, other_chip(step))
     (tan,) = call(tangent_end, "tangent_end", (part, between), [(6,) + spare], [], 30 * work)
-    row, tan = round_beside(row, odd_far(steps[2]), tan)
-    for step in steps[3:]:
-        row, _ = round_beside(row, odd_far(step))
     return call(
         functools.partial(finish, float(rows * cols * count)),
         "finish",
-        (top, last, row, swap(row, other_core), kept, at_one, at_mid, between, tan, smooth),
+        (top, last, row, swap(row, other_chip(steps[-1])), kept, at_one, at_mid, between, tan, smooth),
         [(rows, cols), (rows, cols)],
         [(7,) + spare, (2,) + wide],
         300 * work,

time: 42.6 us -> 33.7 us (0.79)
  starting transfers between devices: 30 us -> 8.3 us
  waiting for transfers between devices: 2.58 us -> 14.6 us
  Pallas kernels: 8.63 us -> 9.67 us
    ppermute x12 -> x10, starting transfers between devices: 30 us -> 8.3 us  [swap(): lax.ppermute(value, 'cross', [(i, other(i) % count) for i in range(count)])]
    ppermute x12 -> x10, waiting for transfers between devices: 2.58 us -> 14.6 us  [swap(): lax.ppermute(value, 'cross', [(i, other(i) % count) for i in range(count)])]
    pallas_call x8 -> x9, Pallas kernels: 8.63 us -> 9.67 us  [call(): pl.pallas_call(body, name=name, out_shape=outs, in_specs=spaces or [VMEM]...]
  transfers between devices with their start and end apart: 12 -> 10, of which waited for: 4 -> 7; matrix products, arithmetic and copies ran while one was open for 0% -> 0% of each run, Pallas kernels for 7% -> 15%
where the time goes in v6:
time: 33.7 us; the launch traced here: 33.5 us
  waiting for transfers between devices  14.6 us (43%)
  Pallas kernels  9.67 us (29%)
  starting transfers between devices  8.3 us (25%)
  between operations  0.71 us (2%)
    ppermute x10, waiting for transfers between devices, swap(): lax.ppermute(value, 'cross', [(i, other(i) % count) for i in range(count)])  14.6 us
    pallas_call x9, Pallas kernels, call(): pl.pallas_call(body, name=name, out_shape=outs, in_specs=spaces or [VMEM]...  9.67 us
    ppermute x10, starting transfers between devices, swap(): lax.ppermute(value, 'cross', [(i, other(i) % count) for i in range(count)])  8.3 us
  transfers between devices with their start and end apart: 10, of which 7 were waited for; matrix products, arithmetic and copies ran while one was open for 0% of the time, Pallas kernels for 15%

profile of v6, /device:TPU:0, one launch (start us, length us, event | category | flops | bytes accessed | tf_op | source)
XLA Modules:
  0.0 33.5 jit_solution(2495385525560309956)
XLA Ops:
  0.6 1.2 %first_speed.1 = f32[1,128]{1,0:T(1,128)S(1)} custom-call(f32[3,256,128]{2,1,0:T(8,128)} %refs_0_.1), custom_call_target="tpu_custom_call" | custom-call | flops 655360 | bytes 393728 | tf_op jit(solution)/shard_map/first_speed/pallas_call | solution.py:534
  1.9 0.5 %collective-permute-start = (f32[1,128]{1,0:T(1,128)S(1)}, f32[1,128]{1,0:T(1,128)S(1)}, u32[]{:S(2)}, u32[]{:S(2)}) collective-permute-start(f32[1,128]{1,0:T(1,128)S(1)} %first_speed.1), channel_id=1, source_target_pairs={{0,1},{1,0},{2,3},{3,2},{4,5},{5,4},{6,7},{7,6},{8,9},{9,8},{10,11... | collective-permute-start | bytes 1544 | tf_op jit(solution)/shard_map/ppermute | solution.py:549
  2.4 0.8 %collective-permute-done = f32[1,128]{1,0:T(1,128)S(1)} collective-permute-done((f32[1,128]{1,0:T(1,128)S(1)}, f32[1,128]{1,0:T(1,128)S(1)}, u32[]{:S(2)}, u32[]{:S(2)}) %collective-permute-start) | collective-permute-done | bytes 544 | tf_op jit(solution)/shard_map/ppermute | solution.py:549
  3.2 2.6 %collective-permute-start.1 = (f32[1,128]{1,0:T(1,128)S(1)}, f32[1,128]{1,0:T(1,128)S(1)}, u32[]{:S(2)}, u32[]{:S(2)}) collective-permute-start(f32[1,128]{1,0:T(1,128)S(1)} %max.18.refs_9_), channel_id=1, source_target_pairs={{0,3},{1,2},{2,1},{3,0},{4,7},{5,6},{6,5},{7,4},{8,11},{9,10},{10,... | collective-permute-start | bytes 1544 | tf_op jit(solution)/shard_map/ppermute | solution.py:549
  5.8 1.8 %prepare.1 = (f32[8,2,144,128]{3,2,1,0:T(8,128)S(1)}, f32[1,2,144,128]{3,2,1,0:T(8,128)S(1)}, f32[9,2,8,128]{3,2,1,0:T(8,128)S(1)}, f32[9,2,8,128]{3,2,1,0:T(8,128)S(1)}, f32[1,128]{1,0:T(1,128)S(1)}) custom-call(f32[3,256,128]{2,1,0:T(8,128)} %refs_0_.1, f32[256,128]{1,0:T(8,128)} %refs_1_.1, f32[256,128]{1,0:T(8,128)} %refs_2_.1, f32[256,128]{1,0:T(8,128)} %refs_3_.1, ...), custom_call_target="tpu_custom_call" | custom-call | flops 3276800 | bytes 2786336 | tf_op jit(solution)/shard_map/prepare/pallas_call | solution.py:534
  7.7 0.4 %collective-permute-start.4 = (f32[9,2,8,128]{3,2,1,0:T(8,128)S(1)}, f32[9,2,8,128]{3,2,1,0:T(8,128)S(1)}, u32[]{:S(2)}, u32[]{:S(2)}) collective-permute-start(f32[9,2,8,128]{3,2,1,0:T(8,128)S(1)} %get-tuple-element.31), channel_id=1, source_target_pairs={{0,1},{1,0},{2,3},{3,2},{4,5},{5,4},{6,7},{7,6},{8,9},{9,8},{10,11... | collective-permute-start | bytes 221192 | tf_op jit(solution)/shard_map/ppermute | solution.py:549
  8.1 0.0 collective-permute-done.1
  8.1 3.8 %collective-permute-start.5 = (f32[9,2,8,128]{3,2,1,0:T(8,128)S(1)}, f32[9,2,8,128]{3,2,1,0:T(8,128)S(1)}, u32[]{:S(2)}, u32[]{:S(2)}) collective-permute-start(f32[9,2,8,128]{3,2,1,0:T(8,128)S(1)} %get-tuple-element.32), channel_id=1, source_target_pairs={{0,15},{1,2},{2,1},{3,4},{4,3},{5,6},{6,5},{7,8},{8,7},{9,10},{10,... | collective-permute-start | bytes 221192 | tf_op jit(solution)/shard_map/ppermute | solution.py:549
  11.8 0.0 collective-permute-start.2
  11.8 3.0 %collective-permute-done.2 = f32[1,128]{1,0:T(1,128)S(1)} collective-permute-done((f32[1,128]{1,0:T(1,128)S(1)}, f32[1,128]{1,0:T(1,128)S(1)}, u32[]{:S(2)}, u32[]{:S(2)}) %collective-permute-start.2) | collective-permute-done | bytes 544 | tf_op jit(solution)/shard_map/ppermute | solution.py:549
  14.8 0.1 collective-permute-start.3
  14.9 0.0 collective-permute-done.4.edge_a
  14.9 0.0 collective-permute-done.5.edge_b
  14.9 0.9 %open_step.1 = (f32[8,2,144,128]{3,2,1,0:T(8,128)S(1)}, f32[1,2,144,128]{3,2,1,0:T(8,128)S(1)}, f32[6,2,144,128]{3,2,1,0:T(8,128)S(1)}, f32[2,2,144,128]{3,2,1,0:T(8,128)S(1)}) custom-call(f32[8,2,144,128]{3,2,1,0:T(8,128)S(1)} %get-tuple-element.29.kept_in, ...), custom_call_target="tpu_custom_call", output_to_operand_aliasing={{0}: (0, {}), {1}: (1, {})} | custom-call | flops 3276800 | bytes 3981312 | tf_op jit(solution)/shard_map/open_step/pallas_call | solution.py:534
  15.8 2.9 %collective-permute-done.3.last = f32[1,128]{1,0:T(1,128)S(1)} collective-permute-done((f32[1,128]{1,0:T(1,128)S(1)}, f32[1,128]{1,0:T(1,128)S(1)}, u32[]{:S(2)}, u32[]{:S(2)}) %collective-permute-start.3) | collective-permute-done | bytes 544 | tf_op jit(solution)/shard_map/ppermute | solution.py:549
  18.7 0.9 %middle.1 = (f32[6,2,144,128]{3,2,1,0:T(8,128)S(1)}, f32[3,2,144,128]{3,2,1,0:T(8,128)S(1)}, f32[2,128]{1,0:T(2,128)S(1)}) custom-call(f32[1,128]{1,0:T(1,128)S(1)} %max.20.top, f32[1,128]{1,0:T(1,128)S(1)} %collective-permute-done.3.last, f32[8,2,144,128]{3,2,1,0:T(8,128)S(1)} %get-tuple-element.33.kept, f32[6,2,144,128]{3,2,1,0:T(8,128)S(1)} %get-tuple-element.34.xy, ...), custom_call_target="tpu_custom_call" | custom-call | flops 3932160 | bytes 3394048 | tf_op jit(solution)/shard_map/middle/pallas_call | solution.py:534
  19.6 0.1 collective-permute-start.6
  19.7 0.7 %regularize.1.smooth = f32[2,2,128,128]{3,2,1,0:T(8,128)S(1)} custom-call(f32[8,2,144,128]{3,2,1,0:T(8,128)S(1)} %get-tuple-element.33.kept, f32[1,2,144,128]{3,2,1,0:T(8,128)S(1)} %get-tuple-element.37.weights), custom_call_target="tpu_custom_call" | custom-call | flops 983040 | bytes 1589248 | tf_op jit(solution)/shard_map/regularize/pallas_call | solution.py:534
  20.4 0.4 %collective-permute-done.6 = f32[2,128]{1,0:T(2,128)S(1)} collective-permute-done((f32[2,128]{1,0:T(2,128)S(1)}, f32[2,128]{1,0:T(2,128)S(1)}, u32[]{:S(2)}, u32[]{:S(2)}) %collective-permute-start.6) | collective-permute-done | bytes 1056 | tf_op jit(solution)/shard_map/ppermute | solution.py:549
  20.8 0.1 add_select_fusion.2
  20.9 0.0 collective-permute-start.7
  20.9 0.5 %tangent_one.1 = (f32[4,2,160,128]{3,2,1,0:T(8,128)S(1)}, f32[3,2,144,128]{3,2,1,0:T(8,128)S(1)}) custom-call(f32[1,128]{1,0:T(1,128)S(1)} %max.20.top, f32[1,128]{1,0:T(1,128)S(1)} %collective-permute-done.3.last, f32[8,2,144,128]{3,2,1,0:T(8,128)S(1)} %get-tuple-element.33.kept, f32[2,2,144,128]{3,2,1,0:T(8,128)S(1)} %get-tuple-element.39.change, ...), custom_call_target="tpu_custom_call" | custom-call | flops 1966080 | bytes 3458048 | tf_op jit(solution)/shard_map/tangent_one/pallas_call | solution.py:534
  21.4 2.5 %collective-permute-done.7 = f32[2,128]{1,0:T(2,128)S(1)} collective-permute-done((f32[2,128]{1,0:T(2,128)S(1)}, f32[2,128]{1,0:T(2,128)S(1)}, u32[]{:S(2)}, u32[]{:S(2)}) %collective-permute-start.7) | collective-permute-done | bytes 1056 | tf_op jit(solution)/shard_map/ppermute | solution.py:549
  23.9 0.1 add_select_fusion.1
  23.9 0.8 %collective-permute-start.8 = (f32[2,128]{1,0:T(2,128)S(1)}, f32[2,128]{1,0:T(2,128)S(1)}, u32[]{:S(2)}, u32[]{:S(2)}) collective-permute-start(f32[2,128]{1,0:T(2,128)S(1)} %add_select_fusion.1), channel_id=1, source_target_pairs={{0,5},{1,4},{2,7},{3,6},{4,1},{5,0},{6,3},{7,2},{8,13},{9,12},{10,... | collective-permute-start | bytes 3080 | tf_op jit(solution)/shard_map/ppermute | solution.py:549
  24.7 0.7 %tangent_mid.1 = (f32[6,2,144,128]{3,2,1,0:T(8,128)S(1)}, f32[9,2,144,128]{3,2,1,0:T(8,128)S(1)}, f32[5,2,160,128]{3,2,1,0:T(8,128)S(1)}) custom-call(f32[1,128]{1,0:T(1,128)S(1)} %max.20.top, f32[1,128]{1,0:T(1,128)S(1)} %collective-permute-done.3.last, f32[8,2,144,128]{3,2,1,0:T(8,128)S(1)} %get-tuple-element.33.kept, ...), custom_call_target="tpu_custom_call" | custom-call | flops 3932160 | bytes 5751808 | tf_op jit(solution)/shard_map/tangent_mid/pallas_call | solution.py:534
  25.4 1.5 %collective-permute-done.8 = f32[2,128]{1,0:T(2,128)S(1)} collective-permute-done((f32[2,128]{1,0:T(2,128)S(1)}, f32[2,128]{1,0:T(2,128)S(1)}, u32[]{:S(2)}, u32[]{:S(2)}) %collective-permute-start.8) | collective-permute-done | bytes 1056 | tf_op jit(solution)/shard_map/ppermute | solution.py:549
  26.9 0.1 add_select_fusion.fast
  27.0 0.1 collective-permute-start.9
  27.1 0.3 tangent_end.1.tan
  27.3 3.6 %collective-permute-done.9.fast_last = f32[2,128]{1,0:T(2,128)S(1)} collective-permute-done((f32[2,128]{1,0:T(2,128)S(1)}, f32[2,128]{1,0:T(2,128)S(1)}, u32[]{:S(2)}, u32[]{:S(2)}) %collective-permute-start.9) | collective-permute-done | bytes 1056 | tf_op jit(solution)/shard_map/ppermute | solution.py:549
  30.9 2.6 %finish.1 = (f32[256,128]{1,0:T(8,128)}, f32[256,128]{1,0:T(8,128)}) custom-call(f32[1,128]{1,0:T(1,128)S(1)} %max.20.top, f32[1,128]{1,0:T(1,128)S(1)} %collective-permute-done.3.last, f32[2,128]{1,0:T(2,128)S(1)} %add_select_fusion.fast, f32[2,128]{1,0:T(2,128)S(1)} %collective-permute-done.9.fast_last, f32[8,2,144,128]{3,2,1,0:T(8,128)S(1)} %get-tuple-element.33.kept, ...), custom_call_target="tpu_custom_call" | custom-call | flops 9830400 | bytes 5721088 | tf_op jit(solution)/shard_map/finish/pallas_call | solution.py:534
  (4 shorter events, 0.0 us)
Async XLA Ops:
  1.9 1.3 %collective-permute-start = (f32[1,128]{1,0:T(1,128)S(1)}, f32[1,128]{1,0:T(1,128)S(1)}, u32[]{:S(2)}, u32[]{:S(2)}) collective-permute-start(f32[1,128]{1,0:T(1,128)S(1)} %first_speed.1), channel_id=1, source_target_pairs={{0,1},{1,0},{2,3},{3,2},{4,5},{5,4},{6,7},{7,6},{8,9},{9,8},{10,11... | collective-permute-start | bytes 1544 | tf_op jit(solution)/shard_map/ppermute | solution.py:549
  3.2 4.9 %collective-permute-start.1 = (f32[1,128]{1,0:T(1,128)S(1)}, f32[1,128]{1,0:T(1,128)S(1)}, u32[]{:S(2)}, u32[]{:S(2)}) collective-permute-start(f32[1,128]{1,0:T(1,128)S(1)} %max.18.refs_9_), channel_id=1, source_target_pairs={{0,3},{1,2},{2,1},{3,0},{4,7},{5,6},{6,5},{7,4},{8,11},{9,10},{10,... | collective-permute-start | bytes 1544 | tf_op jit(solution)/shard_map/ppermute | solution.py:549
  7.7 7.2 %collective-permute-start.4 = (f32[9,2,8,128]{3,2,1,0:T(8,128)S(1)}, f32[9,2,8,128]{3,2,1,0:T(8,128)S(1)}, u32[]{:S(2)}, u32[]{:S(2)}) collective-permute-start(f32[9,2,8,128]{3,2,1,0:T(8,128)S(1)} %get-tuple-element.31), channel_id=1, source_target_pairs={{0,1},{1,0},{2,3},{3,2},{4,5},{5,4},{6,7},{7,6},{8,9},{9,8},{10,11... | collective-permute-start | bytes 221192 | tf_op jit(solution)/shard_map/ppermute | solution.py:549
  8.1 6.8 %collective-permute-start.5 = (f32[9,2,8,128]{3,2,1,0:T(8,128)S(1)}, f32[9,2,8,128]{3,2,1,0:T(8,128)S(1)}, u32[]{:S(2)}, u32[]{:S(2)}) collective-permute-start(f32[9,2,8,128]{3,2,1,0:T(8,128)S(1)} %get-tuple-element.32), channel_id=1, source_target_pairs={{0,15},{1,2},{2,1},{3,4},{4,3},{5,6},{6,5},{7,8},{8,7},{9,10},{10,... | collective-permute-start | bytes 221192 | tf_op jit(solution)/shard_map/ppermute | solution.py:549
  11.8 3.0 %collective-permute-start.2 = (f32[1,128]{1,0:T(1,128)S(1)}, f32[1,128]{1,0:T(1,128)S(1)}, u32[]{:S(2)}, u32[]{:S(2)}) collective-permute-start(f32[1,128]{1,0:T(1,128)S(1)} %max.19), channel_id=1, source_target_pairs={{0,5},{1,4},{2,7},{3,6},{4,1},{5,0},{6,3},{7,2},{8,13},{9,12},{10,... | collective-permute-start | bytes 1544 | tf_op jit(solution)/shard_map/ppermute | solution.py:549
  14.8 3.9 %collective-permute-start.3 = (f32[1,128]{1,0:T(1,128)S(1)}, f32[1,128]{1,0:T(1,128)S(1)}, u32[]{:S(2)}, u32[]{:S(2)}) collective-permute-start(f32[1,128]{1,0:T(1,128)S(1)} %max.20.top), channel_id=1, source_target_pairs={{0,9},{1,8},{2,11},{3,10},{4,13},{5,12},{6,15},{7,14},{8,1},{9,0},... | collective-permute-start | bytes 1544 | tf_op jit(solution)/shard_map/ppermute | solution.py:549
  19.6 1.2 %collective-permute-start.6 = (f32[2,128]{1,0:T(2,128)S(1)}, f32[2,128]{1,0:T(2,128)S(1)}, u32[]{:S(2)}, u32[]{:S(2)}) collective-permute-start(f32[2,128]{1,0:T(2,128)S(1)} %get-tuple-element.36), channel_id=1, source_target_pairs={{0,1},{1,0},{2,3},{3,2},{4,5},{5,4},{6,7},{7,6},{8,9},{9,8},{10,11... | collective-permute-start | bytes 3080 | tf_op jit(solution)/shard_map/ppermute | solution.py:549
  20.9 3.0 %collective-permute-start.7 = (f32[2,128]{1,0:T(2,128)S(1)}, f32[2,128]{1,0:T(2,128)S(1)}, u32[]{:S(2)}, u32[]{:S(2)}) collective-permute-start(f32[2,128]{1,0:T(2,128)S(1)} %add_select_fusion.2), channel_id=1, source_target_pairs={{0,3},{1,2},{2,1},{3,0},{4,7},{5,6},{6,5},{7,4},{8,11},{9,10},{10,... | collective-permute-start | bytes 3080 | tf_op jit(solution)/shard_map/ppermute | solution.py:549
  23.9 3.0 %collective-permute-start.8 = (f32[2,128]{1,0:T(2,128)S(1)}, f32[2,128]{1,0:T(2,128)S(1)}, u32[]{:S(2)}, u32[]{:S(2)}) collective-permute-start(f32[2,128]{1,0:T(2,128)S(1)} %add_select_fusion.1), channel_id=1, source_target_pairs={{0,5},{1,4},{2,7},{3,6},{4,1},{5,0},{6,3},{7,2},{8,13},{9,12},{10,... | collective-permute-start | bytes 3080 | tf_op jit(solution)/shard_map/ppermute | solution.py:549
  27.0 3.9 %collective-permute-start.9 = (f32[2,128]{1,0:T(2,128)S(1)}, f32[2,128]{1,0:T(2,128)S(1)}, u32[]{:S(2)}, u32[]{:S(2)}) collective-permute-start(f32[2,128]{1,0:T(2,128)S(1)} %add_select_fusion.fast), channel_id=1, source_target_pairs={{0,9},{1,8},{2,11},{3,10},{4,13},{5,12},{6,15},{7,14},{8,1},{9,0},... | collective-permute-start | bytes 3080 | tf_op jit(solution)/shard_map/ppermute | solution.py:549
